TPU v7x, 32 devices: a whole 2x2x4 slice. The times are simulated.
32 devices in a mesh: dp: 2 (over core), ctx: 4 (over z), mp: 4 (over y, x).
Axes of the slice: x: 2, y: 2, z: 4, core: 2. Of those that a mesh axis runs over, the one named last changes fastest.
Arguments:
- tokens: bfloat16 [2, 2048, 1024], P('dp', ('ctx', 'mp')), may hold values from -6 to 6
- norm1_gain: bfloat16 [1024], replicated, may hold values from 0.5 to 1.5
- q_weight: bfloat16 [1024, 2048], P(None, 'mp'), may hold values from -0.1875 to 0.1875
- key_matrix: bfloat16 [1024, 1024], P(None, 'mp'), may hold values from -0.1875 to 0.1875
- value_matrix: bfloat16 [1024, 1024], P(None, 'mp'), may hold values from -0.1875 to 0.1875
- q_gain: bfloat16 [128], replicated, may hold values from 0.5 to 1.5
- k_gain: bfloat16 [128], replicated, may hold values from 0.5 to 1.5
- o_weight: bfloat16 [2048, 1024], P('mp'), may hold values from -2 to 2
- norm2_gain: bfloat16 [1024], replicated, may hold values from 0.5 to 1.5
- gate_weight: bfloat16 [1024, 3072], P(None, 'mp'), may hold values from -0.1875 to 0.1875
- up_weight: bfloat16 [1024, 3072], P(None, 'mp'), may hold values from -0.1875 to 0.1875
- down_weight: bfloat16 [3072, 1024], P('mp'), may hold values from -0.109375 to 0.109375
- out_grad: bfloat16 [2, 2048, 1024], P('dp', ('ctx', 'mp')), may hold values from -6 to 6
- lengths: int32 [2, 4], P('dp'), may hold values from 1 to 2045, as said below
- pairing: int32 [4], replicated, may hold values from 0 to 3, each once
Outputs:
- output: bfloat16 [2, 2048, 1024], P('dp', ('ctx', 'mp'))
- input_grad: float32 [2, 2048, 1024], P('dp', ('ctx', 'mp'))
- norm1_gain_grad: float32 [1024], replicated
- q_weight_grad: float32 [1024, 2048], P(None, 'mp')
- k_weight_grad: float32 [1024, 1024], P(None, 'mp')
- v_weight_grad: float32 [1024, 1024], P(None, 'mp')
- q_gain_grad: float32 [128], replicated
- k_gain_grad: float32 [128], replicated
- o_weight_grad: float32 [2048, 1024], P('mp')
- norm2_gain_grad: float32 [1024], replicated
- gate_weight_grad: float32 [1024, 3072], P(None, 'mp')
- up_weight_grad: float32 [1024, 3072], P(None, 'mp')
- down_weight_grad: float32 [3072, 1024], P('mp')
Inputs may be any that keep to these rules, and one draw needn't show every extreme that they name: `lengths`: each row sums to 2048; one document of each row, at a place drawn from the seed, holds all but at most 128 of its tokens; in one row, drawn from the seed, every other document holds one token. Ctx device c holds blocks pairing[c] and 7 - pairing[c] of its sequence.
All inputs are finite; a program needn't handle non-finite values.
Results may differ from a plain program's by a relative error of at most 0.024.
Values may be sent and summed in bfloat16 or wider, within the bound.
No kernel may reach another device: no remote copies, remote signals or barrier semaphores. Data moves between devices by JAX's collectives and lax.ppermute only.
A program may use at most 256 MiB of HBM per device.

v0:
```python
import math

import jax
import jax.numpy as jnp
from jax import lax
from jax.sharding import PartitionSpec as P

EPS = 1e-06
THETA = 1000000.0
NEG = -1e30


def product(form, left, right):
    return jnp.einsum(form, left, right, preferred_element_type=jnp.float32)


def gather_rows(value_rows):
    return lax.all_gather(value_rows, "mp", axis=0, tiled=True)


def sum_rows(value_rows):
    return lax.psum_scatter(
        value_rows.astype(jnp.bfloat16), "mp", scatter_dimension=0, tiled=True
    ).astype(jnp.float32)


def norm_rows(value_rows, gain):
    factor = lax.rsqrt(jnp.mean(value_rows * value_rows, axis=-1, keepdims=True) + EPS)
    return (value_rows * factor * gain, factor)


def norm_back(value_rows, factor, gain, gradient):
    scaled_grad = gradient * gain
    inner_sum = jnp.sum(scaled_grad * value_rows, axis=-1, keepdims=True)
    backward = (
        factor * scaled_grad
        - value_rows * (factor * factor * factor) * inner_sum / value_rows.shape[-1]
    )
    return (backward, gradient * value_rows * factor)


def turn_half(value_rows):
    half_width = value_rows.shape[-1] // 2
    return jnp.concatenate([-value_rows[..., half_width:], value_rows[..., :half_width]], axis=-1)


def rope_tables(token_positions, head_dim):
    half_width = head_dim // 2
    frequency = THETA ** (-(jnp.arange(half_width, dtype=jnp.float32) * 2.0) / head_dim)
    angles = token_positions.astype(jnp.float32)[:, None] * frequency[None, :]
    cosines = jnp.concatenate([jnp.cos(angles), jnp.cos(angles)], axis=-1)
    sines = jnp.concatenate([jnp.sin(angles), jnp.sin(angles)], axis=-1)
    return (cosines, sines)


def rotate(value_rows, cosines, sines):
    return value_rows * cosines[:, None, :] + turn_half(value_rows) * sines[:, None, :]


def rotate_back(value_rows, cosines, sines):
    return value_rows * cosines[:, None, :] - turn_half(value_rows * sines[:, None, :])


def row_positions(pairing, owners, rows_in, half_rows):
    device_count = pairing.shape[0]
    matches = owners[:, None] == jnp.arange(device_count, dtype=jnp.int32)[None, :]
    paired = jnp.sum(jnp.where(matches, pairing[None, :], 0), axis=1)
    chosen = jnp.where(rows_in < half_rows, paired, 2 * device_count - 1 - paired)
    return chosen * half_rows + rows_in % half_rows


def doc_numbers(doc_lengths, token_positions):
    doc_ends = jnp.cumsum(doc_lengths)
    return jnp.sum((token_positions[:, None] >= doc_ends[None, :]).astype(jnp.int32), axis=1)


def pair_terms(
    query_piece, scaled_piece, max_piece, shift_piece, key_piece, value_piece, allowed, score_scale
):
    raw_scores = product("qhgd,khd->hgqk", query_piece, key_piece) * score_scale
    weights_f = jnp.where(allowed, jnp.exp(raw_scores - max_piece[..., None]), 0.0)
    prob_grad = product("qhgd,khd->hgqk", scaled_piece, value_piece)
    score_grad = (weights_f * (prob_grad - shift_piece[..., None])).astype(jnp.bfloat16)
    return (score_grad, weights_f.astype(jnp.bfloat16))


def on_device(
    tokens,
    norm1_gain,
    q_weight,
    key_matrix,
    value_matrix,
    q_gain,
    k_gain,
    o_weight,
    norm2_gain,
    gate_weight,
    up_weight,
    down_weight,
    out_grad,
    lengths,
    pairing,
):
    head_dim = q_gain.shape[0]
    q_heads = q_weight.shape[1] // head_dim
    kv_heads = key_matrix.shape[1] // head_dim
    group_width = q_heads // kv_heads
    q_width = q_heads * head_dim
    kv_width = kv_heads * head_dim
    ctx_rows = tokens.shape[1] * lax.axis_size("mp")
    half_rows = ctx_rows // 2
    seq_rows = ctx_rows * lax.axis_size("ctx")
    key_block = min(seq_rows, 2048)
    key_steps = seq_rows // key_block
    score_scale = 1.0 / math.sqrt(head_dim)
    ctx_here = lax.axis_index("ctx")
    local_index = jnp.arange(ctx_rows, dtype=jnp.int32)
    local_pos = row_positions(
        pairing, jnp.zeros((ctx_rows,), jnp.int32) + ctx_here, local_index, half_rows
    )
    all_index = jnp.arange(seq_rows, dtype=jnp.int32)
    all_pos = row_positions(pairing, all_index // ctx_rows, all_index % ctx_rows, half_rows)
    local_doc = doc_numbers(lengths[0], local_pos)
    all_doc = doc_numbers(lengths[0], all_pos)
    gain1 = norm1_gain.astype(jnp.float32)
    gain2 = norm2_gain.astype(jnp.float32)
    gain_q = q_gain.astype(jnp.float32)
    gain_k = k_gain.astype(jnp.float32)
    tok_share = tokens[0].astype(jnp.float32)
    normed1, inv1 = norm_rows(tok_share, gain1)
    hidden_first = gather_rows(normed1.astype(jnp.bfloat16))
    q_lin = jnp.dot(hidden_first, q_weight, preferred_element_type=jnp.float32)
    key_linear = jnp.dot(hidden_first, key_matrix, preferred_element_type=jnp.float32)
    values_here = jnp.dot(hidden_first, value_matrix, preferred_element_type=jnp.float32).astype(
        jnp.bfloat16
    )
    cosines, sines = rope_tables(local_pos, head_dim)
    q_split = q_lin.reshape(ctx_rows, q_heads, head_dim)
    q_normed, q_inv = norm_rows(q_split, gain_q)
    query_rows = rotate(q_normed, cosines, sines).astype(jnp.bfloat16)
    k_split = key_linear.reshape(ctx_rows, kv_heads, head_dim)
    k_normed, k_inv = norm_rows(k_split, gain_k)
    keys_here = rotate(k_normed, cosines, sines).astype(jnp.bfloat16)
    keys_flat, values_flat = (
        lax.all_gather(keys_here.reshape(ctx_rows, kv_width), "ctx", axis=0, tiled=True),
        lax.all_gather(values_here, "ctx", axis=0, tiled=True),
    )
    keys_all = keys_flat.reshape(seq_rows, kv_heads, head_dim)
    values_all = values_flat.reshape(seq_rows, kv_heads, head_dim)
    q_grouped = query_rows.reshape(ctx_rows, kv_heads, group_width, head_dim)

    def key_view(start):
        key_piece = lax.dynamic_slice_in_dim(keys_all, start, key_block, 0)
        value_piece = lax.dynamic_slice_in_dim(values_all, start, key_block, 0)
        pos_piece = lax.dynamic_slice_in_dim(all_pos, start, key_block, 0)
        doc_piece = lax.dynamic_slice_in_dim(all_doc, start, key_block, 0)
        allowed = (pos_piece[None, :] <= local_pos[:, None]) & (
            doc_piece[None, :] == local_doc[:, None]
        )
        return (key_piece, value_piece, allowed)

    def stats_step(step_index, carry):
        running_max, running_sum = carry
        key_piece, value_piece, allowed = key_view(step_index * key_block)
        raw_scores = product("qhgd,khd->hgqk", q_grouped, key_piece) * score_scale
        masked = jnp.where(allowed, raw_scores, NEG)
        new_max = jnp.maximum(running_max, jnp.max(masked, axis=-1))
        exponent = jnp.where(allowed, jnp.exp(masked - new_max[..., None]), 0.0)
        new_sum = running_sum * jnp.exp(running_max - new_max) + jnp.sum(exponent, axis=-1)
        return (new_max, new_sum)

    start_max = jnp.full((kv_heads, group_width, ctx_rows), NEG, jnp.float32)
    row_max, row_sum = lax.fori_loop(
        0, key_steps, stats_step, (start_max, jnp.zeros_like(start_max))
    )

    def value_step(step_index, accum):
        key_piece, value_piece, allowed = key_view(step_index * key_block)
        raw_scores = product("qhgd,khd->hgqk", q_grouped, key_piece) * score_scale
        weights_low = jnp.where(allowed, jnp.exp(raw_scores - row_max[..., None]), 0.0).astype(
            jnp.bfloat16
        )
        return accum + product("hgqk,khd->qhgd", weights_low, value_piece)

    numer = lax.fori_loop(
        0,
        key_steps,
        value_step,
        jnp.zeros((ctx_rows, kv_heads, group_width, head_dim), jnp.float32),
    )
    sums_rows = jnp.transpose(row_sum, (2, 0, 1))
    out_full = numer / sums_rows[..., None]
    attended_output = out_full.reshape(ctx_rows, q_width).astype(jnp.bfloat16)
    attn_share = sum_rows(jnp.dot(attended_output, o_weight, preferred_element_type=jnp.float32))
    resid = tok_share + attn_share
    normed2, inv2 = norm_rows(resid, gain2)
    hidden2 = gather_rows(normed2.astype(jnp.bfloat16))
    gate_pre = jnp.dot(hidden2, gate_weight, preferred_element_type=jnp.float32)
    up_pre = jnp.dot(hidden2, up_weight, preferred_element_type=jnp.float32)
    sigmoid_gate = jax.nn.sigmoid(gate_pre)
    silu_gate = gate_pre * sigmoid_gate
    activ = (silu_gate * up_pre).astype(jnp.bfloat16)
    ffn_share = sum_rows(jnp.dot(activ, down_weight, preferred_element_type=jnp.float32))
    output = (resid + ffn_share).astype(jnp.bfloat16)[None]
    grad_full = gather_rows(out_grad[0])
    act_grad = product("rd,fd->rf", grad_full, down_weight)
    down_w_grad = product("rf,rd->fd", activ, grad_full)
    gate_grad = (act_grad * up_pre * sigmoid_gate * (1.0 + gate_pre * (1.0 - sigmoid_gate))).astype(
        jnp.bfloat16
    )
    up_grad = (act_grad * silu_gate).astype(jnp.bfloat16)
    gate_w_grad = product("rd,rf->df", hidden2, gate_grad)
    up_w_grad = product("rd,rf->df", hidden2, up_grad)
    hidden2_grad = sum_rows(
        product("rf,df->rd", gate_grad, gate_weight) + product("rf,df->rd", up_grad, up_weight)
    )
    resid_back, norm2_terms = norm_back(resid, inv2, gain2, hidden2_grad)
    resid_grad = out_grad[0].astype(jnp.float32) + resid_back
    resid_full = gather_rows(resid_grad.astype(jnp.bfloat16))
    o_w_grad = product("rc,rd->cd", attended_output, resid_full)
    attn_grad = product("rd,cd->rc", resid_full, o_weight).astype(jnp.bfloat16)
    grad_split = attn_grad.astype(jnp.float32).reshape(ctx_rows, kv_heads, group_width, head_dim)
    out_scaled = (grad_split / sums_rows[..., None]).astype(jnp.bfloat16)
    shift = jnp.transpose(jnp.sum(grad_split * out_full, axis=-1) / sums_rows, (1, 2, 0))
    zero_query = jnp.zeros((ctx_rows, kv_heads, group_width, head_dim), jnp.float32)

    def both_step(step_index, carry):
        query_acc, key_buffer, value_buffer = carry
        start = step_index * key_block
        key_piece, value_piece, allowed = key_view(start)
        score_grad, weights_low = pair_terms(
            q_grouped, out_scaled, row_max, shift, key_piece, value_piece, allowed, score_scale
        )
        query_acc = query_acc + product("hgqk,khd->qhgd", score_grad, key_piece) * score_scale
        key_piece_grad = product("hgqk,qhgd->khd", score_grad, q_grouped) * score_scale
        value_piece_grad = product("hgqk,qhgd->khd", weights_low, out_scaled)
        key_buffer = lax.dynamic_update_slice_in_dim(
            key_buffer, key_piece_grad.reshape(key_block, kv_width), start, 0
        )
        value_buffer = lax.dynamic_update_slice_in_dim(
            value_buffer, value_piece_grad.reshape(key_block, kv_width), start, 0
        )
        return (query_acc, key_buffer, value_buffer)

    zero_keys = jnp.zeros((seq_rows, kv_width), jnp.float32)
    query_grad, key_buffer, value_buffer = lax.fori_loop(
        0, key_steps, both_step, (zero_query, zero_keys, zero_keys)
    )
    key_sum, value_sum = (
        lax.psum_scatter(
            key_buffer.astype(jnp.bfloat16), "ctx", scatter_dimension=0, tiled=True
        ).astype(jnp.float32),
        lax.psum_scatter(
            value_buffer.astype(jnp.bfloat16), "ctx", scatter_dimension=0, tiled=True
        ).astype(jnp.float32),
    )
    key_grad = key_sum.reshape(ctx_rows, kv_heads, head_dim)
    q_rot_grad = query_grad.reshape(ctx_rows, q_heads, head_dim)
    q_lin_grad, q_gain_terms = norm_back(
        q_split, q_inv, gain_q, rotate_back(q_rot_grad, cosines, sines)
    )
    k_lin_grad, k_gain_terms = norm_back(
        k_split, k_inv, gain_k, rotate_back(key_grad, cosines, sines)
    )
    q_low = q_lin_grad.reshape(ctx_rows, q_width).astype(jnp.bfloat16)
    k_low = k_lin_grad.reshape(ctx_rows, kv_width).astype(jnp.bfloat16)
    v_low = value_sum.astype(jnp.bfloat16)
    q_w_grad = product("rd,rc->dc", hidden_first, q_low)
    k_w_grad = product("rd,rc->dc", hidden_first, k_low)
    v_w_grad = product("rd,rc->dc", hidden_first, v_low)
    hidden1_part = (
        product("rc,dc->rd", q_low, q_weight)
        + product("rc,dc->rd", k_low, key_matrix)
        + product("rc,dc->rd", v_low, value_matrix)
    )
    hidden1_grad = sum_rows(hidden1_part)
    tok_back, norm1_terms = norm_back(tok_share, inv1, gain1, hidden1_grad)
    input_grad = (resid_grad + tok_back)[None]
    q_w_grad, k_w_grad, v_w_grad, o_w_grad, gate_w_grad, up_w_grad, down_w_grad = lax.psum(
        (q_w_grad, k_w_grad, v_w_grad, o_w_grad, gate_w_grad, up_w_grad, down_w_grad), ("dp", "ctx")
    )
    gain1_grad, gain2_grad, gainq_grad, gaink_grad = lax.psum(
        (
            jnp.sum(norm1_terms, axis=0),
            jnp.sum(norm2_terms, axis=0),
            jnp.sum(q_gain_terms, axis=(0, 1)),
            jnp.sum(k_gain_terms, axis=(0, 1)),
        ),
        ("dp", "ctx", "mp"),
    )
    return (
        output,
        input_grad,
        gain1_grad,
        q_w_grad,
        k_w_grad,
        v_w_grad,
        gainq_grad,
        gaink_grad,
        o_w_grad,
        gain2_grad,
        gate_w_grad,
        up_w_grad,
        down_w_grad,
    )


def solution(mesh):
    placed = (
        P("dp", ("ctx", "mp"), None),
        P(),
        P(None, "mp"),
        P(None, "mp"),
        P(None, "mp"),
        P(),
        P(),
        P("mp", None),
        P(),
        P(None, "mp"),
        P(None, "mp"),
        P("mp", None),
        P("dp", ("ctx", "mp"), None),
        P("dp", None),
        P(),
    )
    return jax.shard_map(
        on_device,
        mesh=mesh,
        in_specs=placed,
        out_specs=(
            P("dp", ("ctx", "mp"), None),
            P("dp", ("ctx", "mp"), None),
            P(),
            P(None, "mp"),
            P(None, "mp"),
            P(None, "mp"),
            P(),
            P(),
            P("mp", None),
            P(),
            P(None, "mp"),
            P(None, "mp"),
            P("mp", None),
        ),
        check_vma=False,
    )
```

profile of v0, /device:TPU:0, one launch (start us, length us, event | category | flops | bytes accessed | tf_op | source)
XLA Modules:
  0.0 745.4 jit_solution(4680585843171253651)
XLA Ops:
  15.5 24.9 %all-gather.8.cloned.1.call-done = bf16[512,1024]{1,0:T(8,128)(2,1)} async-done(((bf16[128,1024]{1,0:T(8,128)(2,1)}), bf16[512,1024]{1,0:T(8,128)(2,1)}) %all-gather.8.cloned.1.call-update) | async-done | bytes 1048592 | tf_op jit(solution)/shard_map/all_gather | solution.py:18
  46.1 3.0 multiply_reduce_fusion
  52.9 2.8 fusion.19
  55.7 15.9 %all-gather.12.cloned.1.call-done = bf16[2048,256]{0,1:T(8,128)(2,1)} async-done(((bf16[512,256]{0,1:T(8,128)(2,1)}), bf16[2048,256]{0,1:T(8,128)(2,1)}) %all-gather.12.cloned.1.call-update) | async-done | bytes 1048592 | tf_op jit(solution)/shard_map/all_gather | solution.py:145
  71.6 4.9 fusion.6
  76.6 4.2 select_reduce_fusion
  82.4 18.8 %all-gather.10.cloned.1.call-done = bf16[2048,256]{1,0:T(8,128)(2,1)} async-done(((bf16[512,256]{1,0:T(8,128)(2,1)}), bf16[2048,256]{1,0:T(8,128)(2,1)}) %all-gather.10.cloned.1.call-update) | async-done | bytes 1048592 | tf_op jit(solution)/shard_map/all_gather | solution.py:146
  103.3 11.1 %fusion.82 = (bf16[512,2,2,128]{0,3,2,1:T(8,128)(2,1)S(1)}, f32[512,2,2,128]{0,3,2,1:T(8,128)}) fusion(f32[512,2,2]{0,2,1:T(2,128)S(1)} %fusion.74, f32[2,2048,512,2]{2,1,3,0:T(8,128)} %copy-done.2, f32[2,2,512]{2,1,0:T(2,128)S(1)} %broadcast_maximum_fusion, pred[512,2048]{0,1:T(8,128)(4,1)} %compare_and_fusion, bf16[2048,2,128,1]{2,1,0,3:T(2,128)(2,1)} %bitcast.276), kind=kOutput, calls=%fused_computation.178 | convolution fusion | flops 1091043328 | bytes 20463616 | tf_op jit(solution)/shard_map/while/body/eval_jaxpr/hgqk,khd->qhgd/dot_general | solution.py:14
  117.0 27.3 %reduce-scatter.7.cloned.1.call-done = bf16[128,1024]{1,0:T(8,128)(2,1)} async-done(((bf16[512,1024]{1,0:T(8,128)(2,1)}), bf16[128,1024]{1,0:T(8,128)(2,1)}) %reduce-scatter.7.cloned.1.call-update) | async-done | bytes 262160 | tf_op jit(solution)/shard_map/reduce_scatter | solution.py:22
  147.9 26.2 %all-gather.14.cloned.1.call-done = bf16[512,1024]{1,0:T(8,128)(2,1)} async-done(((bf16[128,1024]{1,0:T(8,128)(2,1)}), bf16[512,1024]{1,0:T(8,128)(2,1)}) %all-gather.14.cloned.1.call-update) | async-done | bytes 1048592 | tf_op jit(solution)/shard_map/all_gather | solution.py:18
  174.0 4.0 fusion.83
  180.2 22.4 %all-gather.18.cloned.1.call-done = bf16[1,512,1024]{2,1,0:T(8,128)(2,1)} async-done(((bf16[1,128,1024]{2,1,0:T(8,128)(2,1)}), bf16[1,512,1024]{2,1,0:T(8,128)(2,1)}) %all-gather.18.cloned.1.call-update) | async-done | bytes 1048592 | tf_op jit(solution)/shard_map/all_gather | solution.py:18
  202.5 4.7 multiply_convert_fusion
  211.3 27.8 %reduce-scatter.11.cloned.1.call-done = bf16[128,1024]{1,0:T(8,128)(2,1)} async-done(((bf16[512,1024]{1,0:T(8,128)(2,1)}), bf16[128,1024]{1,0:T(8,128)(2,1)}) %reduce-scatter.11.cloned.1.call-update) | async-done | bytes 262160 | tf_op jit(solution)/shard_map/reduce_scatter | solution.py:22
  242.6 26.7 %all-gather.16.cloned.1.call-done = bf16[512,1024]{1,0:T(8,128)(2,1)} async-done(((bf16[128,1024]{1,0:T(8,128)(2,1)}), bf16[512,1024]{1,0:T(8,128)(2,1)}) %all-gather.16.cloned.1.call-update) | async-done | bytes 1048592 | tf_op jit(solution)/shard_map/all_gather | solution.py:18
  269.3 2.8 fusion.14
  272.2 9.3 %fusion.3 = bf16[2,2,512,2048]{2,3,1,0:T(8,128)(2,1)S(1)} fusion(f32[2,2048,512,2]{2,1,3,0:T(8,128)} %copy-done.2, f32[2,2,512]{2,1,0:T(2,128)S(1)} %bitcast_divide_fusion, f32[2,2,512]{2,1,0:T(2,128)S(1)} %broadcast_maximum_fusion, pred[512,2048]{0,1:T(8,128)(4,1)S(1)} %copy-done.20, bf16[2048,2,128,1]{2,1,0,3:T(2,128)(2,1)S(1)} %bitcast.277, ...), kind=kOutput, calls=%fused_computation.4 | convolution fusion | flops 1099694080 | bytes 27811840 | tf_op jit(solution)/shard_map/while/body/eval_jaxpr/qhgd,khd->hgqk/dot_general | solution.py:14
  281.5 3.8 fusion.9
  285.6 5.0 convolution_multiply_fusion
  293.3 8.9 %fusion.10 = bf16[2,128,2048]{2,1,0:T(8,128)(2,1)} fusion(bf16[512,2,2,128]{0,3,2,1:T(8,128)(2,1)S(1)} %bitcast.283, f32[512,2,2]{0,2,1:T(2,128)S(1)} %fusion.74, f32[2,2048,512,2]{2,1,3,0:T(8,128)} %copy-done.2, f32[2,2,512]{2,1,0:T(2,128)S(1)} %broadcast_maximum_fusion, pred[512,2048]{0,1:T(8,128)(4,1)S(1)} %copy-done.21), kind=kOutput, calls=%fused_computation.17 | convolution fusion | flops 1091829760 | bytes 19415040 | tf_op jit(solution)/shard_map/while/body/eval_jaxpr/hgqk,qhgd->khd/dot_general | solution.py:14
  302.3 2.5 pad_maximum_fusion
  309.1 3.5 reduce-scatter.13.cloned.1.call-done
  316.9 24.3 %reduce-scatter.15.cloned.1.call-done = bf16[512,256]{0,1:T(8,128)(2,1)} async-done(((bf16[2048,256]{0,1:T(8,128)(2,1)}), bf16[512,256]{0,1:T(8,128)(2,1)}) %reduce-scatter.15.cloned.1.call-update) | async-done | bytes 262160 | tf_op jit(solution)/shard_map/reduce_scatter | solution.py:253
  341.2 3.9 add_convert_fusion
  345.2 3.1 convolution_convert_fusion
  348.6 4.3 fusion.92
  352.9 2.7 fusion.93
  355.6 2.7 fusion.25
  365.4 6.3 reduce-scatter.17.cloned.1.call-done
  372.9 39.6 %all-reduce = (f32[1024]{0:T(1024)}, f32[128]{0:T(128)}, f32[128]{0:T(128)}, f32[1024]{0:T(1024)}) all-reduce(f32[1024]{0:T(1024)S(1)} %get-tuple-element.93, f32[128]{0:T(128)S(1)} %bitcast_reduce_fusion, f32[128]{0:T(128)S(1)} %bitcast_reduce_fusion.1, ...), channel_id=1, replica_groups=mesh['dp'=2,'ctx'=4,'mp'=4] {'dp','ctx','mp'}, use_global_device_ids=true, to_apply=%region_23.24 | all-reduce | flops 2304 | bytes 18432 | tf_op jit(solution)/shard_map/psum | solution.py:282
  415.0 308.3 %all-reduce.4.cloned.1.call-done = (f32[1024,512]{1,0:T(8,128)}, f32[1024,256]{1,0:T(8,128)}, f32[1024,256]{1,0:T(8,128)}, f32[512,1024]{1,0:T(8,128)}, f32[1024...) async-done(((f32[1024,512]{1,0:T(8,128)}, f32[1024,256]{1,0:T(8,128)}, f32[1024,256]{1,0:T(8,128)}, f32[512,1024]{1,0:T(8,128)}, f32[1024,768]{1,0:T(8,128)}, ...) | async-done | bytes 15728656 | tf_op jit(solution)/shard_map/psum | solution.py:279
  723.3 3.2 copy.77
  (206 shorter events, 71.5 us)
Async XLA Ops:
  7.2 195.4 %copy-start = (bf16[768,1024]{1,0:T(8,128)(2,1)S(1)}, bf16[768,1024]{1,0:T(8,128)(2,1)}, u32[]{:S(2)}) copy-start(bf16[768,1024]{1,0:T(8,128)(2,1)} %param.26) | copy-start | bytes 4718596
  7.2 33.3 %all-gather.8.cloned.1.call-start = ((), (), s32[]{:S(2)}) async-start(), calls=%async_computation.6 | async-start | bytes 1310720 | tf_op jit(solution)/shard_map/all_gather | solution.py:18
  10.9 60.7 %all-gather.12.cloned.1.call-start = ((), (), s32[]{:S(2)}) async-start(), calls=%async_computation.8 | async-start | bytes 1310720 | tf_op jit(solution)/shard_map/all_gather | solution.py:145
  15.5 37.3 %copy-start.8 = (f32[512,128]{0,1:T(8,128)}, f32[512,128]{0,1:T(8,128)S(1)}, u32[]{:S(2)}) copy-start(f32[512,128]{0,1:T(8,128)S(1)} %get-tuple-element.179) | copy-start | bytes 786436
  43.5 57.7 %all-gather.10.cloned.1.call-start = ((), (), s32[]{:S(2)}) async-start(), calls=%async_computation.7 | async-start | bytes 1310720 | tf_op jit(solution)/shard_map/all_gather | solution.py:146
  52.8 91.5 %reduce-scatter.7.cloned.1.call-start = ((), (), s32[]{:S(2)}) async-start(), calls=%async_computation.9 | async-start | bytes 1310720 | tf_op jit(solution)/shard_map/reduce_scatter | solution.py:22
  71.6 5.0 copy-start.19
  76.5 5.8 copy-start.2
  103.3 11.9 %copy-start.33 = (bf16[512,1024]{1,0:T(8,128)(2,1)S(1)}, bf16[512,1024]{1,0:T(8,128)(2,1)}, u32[]{:S(2)}) copy-start(bf16[512,1024]{1,0:T(8,128)(2,1)} %param.22) | copy-start | bytes 3145732
  114.4 29.9 %copy-start.4 = (bf16[1,128,1024]{2,1,0:T(8,128)(2,1)S(1)}, bf16[1,128,1024]{2,1,0:T(8,128)(2,1)}, u32[]{:S(2)}) copy-start(bf16[1,128,1024]{2,1,0:T(8,128)(2,1)} %param.15) | copy-start | bytes 786436
  117.0 57.1 %all-gather.14.cloned.1.call-start = ((), (), s32[]{:S(2)}) async-start(), calls=%async_computation.10 | async-start | bytes 1310720 | tf_op jit(solution)/shard_map/all_gather | solution.py:18
  147.2 55.3 %all-gather.18.cloned.1.call-start = ((), (), s32[]{:S(2)}) async-start(), calls=%async_computation.17 | async-start | bytes 1310720 | tf_op jit(solution)/shard_map/all_gather | solution.py:18
  147.8 91.3 %reduce-scatter.11.cloned.1.call-start = ((), (), s32[]{:S(2)}) async-start(), calls=%async_computation.12 | async-start | bytes 1310720 | tf_op jit(solution)/shard_map/reduce_scatter | solution.py:22
  174.0 4.0 copy-start.11
  174.0 4.0 copy-start.51
  202.5 5.6 copy-start.50
  211.3 58.1 %all-gather.16.cloned.1.call-start = ((), (), s32[]{:S(2)}) async-start(), calls=%async_computation.13 | async-start | bytes 1310720 | tf_op jit(solution)/shard_map/all_gather | solution.py:18
  242.5 70.0 %reduce-scatter.13.cloned.1.call-start = ((), (), s32[]{:S(2)}) async-start(), calls=%async_computation.14 | async-start | bytes 1310720 | tf_op jit(solution)/shard_map/reduce_scatter | solution.py:250
  272.1 9.4 %copy-start.47 = (bf16[512,512]{0,1:T(8,128)(2,1)}, bf16[512,512]{0,1:T(8,128)(2,1)S(1)}, u32[]{:S(2)}) copy-start(bf16[512,512]{0,1:T(8,128)(2,1)S(1)} %get-tuple-element.178) | copy-start | bytes 1572868
  272.1 9.3 %copy-start.30 = (bf16[512,2,2,128]{0,3,2,1:T(8,128)(2,1)S(1)}, bf16[512,2,2,128]{0,3,2,1:T(8,128)(2,1)}, u32[]{:S(2)}) copy-start(bf16[512,2,2,128]{0,3,2,1:T(8,128)(2,1)} %fusion.19) | copy-start | bytes 1572868
  285.3 55.9 %reduce-scatter.15.cloned.1.call-start = ((), (), s32[]{:S(2)}) async-start(), calls=%async_computation.15 | async-start | bytes 1310720 | tf_op jit(solution)/shard_map/reduce_scatter | solution.py:253
  285.5 6.0 copy-start.15
  302.3 69.4 %reduce-scatter.17.cloned.1.call-start = ((), (), s32[]{:S(2)}) async-start(), calls=%async_computation.16 | async-start | bytes 1310720 | tf_op jit(solution)/shard_map/reduce_scatter | solution.py:22
  345.2 67.3 %reduce-scatter.9.cloned.1.call-start = ((), (), s32[]{:S(2)}) async-start(), calls=%async_computation.11 | async-start | bytes 1310720 | tf_op jit(solution)/shard_map/reduce_scatter | solution.py:22
  348.3 375.0 %all-reduce.4.cloned.1.call-start = ((), (), s32[]{:S(2)}) async-start(), calls=%async_computation.18 | async-start | bytes 31457280 | tf_op jit(solution)/shard_map/psum | solution.py:279
  348.6 4.3 copy-start.12
  348.6 4.3 copy-start.42
  358.3 4.1 copy-start.28
  365.4 47.1 %copy-start.13 = (bf16[128,1024]{1,0:T(8,128)(2,1)S(1)}, bf16[128,1024]{1,0:T(8,128)(2,1)}, u32[]{:S(2)}) copy-start(bf16[128,1024]{1,0:T(8,128)(2,1)} %reduce-scatter.7.cloned.1.call-done) | copy-start | bytes 786436
  365.4 47.1 %copy-start.25 = (bf16[1,128,1024]{2,1,0:T(8,128)(2,1)S(1)}, bf16[1,128,1024]{2,1,0:T(8,128)(2,1)}, u32[]{:S(2)}) copy-start(bf16[1,128,1024]{2,1,0:T(8,128)(2,1)} %param.27) | copy-start | bytes 786436
  365.4 47.1 %copy-start.26 = (bf16[128,1024]{1,0:T(8,128)(2,1)S(1)}, bf16[128,1024]{1,0:T(8,128)(2,1)}, u32[]{:S(2)}) copy-start(bf16[128,1024]{1,0:T(8,128)(2,1)} %reduce-scatter.11.cloned.1.call-done) | copy-start | bytes 786436
  723.3 4.2 copy-start.37
  (35 other events, 81.4 us)
Sparse Core Ops, SparseCore 0:
  11.1 29.3 all-gather.7
  43.6 27.9 all-gather.11
  73.7 27.4 all-gather.9
  117.1 27.1 reduce-scatter.6
  147.4 26.6 all-gather.13
  175.9 26.6 all-gather.17
  211.4 27.7 reduce-scatter.10
  242.6 26.6 all-gather.15
  285.4 27.1 reduce-scatter.12
  315.4 25.7 reduce-scatter.14
  345.3 26.3 reduce-scatter.16
  375.3 27.8 reduce-scatter.8
  407.3 315.9 all-reduce.3
where the time goes:
time: 754 us; the launch traced here: 745 us
  waiting for transfers between devices  533 us (71%)
  matrix products  94.9 us (13%)
  blocking collectives  39.6 us (5%)
  other arithmetic  38 us (5%)
  local copies, waits for them, and re-layouts  23.7 us (3%)
  between operations  14.9 us (2%)
    psum x1, waiting for transfers between devices, on_device(): lax.psum((q_w_grad, k_w_grad, v_w_grad, o_w_grad, gate_w_grad, up_w_grad,...  308 us
    all_gather x4, waiting for transfers between devices, gather_rows(): return lax.all_gather(value_rows, 'mp', axis=0, tiled=True)  100 us
    dot_general x20, matrix products, product(): return jnp.einsum(form, left, right, preferred_element_type=jnp.float32)  78 us
    reduce_scatter x4, waiting for transfers between devices, sum_rows(): lax.psum_scatter(value_rows.astype(jnp.bfloat16), 'mp', scatter_dimension...  61.4 us
    psum x1, blocking collectives, on_device(): lax.psum((jnp.sum(norm1_terms, axis=0), jnp.sum(norm2_terms, axis=0), jnp...  39.6 us
    reduce_scatter x1, waiting for transfers between devices, on_device(): lax.psum_scatter(value_buffer.astype(jnp.bfloat16), 'ctx', scatter_dimens...  24.3 us
    unnamed x115, local copies, waits for them, and re-layouts  21.6 us
    all_gather x1, waiting for transfers between devices, on_device(): lax.all_gather(values_here, 'ctx', axis=0, tiled=True)  18.8 us
  transfers between devices with their start and end apart: 13, of which 12 were waited for; matrix products, arithmetic and copies ran while one was open for 11% of the time, Pallas kernels for 0%

commit v1 on v0

v1 whole, which is shorter than its diff:
```python
import math

import jax
import jax.numpy as jnp
from jax import lax
from jax.experimental import pallas as pl
from jax.experimental.pallas import tpu as pltpu
from jax.sharding import PartitionSpec as P

EPS = 1e-06
THETA = 1000000.0
LOG2E = 1.4426950408889634
BF = jnp.bfloat16
F32 = jnp.float32
VMEM_LIMIT = 52 * 1024 * 1024


def dot(left, right, left_dim, right_dim):
    return lax.dot_general(
        left, right, (((left_dim,), (right_dim,)), ((), ())), preferred_element_type=F32
    )


def whole_spec(array):
    rank = len(array.shape)
    return pl.BlockSpec(array.shape, lambda *_: (0,) * rank)


SMEM = pl.BlockSpec(memory_space=pltpu.SMEM)


def call(kernel, ins, outs, grid=(1,), in_specs=None, out_specs=None, scratch=(), flops=0, name=None):
    in_specs = in_specs or {}
    out_specs = out_specs or {}
    moved = sum(math.prod(a.shape) * a.dtype.itemsize for a in list(ins) + list(outs))
    return pl.pallas_call(
        kernel,
        grid=grid,
        in_specs=[in_specs.get(i, whole_spec(a)) for i, a in enumerate(ins)],
        out_specs=[out_specs.get(i, whole_spec(a)) for i, a in enumerate(outs)],
        out_shape=list(outs),
        scratch_shapes=list(scratch),
        compiler_params=pltpu.CompilerParams(vmem_limit_bytes=VMEM_LIMIT),
        cost_estimate=pl.CostEstimate(flops=flops, bytes_accessed=moved, transcendentals=0),
        name=name,
    )(*ins)


def out(shape, dtype):
    return jax.ShapeDtypeStruct(shape, dtype)


def swap(value, axis, step):
    size = lax.axis_size(axis)
    return lax.ppermute(value, axis, [(i, i ^ step) for i in range(size)])


def swaps(values, axis):
    order = sorted(range(1, len(values)), key=lambda j: -bin(j).count("1"))
    got = {j: swap(values[j], axis, j) for j in order}
    return [got[j] for j in range(1, len(values))]


def from_ctx(value, step):
    size = lax.axis_size("ctx")
    return lax.ppermute(value, "ctx", [((i + step) % size, i) for i in range(size)])


def to_ctx(value, step):
    size = lax.axis_size("ctx")
    return lax.ppermute(value, "ctx", [(i, (i + step) % size) for i in range(size)])


def norm_kernel(rows_ref, gain_ref, normed_ref):
    rows = rows_ref[...].astype(F32)
    factor = lax.rsqrt(jnp.mean(rows * rows, axis=-1, keepdims=True) + EPS)
    normed_ref[...] = (rows * factor * gain_ref[...]).astype(BF)


def resid_kernel(tok_ref, own_ref, *refs):
    *parts, gain_ref, resid_ref, normed_ref = refs
    rows = tok_ref[...].astype(F32) + own_ref[...]
    for part in parts:
        rows = rows + part[...].astype(F32)
    resid_ref[...] = rows
    factor = lax.rsqrt(jnp.mean(rows * rows, axis=-1, keepdims=True) + EPS)
    normed_ref[...] = (rows * factor * gain_ref[...]).astype(BF)


def norm_back(rows, gain, gradient):
    factor = lax.rsqrt(jnp.mean(rows * rows, axis=-1, keepdims=True) + EPS)
    scaled = gradient * gain
    inner = jnp.mean(scaled * rows, axis=-1, keepdims=True)
    return factor * scaled - rows * (factor * factor * factor) * inner, gradient * rows * factor


def resid_back_kernel(resid_ref, grad_ref, gain_ref, own_ref, *refs):
    *parts, full_ref, low_ref, gain_grad_ref = refs
    gradient = own_ref[...]
    for part in parts:
        gradient = gradient + part[...].astype(F32)
    back, terms = norm_back(resid_ref[...], gain_ref[...], gradient)
    total = grad_ref[...].astype(F32) + back
    full_ref[...] = total
    low_ref[...] = total.astype(BF)
    gain_grad_ref[...] = jnp.sum(terms, axis=0, keepdims=True)


def input_back_kernel(tok_ref, resid_grad_ref, gain_ref, *refs):
    *parts, result_ref = refs
    gradient = parts[0][...].astype(F32)
    for part in parts[1:]:
        gradient = gradient + part[...].astype(F32)
    back, _ = norm_back(tok_ref[...].astype(F32), gain_ref[...], gradient)
    result_ref[...] = resid_grad_ref[...] + back


def sum_kernel(*refs):
    *parts, result_ref = refs
    total = parts[0][...].astype(F32)
    for part in parts[1:]:
        total = total + part[...].astype(F32)
    result_ref[...] = total.astype(result_ref.dtype)


def sum_parts(parts, dtype):
    return call(sum_kernel, parts, [out(parts[0].shape, dtype)], name="sum_parts")[0]


def key_rows(linear, gain, cosines, sines):
    heads = []
    for start in range(0, linear.shape[1], gain.shape[1]):
        rows = linear[:, start : start + gain.shape[1]]
        factor = lax.rsqrt(jnp.mean(rows * rows, axis=-1, keepdims=True) + EPS)
        normed = rows * factor * gain
        turned = pltpu.roll(normed, normed.shape[1] // 2, 1)
        heads.append((normed * cosines + turned * sines).astype(BF))
    return heads


def key_value_part(hidden, wk_ref, wv_ref, gk_ref, cos_ref, sin_ref, k_ref, v_ref, klin_ref):
    linear = dot(hidden, wk_ref[...], 1, 0)
    klin_ref[...] = linear
    width = gk_ref.shape[1]
    for head, rows in enumerate(key_rows(linear, gk_ref[...], cos_ref[...], sin_ref[...])):
        k_ref[:, head * width : (head + 1) * width] = rows
    v_ref[...] = dot(hidden, wv_ref[...], 1, 0).astype(BF)


def turn_rows(value):
    half = value.shape[0] // 2
    return jnp.concatenate([-value[half:], value[:half]], axis=0)


def own_kernel(count, *refs):
    parts = refs[:count]
    (wq_ref, wk_ref, wv_ref, gq_ref, gk_ref, cos_t_ref, sin_t_ref, cos_ref, sin_ref) = refs[
        count : count + 9
    ]
    qt_ref, qlin_ref, k_ref, v_ref, klin_ref, hidden_ref = refs[count + 9 :]
    share = parts[0].shape[0]
    for j, part in enumerate(parts):
        hidden_ref[j * share : (j + 1) * share, :] = part[...]
    hidden = hidden_ref[...]
    key_value_part(hidden, wk_ref, wv_ref, gk_ref, cos_ref, sin_ref, k_ref, v_ref, klin_ref)
    linear = dot(wq_ref[...], hidden, 0, 1)
    qlin_ref[...] = linear
    width = gq_ref.shape[0]
    for start in range(0, linear.shape[0], width):
        rows = linear[start : start + width]
        factor = lax.rsqrt(jnp.mean(rows * rows, axis=0, keepdims=True) + EPS)
        normed = rows * factor * gq_ref[...]
        qt_ref[start : start + width, :] = (
            normed * cos_t_ref[...] + turn_rows(normed) * sin_t_ref[...]
        ).astype(BF)


def remote_kernel(count, *refs):
    parts = refs[:count]
    wk_ref, wv_ref, gk_ref, cos_ref, sin_ref = refs[count : count + 5]
    k_ref, v_ref, klin_ref, hidden_ref = refs[count + 5 :]
    share = parts[0].shape[1]
    for j, part in enumerate(parts):
        hidden_ref[j * share : (j + 1) * share, :] = part[0]
    key_value_part(
        hidden_ref[...], wk_ref, wv_ref, gk_ref, cos_ref, sin_ref, k_ref, v_ref, klin_ref
    )


def place_slots(target_ref, refs, groups, rows):
    if len(refs) == 1:
        return refs[0]
    for ref, group in zip(refs, groups):
        for i, slot in enumerate(group):
            target_ref[pl.ds(slot * rows, rows), :] = ref[i * rows : (i + 1) * rows, :]
    return target_ref


def lanes_of(ref, half_index, half, width):
    heads = [
        ref[start : start + width, half_index * half : (half_index + 1) * half]
        for start in range(0, ref.shape[0], width)
    ]
    return jnp.concatenate(heads, axis=1)


def attend_kernel(groups, ctx_rows, width, mp, *refs):
    n = len(groups)
    order_ref, last_ref, kpos_ref, qpos_ref, qlow_ref, qt_ref, wo_ref = refs[:7]
    k_refs, v_refs = refs[7 : 7 + n], refs[7 + n : 7 + 2 * n]
    rest = refs[7 + 2 * n :]
    ot_ref, attt_ref, sums_ref = rest[:3]
    part_refs = rest[3 : 3 + mp]
    k_all, v_all, numer, sums, projected = rest[3 + mp :]
    half = ctx_rows // 2
    share = ctx_rows // mp
    per_group = qt_ref.shape[0] // width
    k_all = place_slots(k_all, k_refs, groups, ctx_rows)
    v_all = place_slots(v_all, v_refs, groups, ctx_rows)
    scale = LOG2E / math.sqrt(width)
    for t in range(2):
        queries = lanes_of(qt_ref, t, half, width)
        qpos = jnp.concatenate([qpos_ref[:, t * half : (t + 1) * half]] * per_group, axis=1)
        qlow = jnp.concatenate([qlow_ref[:, t * half : (t + 1) * half]] * per_group, axis=1)
        numer[...] = jnp.zeros_like(numer)
        sums[...] = jnp.zeros_like(sums)

        def step(i, carry):
            start = pl.multiple_of(order_ref[i] * half, half)
            scores = dot(k_all[pl.ds(start, half), :], queries, 1, 0)
            kpos = kpos_ref[...] + i * half
            seen = (kpos <= qpos) & (kpos >= qlow)
            weights = jnp.where(seen, jnp.exp2(scores * scale), 0.0)
            sums[...] += jnp.sum(weights, axis=0, keepdims=True)
            numer[...] += dot(v_all[pl.ds(start, half), :], weights.astype(BF), 0, 0)
            return carry

        lax.fori_loop(0, last_ref[t] + 1, step, 0)
        total = sums[...]
        sums_ref[0, t : t + 1, :] = total
        result = numer[...] / total
        for head in range(per_group):
            piece = result[:, head * half : (head + 1) * half]
            ot_ref[head * width : (head + 1) * width, t * half : (t + 1) * half] = piece
            attt_ref[head * width : (head + 1) * width, t * half : (t + 1) * half] = piece.astype(BF)
    added = dot(attt_ref[...], wo_ref[...], 0, 0)
    group = pl.program_id(0)

    @pl.when(group == 0)
    def _():
        projected[...] = added

    @pl.when(group > 0)
    def _():
        projected[...] += added

    @pl.when(group == pl.num_programs(0) - 1)
    def _():
        for j, ref in enumerate(part_refs):
            ref[...] = projected[j * share : (j + 1) * share, :].astype(ref.dtype)


def feed_kernel(count, *refs):
    peer_ref = refs[0]
    parts = refs[1 : 1 + count]
    grad_ref, wg_ref, wu_ref, wd_ref = refs[1 + count : 5 + count]
    hidden_ref, grads_ref, act_ref, gg_ref, ug_ref = refs[5 + count : 10 + count]
    part_refs = refs[10 + count : 10 + 2 * count]
    total = refs[10 + 2 * count]
    share = parts[0].shape[0]
    step = pl.program_id(0)

    @pl.when(step == 0)
    def _():
        for j, part in enumerate(parts):
            hidden_ref[j * share : (j + 1) * share, :] = part[...]
            place = pl.multiple_of(peer_ref[j] * share, share)
            grads_ref[j * share : (j + 1) * share, :] = grad_ref[pl.ds(place, share), :]

    hidden = hidden_ref[...]
    gate = dot(hidden, wg_ref[...], 1, 0)
    up = dot(hidden, wu_ref[...], 1, 0)
    act_grad = dot(grads_ref[...], wd_ref[...], 1, 1)
    sig = 1.0 / (1.0 + jnp.exp(-gate))
    silu = gate * sig
    act_ref[...] = (silu * up).astype(BF)
    gate_grad = (act_grad * up * sig * (1.0 + gate * (1.0 - sig))).astype(BF)
    up_grad = (act_grad * silu).astype(BF)
    gg_ref[...] = gate_grad
    ug_ref[...] = up_grad
    added = dot(gate_grad, wg_ref[...], 1, 1) + dot(up_grad, wu_ref[...], 1, 1)

    @pl.when(step == 0)
    def _():
        total[...] = added

    @pl.when(step > 0)
    def _():
        total[...] += added

    @pl.when(step == pl.num_programs(0) - 1)
    def _():
        for j, ref in enumerate(part_refs):
            ref[...] = total[j * share : (j + 1) * share, :].astype(ref.dtype)


def feed_weights_kernel(hidden_ref, grads_ref, act_ref, gg_ref, ug_ref, wd_ref, *refs):
    dg_ref, du_ref, dd_ref = refs[:3]
    *part_refs, total = refs[3:]
    share = part_refs[0].shape[0]
    step = pl.program_id(0)
    dg_ref[...] = dot(hidden_ref[...], gg_ref[...], 0, 0).astype(BF)
    du_ref[...] = dot(hidden_ref[...], ug_ref[...], 0, 0).astype(BF)
    dd_ref[...] = dot(act_ref[...], grads_ref[...], 0, 0).astype(BF)
    added = dot(act_ref[...], wd_ref[...], 1, 0)

    @pl.when(step == 0)
    def _():
        total[...] = added

    @pl.when(step > 0)
    def _():
        total[...] += added

    @pl.when(step == pl.num_programs(0) - 1)
    def _():
        for j, ref in enumerate(part_refs):
            ref[...] = total[j * share : (j + 1) * share, :].astype(ref.dtype)


def attend_back_kernel(groups, ctx_rows, width, mp, *refs):
    n = len(groups)
    order_ref, last_ref, kpos_ref, qpos_ref, qlow_ref = refs[:5]
    low_refs = refs[5 : 5 + mp]
    wo_ref, qt_ref, qlin_ref, ot_ref, sums_ref, gq_ref, cos_t_ref, sin_t_ref = refs[
        5 + mp : 13 + mp
    ]
    at = 13 + mp
    k_refs, v_refs = refs[at : at + n], refs[at + n : at + 2 * n]
    at += 2 * n
    ql_ref, dk, dv, gqg_ref = refs[at : at + 4]
    k_all, v_all, dq, low_all, dqt = refs[at + 4 :]
    half = ctx_rows // 2
    share = ctx_rows // mp
    per_group = qt_ref.shape[0] // width
    scale = LOG2E / math.sqrt(width)
    score_scale = 1.0 / math.sqrt(width)
    group = pl.program_id(0)
    k_all = place_slots(k_all, k_refs, groups, ctx_rows)
    v_all = place_slots(v_all, v_refs, groups, ctx_rows)
    dk[...] = jnp.zeros_like(dk)
    dv[...] = jnp.zeros_like(dv)

    @pl.when(group == 0)
    def _():
        for j, ref in enumerate(low_refs):
            low_all[j * share : (j + 1) * share, :] = ref[...]
        gqg_ref[...] = jnp.zeros_like(gqg_ref)

    att_grad = dot(wo_ref[...], low_all[...], 1, 1).astype(BF).astype(F32)
    for t in range(2):
        queries = lanes_of(qt_ref, t, half, width)
        pre = lanes_of(ot_ref, t, half, width)
        grads = jnp.concatenate(
            [
                att_grad[h * width : (h + 1) * width, t * half : (t + 1) * half]
                for h in range(per_group)
            ],
            axis=1,
        )
        inverse = 1.0 / sums_ref[0, t : t + 1, :]
        scaled = (grads * inverse).astype(BF)
        shift = jnp.sum(grads * pre, axis=0, keepdims=True) * inverse
        qpos = jnp.concatenate([qpos_ref[:, t * half : (t + 1) * half]] * per_group, axis=1)
        qlow = jnp.concatenate([qlow_ref[:, t * half : (t + 1) * half]] * per_group, axis=1)
        dq[...] = jnp.zeros_like(dq)

        def step(i, carry):
            start = pl.multiple_of(order_ref[i] * half, half)
            keys = k_all[pl.ds(start, half), :]
            scores = dot(keys, queries, 1, 0)
            prob_grad = dot(v_all[pl.ds(start, half), :], scaled, 1, 0)
            kpos = kpos_ref[...] + i * half
            seen = (kpos <= qpos) & (kpos >= qlow)
            weights = jnp.where(seen, jnp.exp2(scores * scale), 0.0)
            score_grad = (weights * (prob_grad - shift)).astype(BF)
            dv[pl.ds(start, half), :] += dot(weights.astype(BF), scaled, 1, 1)
            dk[pl.ds(start, half), :] += dot(score_grad, queries, 1, 1)
            dq[...] += dot(keys, score_grad, 0, 0)
            return carry

        lax.fori_loop(0, last_ref[t] + 1, step, 0)
        for head in range(per_group):
            dqt[head * width : (head + 1) * width, t * half : (t + 1) * half] = dq[
                :, head * half : (head + 1) * half
            ]
    for head in range(per_group):
        rows = qlin_ref[head * width : (head + 1) * width, :]
        rotated = dqt[head * width : (head + 1) * width, :] * score_scale
        gradient = rotated * cos_t_ref[...] - turn_rows(rotated) * sin_t_ref[...]
        factor = lax.rsqrt(jnp.mean(rows * rows, axis=0, keepdims=True) + EPS)
        gained = gradient * gq_ref[...]
        inner = jnp.mean(gained * rows, axis=0, keepdims=True)
        ql_ref[head * width : (head + 1) * width, :] = (
            factor * gained - rows * (factor * factor * factor) * inner
        ).astype(BF)
        gqg_ref[...] += jnp.sum(gradient * rows * factor, axis=1, keepdims=True)


def hidden_back_kernel(own, mp, *refs):
    if own:
        ql_ref, wq_ref, *refs = refs
    dk_ref, dv_ref, klin_ref, cos_ref, sin_ref, gk_ref, wk_ref, wv_ref = refs[:8]
    kl_ref, vl_ref, gkg_ref = refs[8:11]
    part_refs = refs[11:]
    share = part_refs[0].shape[1]
    width = gk_ref.shape[1]
    score_scale = 1.0 / math.sqrt(width)

    @pl.when(pl.program_id(0) == 0)
    def _():
        gkg_ref[...] = jnp.zeros_like(gkg_ref)

    for start in range(0, dk_ref.shape[1], width):
        head = slice(start, start + width)
        rotated = dk_ref[:, head] * score_scale
        gradient = rotated * cos_ref[...] - pltpu.roll(rotated, width // 2, 1) * sin_ref[...]
        back, terms = norm_back(klin_ref[:, head], gk_ref[...], gradient)
        kl_ref[:, head] = back.astype(BF)
        gkg_ref[...] += jnp.sum(terms, axis=0, keepdims=True)
    vl_ref[...] = dv_ref[...].astype(BF)
    total = dot(kl_ref[...], wk_ref[...], 1, 1) + dot(vl_ref[...], wv_ref[...], 1, 1)
    if own:
        total = total + dot(ql_ref[...], wq_ref[...], 0, 1)
    for j, ref in enumerate(part_refs):
        ref[0] = total[j * share : (j + 1) * share, :].astype(ref.dtype)


def weights_kernel(groups, mp, *refs):
    n = len(groups)
    core_ref, ql_ref, attt_ref = refs[:3]
    hidden_refs, kl_refs, vl_refs = refs[3 : 3 + n], refs[3 + n : 3 + 2 * n], refs[3 + 2 * n : 3 + 3 * n]
    low_refs = refs[3 + 3 * n : 3 + 3 * n + mp]
    wq_ref, wk_ref, wv_ref, gain_ref, mine_ref, other_ref, gain_grad_ref, accum, low_all, keep = refs[
        3 + 3 * n + mp :
    ]
    step = pl.program_id(0)
    model = gain_ref.shape[0]
    q_width, k_width = ql_ref.shape[0], kl_refs[0].shape[1]
    share = low_refs[0].shape[0]

    @pl.when(step == 0)
    def _():
        for j, ref in enumerate(low_refs):
            low_all[j * share : (j + 1) * share, :] = ref[...]
        keep[:model, :q_width] = dot(hidden_refs[0][...], ql_ref[...], 0, 1)
        keep[model:, :] = dot(attt_ref[...], low_all[...], 1, 0)
        accum[...] = jnp.zeros_like(accum)

    first = 0
    for hidden_ref, kl_ref, vl_ref, slots in zip(hidden_refs, kl_refs, vl_refs, groups):

        @pl.when((step >= first) & (step < first + len(slots)))
        def _():
            hidden = hidden_ref[...]
            accum[:, :k_width] += dot(hidden, kl_ref[...], 0, 0)
            accum[:, k_width:] += dot(hidden, vl_ref[...], 0, 0)

        first += len(slots)

    @pl.when(step == pl.num_programs(0) - 1)
    def _():
        keep[:model, q_width:] = accum[...]
        terms = jnp.sum(keep[:model, :q_width] * wq_ref[...].astype(F32), axis=1, keepdims=True)
        terms += jnp.sum(accum[:, :k_width] * wk_ref[...].astype(F32), axis=1, keepdims=True)
        terms += jnp.sum(accum[:, k_width:] * wv_ref[...].astype(F32), axis=1, keepdims=True)
        gain_grad_ref[...] = terms / gain_ref[...]
        rows = mine_ref.shape[0]
        core = core_ref[0]
        mine_ref[...] = keep[pl.ds(pl.multiple_of(core * rows, rows), rows), :].astype(BF)
        other_ref[...] = keep[pl.ds(pl.multiple_of((1 - core) * rows, rows), rows), :].astype(BF)


def split_kernel(place_ref, mine_ref, got_ref, *refs):
    rows = refs[0].shape[0]
    for k, ref in enumerate(refs):
        here = pl.ds(pl.multiple_of(place_ref[k] * rows, rows), rows)
        ref[...] = (mine_ref[here, :].astype(F32) + got_ref[here, :].astype(F32)).astype(ref.dtype)


def spread_kernel(q_width, k_width, model, *refs):
    place_ref = refs[0]
    *chunks, dq_ref, dk_ref, dv_ref, do_ref, full = refs[1:]
    rows = chunks[0].shape[0]
    for i, ref in enumerate(chunks):
        full[pl.ds(pl.multiple_of(place_ref[i] * rows, rows), rows), :] = ref[...].astype(F32)
    dq_ref[...] = full[:model, :q_width]
    dk_ref[...] = full[:model, q_width : q_width + k_width]
    dv_ref[...] = full[:model, q_width + k_width :]
    do_ref[...] = full[model:, :]


def slot_blocks(group, rows, width):
    first = group[0]
    gap = group[1] - group[0] if len(group) > 1 else 1
    return pl.BlockSpec((rows, width), lambda i: (first + gap * i, 0))


def on_device(
    tokens,
    norm1_gain,
    q_weight,
    key_matrix,
    value_matrix,
    q_gain,
    k_gain,
    o_weight,
    norm2_gain,
    gate_weight,
    up_weight,
    down_weight,
    out_grad,
    lengths,
    pairing,
):
    width = q_gain.shape[0]
    model = tokens.shape[2]
    share = tokens.shape[1]
    mp = lax.axis_size("mp")
    ctx = lax.axis_size("ctx")
    q_width = q_weight.shape[1]
    k_width = key_matrix.shape[1]
    kv_heads = k_width // width
    group_width = q_width // kv_heads
    feed = gate_weight.shape[1]
    ctx_rows = share * mp
    half = ctx_rows // 2
    seq_rows = ctx_rows * ctx
    few = ctx <= 4
    here_ctx = lax.axis_index("ctx")
    here_mp = lax.axis_index("mp")
    here_dp = lax.axis_index("dp")
    gain1 = norm1_gain.astype(F32)[None, :]
    gain2 = norm2_gain.astype(F32)[None, :]
    gq_col = q_gain.astype(F32)[:, None]
    gk_row = k_gain.astype(F32)[None, :]
    tok = tokens[0]
    og = out_grad[0]

    h1_share = call(norm_kernel, [tok, gain1], [out((share, model), BF)], name="norm1")[0]
    own_parts = [h1_share] + swaps([h1_share] * mp, "mp")
    if few:
        near = [from_ctx(h1_share, k) for k in range(1, ctx)]
        if ctx == 4:
            remote = [((1, 3), jnp.stack([near[0], near[2]])), ((2,), near[1][None])]
        else:
            remote = [(tuple(range(1, ctx)), jnp.stack(near))]
    else:
        every = lax.all_gather(h1_share, "ctx", axis=0)
        every = jnp.concatenate([every, every], axis=0)
        every = lax.dynamic_slice_in_dim(every, here_ctx + 1, ctx - 1, 0)
        remote = [(tuple(range(1, ctx)), every)]
    remote_parts = [[value] + swaps([value] * mp, "mp") for _, value in remote]
    groups = [(0,)] + [slots for slots, _ in remote]

    slot_ctx = (here_ctx + jnp.arange(ctx, dtype=jnp.int32)) % ctx
    slot_pair = jnp.sum(
        jnp.where(slot_ctx[:, None] == jnp.arange(ctx, dtype=jnp.int32)[None, :], pairing[None, :], 0),
        axis=1,
    )
    peers = here_mp ^ jnp.arange(mp, dtype=jnp.int32)
    rows_in = (peers[:, None] * share + jnp.arange(share, dtype=jnp.int32)[None, :]).reshape(-1)
    blocks = jnp.where(
        rows_in[None, :] < half, slot_pair[:, None], 2 * ctx - 1 - slot_pair[:, None]
    )
    positions = (blocks * half + (rows_in % half)[None, :]).reshape(-1)
    block_ids = blocks[:, ::half].reshape(-1)
    block_order = jnp.sum(
        jnp.where(
            block_ids[None, :] == jnp.arange(2 * ctx, dtype=jnp.int32)[:, None],
            jnp.arange(2 * ctx, dtype=jnp.int32)[None, :],
            0,
        ),
        axis=1,
    )
    last_block = block_ids[:2]
    own_pos = positions[:ctx_rows]
    doc_ends = jnp.cumsum(lengths[0])
    own_low = jnp.max(
        jnp.where(doc_ends[None, :] <= own_pos[:, None], doc_ends[None, :], 0), axis=1
    )
    qpos, qlow, kpos = own_pos[None, :], own_low[None, :], (rows_in % half)[:half, None]
    frequency = THETA ** (-(jnp.arange(width // 2, dtype=F32) * 2.0) / width)
    angles = positions.astype(F32)[:, None] * frequency[None, :]
    cos_half, sin_half = jnp.cos(angles), jnp.sin(angles)
    cosines = jnp.concatenate([cos_half, cos_half], axis=1)
    sines = jnp.concatenate([-sin_half, sin_half], axis=1)
    angles_t = frequency[:, None] * own_pos.astype(F32)[None, :]
    cos_t, sin_t = jnp.cos(angles_t), jnp.sin(angles_t)
    cosines_t = jnp.concatenate([cos_t, cos_t], axis=0)
    sines_t = jnp.concatenate([sin_t, sin_t], axis=0)

    qt, qlin, k_own, v_own, klin_own, h1_own = call(
        lambda *refs: own_kernel(mp, *refs),
        own_parts
        + [q_weight, key_matrix, value_matrix, gq_col, gk_row, cosines_t, sines_t, cosines, sines],
        [
            out((q_width, ctx_rows), BF),
            out((q_width, ctx_rows), F32),
            out((ctx_rows, k_width), BF),
            out((ctx_rows, k_width), BF),
            out((ctx_rows, k_width), F32),
            out((ctx_rows, model), BF),
        ],
        in_specs={
            mp + 7: pl.BlockSpec((ctx_rows, width), lambda i: (0, 0)),
            mp + 8: pl.BlockSpec((ctx_rows, width), lambda i: (0, 0)),
        },
        flops=2 * ctx_rows * model * (q_width + 2 * k_width),
        name="own_rows",
    )
    keys, values, klins, hiddens = [k_own], [v_own], [klin_own], [h1_own]
    for (slots, _), parts in zip(remote, remote_parts):
        size = len(slots)
        k_new, v_new, klin_new, h1_new = call(
            lambda *refs: remote_kernel(mp, *refs),
            parts + [key_matrix, value_matrix, gk_row, cosines, sines],
            [
                out((size * ctx_rows, k_width), BF),
                out((size * ctx_rows, k_width), BF),
                out((size * ctx_rows, k_width), F32),
                out((size * ctx_rows, model), BF),
            ],
            grid=(size,),
            in_specs={
                **{j: pl.BlockSpec((1, share, model), lambda i: (i, 0, 0)) for j in range(mp)},
                mp + 3: slot_blocks(slots, ctx_rows, width),
                mp + 4: slot_blocks(slots, ctx_rows, width),
            },
            out_specs={
                0: pl.BlockSpec((ctx_rows, k_width), lambda i: (i, 0)),
                1: pl.BlockSpec((ctx_rows, k_width), lambda i: (i, 0)),
                2: pl.BlockSpec((ctx_rows, k_width), lambda i: (i, 0)),
                3: pl.BlockSpec((ctx_rows, model), lambda i: (i, 0)),
            },
            flops=4 * size * ctx_rows * model * k_width,
            name="remote_rows",
        )
        keys.append(k_new)
        values.append(v_new)
        klins.append(klin_new)
        hiddens.append(h1_new)

    if few:
        joined, buffers = groups, {}
    else:
        joined = [tuple(range(ctx))]
        keys, values = [jnp.concatenate(keys, axis=0)], [jnp.concatenate(values, axis=0)]
        buffers = {"pipeline_mode": pl.Buffered(1)}
    by_head = [
        pl.BlockSpec((ctx_rows * len(slots), width), lambda h: (0, h), **buffers) for slots in joined
    ]
    n = len(joined)
    copies = [pltpu.VMEM((seq_rows if few else 16, width), BF)] * 2
    lanes = group_width // width * half
    t_block = pl.BlockSpec((group_width, ctx_rows), lambda h: (h, 0))
    wo_block = pl.BlockSpec((group_width, model), lambda h: (h, 0))
    sums_block = pl.BlockSpec((1, 2, lanes), lambda h: (h, 0, 0))
    pair_flops = 2 * q_width * ctx_rows * seq_rows
    ot, att_t, sums, *o_parts = call(
        lambda *refs: attend_kernel(joined, ctx_rows, width, mp, *refs),
        [block_order, last_block, kpos, qpos, qlow, qt, o_weight] + keys + values,
        [
            out((q_width, ctx_rows), F32),
            out((q_width, ctx_rows), BF),
            out((kv_heads, 2, lanes), F32),
            out((share, model), F32),
        ]
        + [out((share, model), BF)] * (mp - 1),
        grid=(kv_heads,),
        in_specs={
            0: SMEM,
            1: SMEM,
            5: t_block,
            6: wo_block,
            **{7 + i: by_head[i] for i in range(n)},
            **{7 + n + i: by_head[i] for i in range(n)},
        },
        out_specs={0: t_block, 1: t_block, 2: sums_block},
        scratch=copies
        + [
            pltpu.VMEM((width, lanes), F32),
            pltpu.VMEM((1, lanes), F32),
            pltpu.VMEM((ctx_rows, model), F32),
        ],
        flops=2 * pair_flops,
        name="attend",
    )
    resid, h2_share = call(
        resid_kernel,
        [tok, o_parts[0]] + swaps(o_parts, "mp") + [gain2],
        [out((share, model), F32), out((share, model), BF)],
        name="resid",
    )

    grad_full = lax.all_gather(og, "mp", axis=0, tiled=True)
    tile = 256 if feed % 256 == 0 else feed
    col_block = pl.BlockSpec((model, tile), lambda i: (0, i))
    row_block = pl.BlockSpec((tile, model), lambda i: (i, 0))
    act_block = pl.BlockSpec((ctx_rows, tile), lambda i: (0, i))
    h2_full, og_full, act, gate_grad, up_grad, *h2_parts = call(
        lambda *refs: feed_kernel(mp, *refs),
        [peers, h2_share]
        + swaps([h2_share] * mp, "mp")
        + [grad_full, gate_weight, up_weight, down_weight],
        [out((ctx_rows, model), BF)] * 2
        + [out((ctx_rows, feed), BF)] * 3
        + [out((share, model), F32)]
        + [out((share, model), BF)] * (mp - 1),
        grid=(feed // tile,),
        in_specs={0: SMEM, mp + 2: col_block, mp + 3: col_block, mp + 4: row_block},
        out_specs={2: act_block, 3: act_block, 4: act_block},
        scratch=[pltpu.VMEM((ctx_rows, model), F32)],
        flops=10 * ctx_rows * model * feed,
        name="feed",
    )
    h2_got = swaps(h2_parts, "mp")
    dg, du, dd, *f_parts = call(
        feed_weights_kernel,
        [h2_full, og_full, act, gate_grad, up_grad, down_weight],
        [out((model, feed), BF)] * 2
        + [out((feed, model), BF), out((share, model), F32)]
        + [out((share, model), BF)] * (mp - 1),
        grid=(feed // tile,),
        in_specs={2: act_block, 3: act_block, 4: act_block, 5: row_block},
        out_specs={0: col_block, 1: col_block, 2: row_block},
        scratch=[pltpu.VMEM((ctx_rows, model), F32)],
        flops=8 * ctx_rows * model * feed,
        name="feed_weights",
    )
    dg, du, dd = lax.psum((dg, du, dd), ("dp", "ctx"))

    resid_grad, low_share, gain2_part = call(
        resid_back_kernel,
        [resid, og, gain2, h2_parts[0]] + h2_got,
        [out((share, model), F32), out((share, model), BF), out((1, model), F32)],
        name="resid_back",
    )
    low_parts = [low_share] + swaps([low_share] * mp, "mp")

    head_rows = pl.BlockSpec((seq_rows, width), lambda h: (0, h), **buffers)
    ql, dk, dv, gq_part = call(
        lambda *refs: attend_back_kernel(joined, ctx_rows, width, mp, *refs),
        [block_order, last_block, kpos, qpos, qlow]
        + low_parts
        + [o_weight, qt, qlin, ot, sums, gq_col, cosines_t, sines_t]
        + keys
        + values,
        [
            out((q_width, ctx_rows), BF),
            out((seq_rows, k_width), F32),
            out((seq_rows, k_width), F32),
            out((width, 1), F32),
        ],
        grid=(kv_heads,),
        in_specs={
            0: SMEM,
            1: SMEM,
            5 + mp: wo_block,
            6 + mp: t_block,
            7 + mp: t_block,
            8 + mp: t_block,
            9 + mp: sums_block,
            **{13 + mp + m * n + i: by_head[i] for m in range(2) for i in range(n)},
        },
        out_specs={0: t_block, 1: head_rows, 2: head_rows},
        scratch=copies
        + [
            pltpu.VMEM((width, lanes), F32),
            pltpu.VMEM((ctx_rows, model), BF),
            pltpu.VMEM((group_width, ctx_rows), F32),
        ],
        flops=5 * pair_flops,
        name="attend_back",
    )

    f_got = swaps(f_parts, "mp")
    output = call(
        sum_kernel, [resid, f_parts[0]] + f_got, [out((share, model), BF)], name="output"
    )[0][None]

    lows = {}

    def hidden_back(slots):
        size = len(slots)
        own = slots == (0,)
        at = groups.index(slots)
        ins = ([ql, q_weight] if own else []) + [
            dk, dv, klins[at], cosines, sines, gk_row, key_matrix, value_matrix
        ]
        skip = 2 if own else 0
        block = slot_blocks(slots, ctx_rows, k_width)
        table = slot_blocks(slots, ctx_rows, width)
        here = pl.BlockSpec((ctx_rows, k_width), lambda i: (i, 0))
        kl, vl, gk_part, *parts = call(
            lambda *refs: hidden_back_kernel(own, mp, *refs),
            ins,
            [out((size * ctx_rows, k_width), BF)] * 2
            + [out((1, width), F32), out((size, share, model), F32)]
            + [out((size, share, model), BF)] * (mp - 1),
            grid=(size,),
            in_specs={skip: block, skip + 1: block, skip + 2: here, skip + 3: table, skip + 4: table},
            out_specs={
                0: here,
                1: here,
                **{3 + j: pl.BlockSpec((1, share, model), lambda i: (i, 0, 0)) for j in range(mp)},
            },
            flops=4 * size * ctx_rows * model * k_width,
            name="hidden_back",
        )
        lows[at] = (kl, vl, gk_part)
        return parts, swaps(parts, "mp")

    terms = []
    if few:
        for slots in ([(2,), (1, 3)] if ctx == 4 else [tuple(range(1, ctx))]):
            parts, got = hidden_back(slots)
            for i, slot in enumerate(slots):
                summed = sum_parts([p[i] for p in [parts[0]] + got], BF)
                terms.append(to_ctx(summed, slot))
    else:
        parts, got = hidden_back(tuple(range(1, ctx)))
        summed = (parts[0] + sum(p.astype(F32) for p in got)).astype(BF)
        padded = jnp.concatenate([jnp.zeros_like(summed[:1]), summed], axis=0)
        padded = jnp.concatenate([padded, padded], axis=0)
        natural = lax.dynamic_slice_in_dim(padded, (ctx - here_ctx) % ctx, ctx, 0)
        terms.append(lax.psum_scatter(natural, "ctx", scatter_dimension=0, tiled=False))
    parts, got = hidden_back((0,))
    terms = [p[0] for p in [parts[0]] + got] + terms
    input_grad = call(
        input_back_kernel, [tok, resid_grad, gain1] + terms, [out((share, model), F32)], name="input_back"
    )[0][None]

    total_rows = model + q_width
    kls, vls, gk_parts = zip(*[lows[i] for i in range(len(groups))])
    gk_part = sum(gk_parts[1:], gk_parts[0])
    m = len(groups)
    starts = [sum(len(slots) for slots in groups[:i]) for i in range(m)]

    def stepped(i, rows, columns):
        first, size = starts[i], len(groups[i])
        return pl.BlockSpec((rows, columns), lambda s: (jnp.clip(s - first, 0, size - 1), 0))

    mine, other, gain1_part = call(
        lambda *refs: weights_kernel(groups, mp, *refs),
        [here_dp[None], ql, att_t]
        + hiddens
        + list(kls)
        + list(vls)
        + low_parts
        + [q_weight, key_matrix, value_matrix, norm1_gain.astype(F32)[:, None]],
        [out((total_rows // 2, q_width + 2 * k_width), BF)] * 2 + [out((model, 1), F32)],
        grid=(ctx,),
        in_specs={
            0: SMEM,
            **{3 + i: stepped(i, ctx_rows, model) for i in range(m)},
            **{3 + m + i: stepped(i, ctx_rows, k_width) for i in range(m)},
            **{3 + 2 * m + i: stepped(i, ctx_rows, k_width) for i in range(m)},
        },
        scratch=[
            pltpu.VMEM((model, 2 * k_width), F32),
            pltpu.VMEM((ctx_rows, model), BF),
            pltpu.VMEM((total_rows, q_width + 2 * k_width), F32),
        ],
        flops=2 * model * (ctx_rows * q_width * 2 + 2 * seq_rows * k_width),
        name="weights",
    )
    got = swap(other, "dp", 1)
    if few:
        rows = total_rows // 2 // ctx
        places = slot_ctx
        pieces = call(
            split_kernel,
            [places, mine, got],
            [out((rows, mine.shape[1]), F32)] + [out((rows, mine.shape[1]), BF)] * (ctx - 1),
            in_specs={0: SMEM},
            name="split",
        )
        chunk = sum_parts(
            [pieces[0]] + [to_ctx(pieces[k], k) for k in range(1, ctx)], BF
        )
        chunks = [chunk] + [from_ctx(chunk, k) for k in range(1, ctx)]
        chunks = chunks + [swap(c, "dp", 1) for c in chunks]
        spots = jnp.concatenate([places + here_dp * ctx, places + (1 - here_dp) * ctx])
    else:
        chunk = lax.psum(sum_parts([mine, got], BF), "ctx")
        chunks = [chunk, swap(chunk, "dp", 1)]
        spots = jnp.stack([here_dp, 1 - here_dp])
    q_w_grad, k_w_grad, v_w_grad, o_w_grad = call(
        lambda *refs: spread_kernel(q_width, k_width, model, *refs),
        [spots] + chunks,
        [
            out((model, q_width), F32),
            out((model, k_width), F32),
            out((model, k_width), F32),
            out((q_width, model), F32),
        ],
        in_specs={0: SMEM},
        scratch=[pltpu.VMEM((total_rows, q_width + 2 * k_width), F32)],
        name="spread",
    )

    gains = jnp.concatenate(
        [gain1_part.reshape(-1), gain2_part.reshape(-1), gq_part.reshape(-1), gk_part.reshape(-1)]
    )
    if few:
        gains = gains + swap(gains, "dp", 1)
        gains = sum(swaps([gains] * mp, "mp"), gains)
        gains = sum([from_ctx(gains, k) for k in range(1, ctx)], gains)
    else:
        gains = lax.psum(gains, ("dp", "ctx", "mp"))
    return (
        output,
        input_grad,
        gains[:model],
        q_w_grad,
        k_w_grad,
        v_w_grad,
        gains[2 * model : 2 * model + width],
        gains[2 * model + width :],
        o_w_grad,
        gains[model : 2 * model],
        dg.astype(F32),
        du.astype(F32),
        dd.astype(F32),
    )


def solution(mesh):
    placed = (
        P("dp", ("ctx", "mp"), None),
        P(),
        P(None, "mp"),
        P(None, "mp"),
        P(None, "mp"),
        P(),
        P(),
        P("mp", None),
        P(),
        P(None, "mp"),
        P(None, "mp"),
        P("mp", None),
        P("dp", ("ctx", "mp"), None),
        P("dp", None),
        P(),
    )
    return jax.shard_map(
        on_device,
        mesh=mesh,
        in_specs=placed,
        out_specs=(
            P("dp", ("ctx", "mp"), None),
            P("dp", ("ctx", "mp"), None),
            P(),
            P(None, "mp"),
            P(None, "mp"),
            P(None, "mp"),
            P(),
            P(),
            P("mp", None),
            P(),
            P(None, "mp"),
            P(None, "mp"),
            P("mp", None),
        ),
        check_vma=False,
    )
```

time: 754 us -> 432 us (0.57)
  waiting for transfers between devices: 533 us -> 198 us
  Pallas kernels: 0 us -> 100 us
  matrix products: 94.9 us -> 0 us
  starting transfers between devices: 1.17 us -> 84.8 us
  blocking collectives: 39.6 us -> 0 us
  other arithmetic: 38 us -> 18 us
  local copies, waits for them, and re-layouts: 23.7 us -> 13.8 us
    psum x1, waiting for transfers between devices: 308 us -> 12.5 us  [on_device(): dg, du, dd = lax.psum((dg, du, dd), ('dp', 'ctx'))]
    ppermute x0 -> x57, waiting for transfers between devices: none -> 186 us  [the longest x6 93.5 us: to_ctx(): lax.ppermute(value, 'ctx', [(i, (i + step) % size) for i in range(size)])]
    all_gather x6 -> x1, waiting for transfers between devices: 135 us -> 0.01 us  [on_device(): grad_full = lax.all_gather(og, 'mp', axis=0, tiled=True)]
    pallas_call x0 -> x22, Pallas kernels: none -> 100 us  [call(): pl.pallas_call(kernel, grid=grid, in_specs=[in_specs.get(i, whole_spec(a)...]
    dot_general x27 -> x0, matrix products: 94.9 us -> none  [the longest x20 78 us: product(): return jnp.einsum(form, left, right, preferred_element_type=jnp.float32)]
    reduce_scatter x6 -> x0, waiting for transfers between devices: 89.2 us -> none  [the longest x4 61.4 us: sum_rows(): lax.psum_scatter(value_rows.astype(jnp.bfloat16), 'mp', scatter_dimension...]
    ppermute x0 -> x57, starting transfers between devices: none -> 84.7 us  [the longest x42 43 us: swap(): return lax.ppermute(value, axis, [(i, i ^ step) for i in range(size)])]
    psum x1 -> x0, blocking collectives: 39.6 us -> none  [on_device(): lax.psum((jnp.sum(norm1_terms, axis=0), jnp.sum(norm2_terms, axis=0), jnp...]
  transfers between devices with their start and end apart: 13 -> 59, of which waited for: 12 -> 24; matrix products, arithmetic and copies ran while one was open for 11% -> 5% of each run, Pallas kernels for 0% -> 10%
where the time goes in v1:
time: 432 us; the launch traced here: 430 us
  waiting for transfers between devices  198 us (46%)
  Pallas kernels  100 us (23%)
  starting transfers between devices  84.8 us (20%)
  other arithmetic  18 us (4%)
  between operations  14.6 us (3%)
  local copies, waits for them, and re-layouts  13.8 us (3%)
    pallas_call x22, Pallas kernels, call(): pl.pallas_call(kernel, grid=grid, in_specs=[in_specs.get(i, whole_spec(a)...  100 us
    ppermute x6, waiting for transfers between devices, to_ctx(): lax.ppermute(value, 'ctx', [(i, (i + step) % size) for i in range(size)])  93.5 us
    ppermute x42, waiting for transfers between devices, swap(): return lax.ppermute(value, axis, [(i, i ^ step) for i in range(size)])  81.4 us
    ppermute x42, starting transfers between devices, swap(): return lax.ppermute(value, axis, [(i, i ^ step) for i in range(size)])  43 us
    ppermute x9, starting transfers between devices, from_ctx(): lax.ppermute(value, 'ctx', [((i + step) % size, i) for i in range(size)])  31.8 us
    psum x1, waiting for transfers between devices, on_device(): dg, du, dd = lax.psum((dg, du, dd), ('dp', 'ctx'))  12.5 us
    ppermute x9, waiting for transfers between devices, from_ctx(): lax.ppermute(value, 'ctx', [((i + step) % size, i) for i in range(size)])  10.6 us
    ppermute x6, starting transfers between devices, to_ctx(): lax.ppermute(value, 'ctx', [(i, (i + step) % size) for i in range(size)])  9.97 us
  transfers between devices with their start and end apart: 59, of which 24 were waited for; matrix products, arithmetic and copies ran while one was open for 5% of the time, Pallas kernels for 10%

profile of v1, /device:TPU:0, one launch (start us, length us, event | category | flops | bytes accessed | tf_op | source)
XLA Modules:
  0.0 429.6 jit_solution(4406647133181976166)
XLA Ops:
  20.0 3.7 fusion
  31.6 8.2 %collective-permute-done.8 = bf16[128,1024]{1,0:T(8,128)(2,1)S(1)} collective-permute-done((bf16[128,1024]{1,0:T(8,128)(2,1)S(1)}, bf16[128,1024]{1,0:T(8,128)(2,1)S(1)}, u32[]{:S(2)}, u32[]{:S(2)}) %collective-permute-start.8) | collective-permute-done | bytes 262176 | tf_op jit(solution)/shard_map/ppermute | solution.py:66
  41.2 27.3 %collective-permute-done.9.refs_1_ = bf16[1,128,1024]{2,1,0:T(8,128)(2,1)S(1)} collective-permute-done((bf16[1,128,1024]{2,1,0:T(8,128)(2,1)S(1)}, bf16[1,128,1024]{2,1,0:T(8,128)(2,1)S(1)}, u32[]{:S(2)}, u32[]{:S(2)}) %collective-permute-start.9) | collective-permute-done | bytes 262176 | tf_op jit(solution)/shard_map/ppermute | solution.py:55
  71.1 4.5 %own_rows.1 = (bf16[512,512]{1,0:T(8,128)(2,1)}, f32[512,512]{1,0:T(8,128)}, bf16[512,256]{1,0:T(8,128)(2,1)S(1)}, bf16[512,256]{1,0:T(8,128)(2,1)S(1)}, f32[512,256]{1,0:T(8,128)}, /*index=5*/bf16[512,1024]{1,0:T(8,128)(2,1)}) custom-call(bf16[128,1024]{1,0:T(8,128)(2,1)S(1)} %norm1.1.refs_0_, bf16[128,1024]{1,0:T(8,128)(2,1)S(1)} %collective-permute-done.refs_1_, ...), custom_call_target="tpu_custom_call" | custom-call | flops 1073741824 | bytes 9438208 | tf_op jit(solution)/shard_map/own_rows/pallas_call | solution.py:36
  76.8 3.7 remote_rows.3
  80.5 5.7 %remote_rows.2 = (bf16[1024,256]{1,0:T(8,128)(2,1)S(1)}, bf16[1024,256]{1,0:T(8,128)(2,1)S(1)}, f32[1024,256]{1,0:T(8,128)}, bf16[1024,1024]{1,0:T(8,128)(2,1)}) custom-call(bf16[2,128,1024]{2,1,0:T(8,128)(2,1)S(1)} %pad_maximum_fusion.2.refs_0_, bf16[2,128,1024]{2,1,0:T(8,128)(2,1)} %collective-permute-done.5.refs_1_, ...), custom_call_target="tpu_custom_call" | custom-call | flops 1073741824 | bytes 9437696 | tf_op jit(solution)/shard_map/remote_rows/pallas_call | solution.py:36
  88.0 11.3 %attend.1 = (f32[512,512]{1,0:T(8,128)}, bf16[512,512]{1,0:T(8,128)(2,1)}, f32[2,2,512]{2,1,0:T(2,128)S(1)}, f32[128,1024]{1,0:T(8,128)}, bf16[128,1024]{1,0:T(8...) custom-call(s32[8]{0:T(128)S(1)} %select_reduce_fusion.1.refs_0_, ...), custom_call_target="tpu_custom_call" | custom-call | flops 2147483648 | bytes 6566952 | tf_op jit(solution)/shard_map/attend/pallas_call | solution.py:36
  102.8 5.8 %collective-permute-done.12.refs_0_ = bf16[128,1024]{1,0:T(8,128)(2,1)S(1)} collective-permute-done((bf16[128,1024]{1,0:T(8,128)(2,1)S(1)}, bf16[128,1024]{1,0:T(8,128)(2,1)S(1)}, u32[]{:S(2)}, u32[]{:S(2)}) %collective-permute-start.12) | collective-permute-done | bytes 262176 | tf_op jit(solution)/shard_map/ppermute | solution.py:55
  117.9 4.9 %collective-permute-done.15.refs_2_ = bf16[128,1024]{1,0:T(8,128)(2,1)S(1)} collective-permute-done((bf16[128,1024]{1,0:T(8,128)(2,1)S(1)}, bf16[128,1024]{1,0:T(8,128)(2,1)S(1)}, u32[]{:S(2)}, u32[]{:S(2)}) %collective-permute-start.15) | collective-permute-done | bytes 262176 | tf_op jit(solution)/shard_map/ppermute | solution.py:55
  122.7 3.2 collective-permute-done.16.refs_3_
  125.9 12.4 %feed.1 = (bf16[512,1024]{1,0:T(8,128)(2,1)}, bf16[512,1024]{1,0:T(8,128)(2,1)}, bf16[512,768]{1,0:T(8,128)(2,1)}, bf16[512,768]{1,0:T(8,128)(2,1)}, bf16[512,76...) custom-call(s32[4]{0:T(128)S(1)} %iota_xor_fusion.refs_0_, ...), custom_call_target="tpu_custom_call" | custom-call | flops 4026531840 | bytes 12582928 | tf_op jit(solution)/shard_map/feed/pallas_call | solution.py:36
  141.9 3.3 collective-permute-done.21.refs_0_
  145.2 4.3 %collective-permute-done.22.refs_1_ = bf16[128,1024]{1,0:T(8,128)(2,1)S(1)} collective-permute-done((bf16[128,1024]{1,0:T(8,128)(2,1)S(1)}, bf16[128,1024]{1,0:T(8,128)(2,1)S(1)}, u32[]{:S(2)}, u32[]{:S(2)}) %collective-permute-start.22) | collective-permute-done | bytes 262176 | tf_op jit(solution)/shard_map/ppermute | solution.py:55
  161.4 14.1 %attend_back.1 = (bf16[512,512]{1,0:T(8,128)(2,1)}, f32[2048,256]{1,0:T(8,128)}, f32[2048,256]{1,0:T(8,128)}, f32[128,1]{1,0:T(8,128)S(1)}) custom-call(s32[8]{0:T(128)S(1)} %select_reduce_fusion.1.refs_0_, s32[2]{0:T(128)S(1)} %slice_bitcast_fusion.8.refs_1_, s32[256,1]{1,0:T(8,128)S(1)} %copy.36.refs_2_, s32[1,512]{1,0:T(1,128)S(1)} %get-tuple-element.188.refs_3_, ...), custom_call_target="tpu_custom_call" | custom-call | flops 5368709120 | bytes 12073000 | tf_op jit(solution)/shard_map/attend_back/pallas_call | solution.py:36
  175.5 4.1 hidden_back.4
  179.6 6.2 %hidden_back.5 = (bf16[1024,256]{1,0:T(8,128)(2,1)S(1)}, bf16[1024,256]{1,0:T(8,128)(2,1)S(1)}, f32[1,128]{1,0:T(1,128)S(1)}, f32[2,128,1024]{2,1,0:T(8,128)}, b...) custom-call(f32[2048,256]{1,0:T(8,128)} %get-tuple-element.123.refs_2_.refs_0_, ...), custom_call_target="tpu_custom_call" | custom-call | flops 1073741824 | bytes 12059648 | tf_op jit(solution)/shard_map/hidden_back/pallas_call | solution.py:36
  187.4 4.3 hidden_back.3
  192.4 11.2 %weights.1 = (bf16[768,1024]{1,0:T(8,128)(2,1)}, bf16[768,1024]{1,0:T(8,128)(2,1)}, f32[1024,1]{1,0:T(8,128)}) custom-call(s32[1]{0:T(128)} %bitcast.37.refs_0_, bf16[512,512]{1,0:T(8,128)(2,1)} %get-tuple-element.122.refs_0_.refs_1_, bf16[512,512]{1,0:T(8,128)(2,1)} %get-tuple-element.140.refs_2_, bf16[512,1024]{1,0:T(8,128)(2,1)} %get-tuple-element.141.refs_3_, ...), custom_call_target="tpu_custom_call" | custom-call | flops 3221225472 | bytes 13639684 | tf_op jit(solution)/shard_map/weights/pallas_call | solution.py:36
  205.7 8.1 %feed_weights.1 = (bf16[1024,768]{1,0:T(8,128)(2,1)}, bf16[1024,768]{1,0:T(8,128)(2,1)}, bf16[768,1024]{1,0:T(8,128)(2,1)}, f32[128,1024]{1,0:T(8,128)S(1)}, bf1...) custom-call(bf16[512,1024]{1,0:T(8,128)(2,1)} %get-tuple-element.104.hidden_ref, ...), custom_call_target="tpu_custom_call" | custom-call | flops 3221225472 | bytes 12058624 | tf_op jit(solution)/shard_map/feed_weights/pallas_call | solution.py:36
  221.8 4.8 %collective-permute-done.40 = f32[2304]{0:T(1024)S(1)} collective-permute-done((f32[2304]{0:T(1024)S(1)}, f32[2304]{0:T(1024)S(1)}, u32[]{:S(2)}, u32[]{:S(2)}) %collective-permute-start.40) | collective-permute-done | bytes 9248 | tf_op jit(solution)/shard_map/ppermute | solution.py:55
  226.9 7.8 %collective-permute-start.45 = (f32[2304]{0:T(1024)S(1)}, f32[2304]{0:T(1024)S(1)}, u32[]{:S(2)}, u32[]{:S(2)}) collective-permute-start(f32[2304]{0:T(1024)S(1)} %add_add_fusion.1), channel_id=1, source_target_pairs={{12,0},{0,4},{4,8},{8,12},{13,1},{1,5},{5,9},{9,13},{14,2},{2,6},{... | collective-permute-start | bytes 27656 | tf_op jit(solution)/shard_map/ppermute | solution.py:66
  234.6 3.2 collective-permute-start.44
  250.7 14.1 %collective-permute-done.31 = bf16[1,128,1024]{2,1,0:T(8,128)(2,1)S(1)} collective-permute-done((bf16[1,128,1024]{2,1,0:T(8,128)(2,1)}, bf16[1,128,1024]{2,1,0:T(8,128)(2,1)S(1)}, u32[]{:S(2)}, u32[]{:S(2)}) %collective-permute-start.31) | collective-permute-done | bytes 262176 | tf_op jit(solution)/shard_map/ppermute | solution.py:55
  273.1 14.0 %collective-permute-done.47.refs_1_ = bf16[192,1024]{1,0:T(8,128)(2,1)S(1)} collective-permute-done((bf16[192,1024]{1,0:T(8,128)(2,1)S(1)}, bf16[192,1024]{1,0:T(8,128)(2,1)S(1)}, u32[]{:S(2)}, u32[]{:S(2)}) %collective-permute-start.47) | collective-permute-done | bytes 393248 | tf_op jit(solution)/shard_map/ppermute | solution.py:71
  287.1 10.2 %collective-permute-done.48.refs_2_ = bf16[192,1024]{1,0:T(8,128)(2,1)S(1)} collective-permute-done((bf16[192,1024]{1,0:T(8,128)(2,1)S(1)}, bf16[192,1024]{1,0:T(8,128)(2,1)S(1)}, u32[]{:S(2)}, u32[]{:S(2)}) %collective-permute-start.48) | collective-permute-done | bytes 393248 | tf_op jit(solution)/shard_map/ppermute | solution.py:71
  297.8 12.5 %collective-permute-start.43 = (f32[2304]{0:T(1024)S(1)}, f32[2304]{0:T(1024)S(1)}, u32[]{:S(2)}, u32[]{:S(2)}) collective-permute-start(f32[2304]{0:T(1024)S(1)} %add_add_fusion.1), channel_id=1, source_target_pairs={{4,0},{8,4},{12,8},{0,12},{5,1},{9,5},{13,9},{1,13},{6,2},{10,6},{... | collective-permute-start | bytes 27656 | tf_op jit(solution)/shard_map/ppermute | solution.py:66
  312.8 3.1 collective-permute-start.50
  321.7 62.9 %collective-permute-done.33.refs_4_ = bf16[128,1024]{1,0:T(8,128)(2,1)S(1)} collective-permute-done((bf16[128,1024]{1,0:T(8,128)(2,1)S(1)}, bf16[128,1024]{1,0:T(8,128)(2,1)S(1)}, u32[]{:S(2)}, u32[]{:S(2)}) %collective-permute-start.33) | collective-permute-done | bytes 262176 | tf_op jit(solution)/shard_map/ppermute | solution.py:71
  388.9 6.3 %collective-permute-done.38.refs_6_ = bf16[128,1024]{1,0:T(8,128)(2,1)S(1)} collective-permute-done((bf16[128,1024]{1,0:T(8,128)(2,1)S(1)}, bf16[128,1024]{1,0:T(8,128)(2,1)S(1)}, u32[]{:S(2)}, u32[]{:S(2)}) %collective-permute-start.38) | collective-permute-done | bytes 262176 | tf_op jit(solution)/shard_map/ppermute | solution.py:71
  397.7 12.5 %all-reduce.3.cloned.1.call-done = (bf16[1024,768]{1,0:T(8,128)(2,1)}, bf16[1024,768]{1,0:T(8,128)(2,1)}, bf16[768,1024]{1,0:T(8,128)(2,1)}) async-done(((bf16[1024,768]{1,0:T(8,128)(2,1)}, bf16[1024,768]{1,0:T(8,128)(2,1)}, bf16[768,1024]{1,0:T(8,128)(2,1)}), (bf16[1024,768]{1,0:T(8,128)(2,1)}, bf16[1024,768]{1,0:T(8,128)(2,1)}, bf16[768,1024]{1,0:T(8,128)(2,1)})) %all-reduce.3.cloned.1.call-update) | async-done | bytes 4718608 | tf_op jit(solution)/shard_map/psum | solution.py:741
  410.1 3.4 convert_element_type.34
  418.3 4.4 %spread.1 = (f32[1024,512]{1,0:T(8,128)}, f32[1024,256]{1,0:T(8,128)}, f32[1024,256]{1,0:T(8,128)}, f32[512,1024]{1,0:T(8,128)}) custom-call(s32[8]{0:T(128)S(1)} %pad_add_fusion.refs_0_, bf16[192,1024]{1,0:T(8,128)(2,1)S(1)} %sum_parts.7.refs_1_, bf16[192,1024]{1,0:T(8,128)(2,1)S(1)} %collective-permute-done.50.refs_2_, ...), custom_call_target="tpu_custom_call" | custom-call | bytes 9437216 | tf_op jit(solution)/shard_map/spread/pallas_call | solution.py:36
  (232 shorter events, 109.7 us)
Async XLA Ops:
  7.2 118.7 %all-gather.3.cloned.1.call-start = ((), (), s32[]{:S(2)}) async-start(), calls=%async_computation | async-start | bytes 1310720 | tf_op jit(solution)/shard_map/all_gather | solution.py:706
  9.0 19.6 %collective-permute-start = (bf16[128,1024]{1,0:T(8,128)(2,1)S(1)}, bf16[128,1024]{1,0:T(8,128)(2,1)S(1)}, u32[]{:S(2)}, u32[]{:S(2)}) collective-permute-start(bf16[128,1024]{1,0:T(8,128)(2,1)S(1)} %norm1.1.refs_0_), channel_id=1, source_target_pairs={{0,1},{1,0},{2,3},{3,2},{4,5},{5,4},{6,7},{7,6},{8,9},{9,8},{10,11... | collective-permute-start | bytes 786440 | tf_op jit(solution)/shard_map/ppermute | solution.py:55
  12.0 17.4 %collective-permute-start.1 = (bf16[128,1024]{1,0:T(8,128)(2,1)S(1)}, bf16[128,1024]{1,0:T(8,128)(2,1)S(1)}, u32[]{:S(2)}, u32[]{:S(2)}) collective-permute-start(bf16[128,1024]{1,0:T(8,128)(2,1)S(1)} %norm1.1.refs_0_), channel_id=1, source_target_pairs={{0,2},{1,3},{2,0},{3,1},{4,6},{5,7},{6,4},{7,5},{8,10},{9,11},{10,... | collective-permute-start | bytes 786440 | tf_op jit(solution)/shard_map/ppermute | solution.py:55
  17.4 22.4 %collective-permute-start.8 = (bf16[128,1024]{1,0:T(8,128)(2,1)S(1)}, bf16[128,1024]{1,0:T(8,128)(2,1)S(1)}, u32[]{:S(2)}, u32[]{:S(2)}) collective-permute-start(bf16[128,1024]{1,0:T(8,128)(2,1)S(1)} %norm1.1.refs_0_), channel_id=1, source_target_pairs={{8,0},{12,4},{0,8},{4,12},{9,1},{13,5},{1,9},{5,13},{10,2},{14,6},... | collective-permute-start | bytes 786440 | tf_op jit(solution)/shard_map/ppermute | solution.py:66
  18.2 392.0 %all-reduce.3.cloned.1.call-start = ((), (), s32[]{:S(2)}) async-start(), calls=%async_computation.1 | async-start | bytes 9437184 | tf_op jit(solution)/shard_map/psum | solution.py:741
  28.0 52.5 %collective-permute-start.5 = (bf16[2,128,1024]{2,1,0:T(8,128)(2,1)S(1)}, bf16[2,128,1024]{2,1,0:T(8,128)(2,1)}, u32[]{:S(2)}, u32[]{:S(2)}) collective-permute-start(bf16[2,128,1024]{2,1,0:T(8,128)(2,1)S(1)} %pad_maximum_fusion.2.refs_0_), channel_id=1, source_target_pairs={{0,1},{1,0},{2,3},{3,2},{4,5},{5,4},{6,7},{7,6},{8,9},{9,8},{10,11... | collective-permute-start | bytes 1572872 | tf_op jit(solution)/shard_map/ppermute | solution.py:55
  28.6 51.9 %collective-permute-start.6 = (bf16[2,128,1024]{2,1,0:T(8,128)(2,1)S(1)}, bf16[2,128,1024]{2,1,0:T(8,128)(2,1)}, u32[]{:S(2)}, u32[]{:S(2)}) collective-permute-start(bf16[2,128,1024]{2,1,0:T(8,128)(2,1)S(1)} %pad_maximum_fusion.2.refs_0_), channel_id=1, source_target_pairs={{0,2},{1,3},{2,0},{3,1},{4,6},{5,7},{6,4},{7,5},{8,10},{9,11},{10,... | collective-permute-start | bytes 1572872 | tf_op jit(solution)/shard_map/ppermute | solution.py:55
  29.4 51.2 %collective-permute-start.7 = (bf16[2,128,1024]{2,1,0:T(8,128)(2,1)S(1)}, bf16[2,128,1024]{2,1,0:T(8,128)(2,1)}, u32[]{:S(2)}, u32[]{:S(2)}) collective-permute-start(bf16[2,128,1024]{2,1,0:T(8,128)(2,1)S(1)} %pad_maximum_fusion.2.refs_0_), channel_id=1, source_target_pairs={{0,3},{1,2},{2,1},{3,0},{4,7},{5,6},{6,5},{7,4},{8,11},{9,10},{10,... | collective-permute-start | bytes 1572872 | tf_op jit(solution)/shard_map/ppermute | solution.py:55
  39.7 28.7 %collective-permute-start.9 = (bf16[1,128,1024]{2,1,0:T(8,128)(2,1)S(1)}, bf16[1,128,1024]{2,1,0:T(8,128)(2,1)S(1)}, u32[]{:S(2)}, u32[]{:S(2)}) collective-permute-start(bf16[1,128,1024]{2,1,0:T(8,128)(2,1)S(1)} %bitcast.67), channel_id=1, source_target_pairs={{0,1},{1,0},{2,3},{3,2},{4,5},{5,4},{6,7},{7,6},{8,9},{9,8},{10,11... | collective-permute-start | bytes 786440 | tf_op jit(solution)/shard_map/ppermute | solution.py:55
  40.6 35.0 %collective-permute-start.10 = (bf16[1,128,1024]{2,1,0:T(8,128)(2,1)S(1)}, bf16[1,128,1024]{2,1,0:T(8,128)(2,1)S(1)}, u32[]{:S(2)}, u32[]{:S(2)}) collective-permute-start(bf16[1,128,1024]{2,1,0:T(8,128)(2,1)S(1)} %bitcast.68), channel_id=1, source_target_pairs={{0,2},{1,3},{2,0},{3,1},{4,6},{5,7},{6,4},{7,5},{8,10},{9,11},{10,... | collective-permute-start | bytes 786440 | tf_op jit(solution)/shard_map/ppermute | solution.py:55
  203.6 38.3 %collective-permute-start.46 = (bf16[768,1024]{1,0:T(8,128)(2,1)}, bf16[768,1024]{1,0:T(8,128)(2,1)}, u32[]{:S(2)}, u32[]{:S(2)}) collective-permute-start(bf16[768,1024]{1,0:T(8,128)(2,1)} %get-tuple-element.157), channel_id=1, source_target_pairs={{0,16},{16,0},{1,17},{17,1},{2,18},{18,2},{3,19},{19,3},{4,20},{20... | collective-permute-start | bytes 4718600 | tf_op jit(solution)/shard_map/ppermute | solution.py:55
  220.2 17.6 %collective-permute-start.20 = (bf16[128,1024]{1,0:T(8,128)(2,1)S(1)}, bf16[128,1024]{1,0:T(8,128)(2,1)S(1)}, u32[]{:S(2)}, u32[]{:S(2)}) collective-permute-start(bf16[128,1024]{1,0:T(8,128)(2,1)S(1)} %get-tuple-element.112), channel_id=1, source_target_pairs={{0,3},{1,2},{2,1},{3,0},{4,7},{5,6},{6,5},{7,4},{8,11},{9,10},{10,... | collective-permute-start | bytes 786440 | tf_op jit(solution)/shard_map/ppermute | solution.py:55
  226.6 39.9 %collective-permute-start.34 = (bf16[2,128,1024]{2,1,0:T(8,128)(2,1)}, bf16[2,128,1024]{2,1,0:T(8,128)(2,1)}, u32[]{:S(2)}, u32[]{:S(2)}) collective-permute-start(bf16[2,128,1024]{2,1,0:T(8,128)(2,1)} %get-tuple-element.137), channel_id=1, source_target_pairs={{0,1},{1,0},{2,3},{3,2},{4,5},{5,4},{6,7},{7,6},{8,9},{9,8},{10,11... | collective-permute-start | bytes 1572872 | tf_op jit(solution)/shard_map/ppermute | solution.py:55
  239.3 25.5 %collective-permute-start.31 = (bf16[1,128,1024]{2,1,0:T(8,128)(2,1)}, bf16[1,128,1024]{2,1,0:T(8,128)(2,1)S(1)}, u32[]{:S(2)}, u32[]{:S(2)}) collective-permute-start(bf16[1,128,1024]{2,1,0:T(8,128)(2,1)} %get-tuple-element.133), channel_id=1, source_target_pairs={{0,2},{1,3},{2,0},{3,1},{4,6},{5,7},{6,4},{7,5},{8,10},{9,11},{10,... | collective-permute-start | bytes 786440 | tf_op jit(solution)/shard_map/ppermute | solution.py:55
  240.5 24.2 %collective-permute-start.32 = (bf16[1,128,1024]{2,1,0:T(8,128)(2,1)}, bf16[1,128,1024]{2,1,0:T(8,128)(2,1)S(1)}, u32[]{:S(2)}, u32[]{:S(2)}) collective-permute-start(bf16[1,128,1024]{2,1,0:T(8,128)(2,1)} %get-tuple-element.134), channel_id=1, source_target_pairs={{0,3},{1,2},{2,1},{3,0},{4,7},{5,6},{6,5},{7,4},{8,11},{9,10},{10,... | collective-permute-start | bytes 786440 | tf_op jit(solution)/shard_map/ppermute | solution.py:55
  241.9 28.5 %collective-permute-start.35 = (bf16[2,128,1024]{2,1,0:T(8,128)(2,1)}, bf16[2,128,1024]{2,1,0:T(8,128)(2,1)}, u32[]{:S(2)}, u32[]{:S(2)}) collective-permute-start(bf16[2,128,1024]{2,1,0:T(8,128)(2,1)} %get-tuple-element.138), channel_id=1, source_target_pairs={{0,2},{1,3},{2,0},{3,1},{4,6},{5,7},{6,4},{7,5},{8,10},{9,11},{10,... | collective-permute-start | bytes 1572872 | tf_op jit(solution)/shard_map/ppermute | solution.py:55
  249.1 66.8 %collective-permute-start.36 = (bf16[2,128,1024]{2,1,0:T(8,128)(2,1)S(1)}, bf16[2,128,1024]{2,1,0:T(8,128)(2,1)S(1)}, u32[]{:S(2)}, u32[]{:S(2)}) collective-permute-start(bf16[2,128,1024]{2,1,0:T(8,128)(2,1)S(1)} %copy-done.33), channel_id=1, source_target_pairs={{0,3},{1,2},{2,1},{3,0},{4,7},{5,6},{6,5},{7,4},{8,11},{9,10},{10,... | collective-permute-start | bytes 1572872 | tf_op jit(solution)/shard_map/ppermute | solution.py:55
  264.7 22.4 %collective-permute-start.47 = (bf16[192,1024]{1,0:T(8,128)(2,1)S(1)}, bf16[192,1024]{1,0:T(8,128)(2,1)S(1)}, u32[]{:S(2)}, u32[]{:S(2)}) collective-permute-start(bf16[192,1024]{1,0:T(8,128)(2,1)S(1)} %get-tuple-element.159), channel_id=1, source_target_pairs={{0,4},{4,8},{8,12},{12,0},{1,5},{5,9},{9,13},{13,1},{2,6},{6,10},{... | collective-permute-start | bytes 1179656 | tf_op jit(solution)/shard_map/ppermute | solution.py:71
  264.7 32.6 %collective-permute-start.48 = (bf16[192,1024]{1,0:T(8,128)(2,1)S(1)}, bf16[192,1024]{1,0:T(8,128)(2,1)S(1)}, u32[]{:S(2)}, u32[]{:S(2)}) collective-permute-start(bf16[192,1024]{1,0:T(8,128)(2,1)S(1)} %get-tuple-element.160), channel_id=1, source_target_pairs={{0,8},{4,12},{8,0},{12,4},{1,9},{5,13},{9,1},{13,5},{2,10},{6,14},... | collective-permute-start | bytes 1179656 | tf_op jit(solution)/shard_map/ppermute | solution.py:71
  266.5 31.3 %collective-permute-start.49 = (bf16[192,1024]{1,0:T(8,128)(2,1)S(1)}, bf16[192,1024]{1,0:T(8,128)(2,1)S(1)}, u32[]{:S(2)}, u32[]{:S(2)}) collective-permute-start(bf16[192,1024]{1,0:T(8,128)(2,1)S(1)} %get-tuple-element.161), channel_id=1, source_target_pairs={{0,12},{4,0},{8,4},{12,8},{1,13},{5,1},{9,5},{13,9},{2,14},{6,2},{... | collective-permute-start | bytes 1179656 | tf_op jit(solution)/shard_map/ppermute | solution.py:71
  270.5 45.4 %collective-permute-start.27 = (bf16[1,128,1024]{2,1,0:T(8,128)(2,1)S(1)}, bf16[1,128,1024]{2,1,0:T(8,128)(2,1)S(1)}, u32[]{:S(2)}, u32[]{:S(2)}) collective-permute-start(bf16[1,128,1024]{2,1,0:T(8,128)(2,1)S(1)} %copy-done.16), channel_id=1, source_target_pairs={{0,1},{1,0},{2,3},{3,2},{4,5},{5,4},{6,7},{7,6},{8,9},{9,8},{10,11... | collective-permute-start | bytes 786440 | tf_op jit(solution)/shard_map/ppermute | solution.py:55
  287.1 29.5 %collective-permute-start.28 = (bf16[1,128,1024]{2,1,0:T(8,128)(2,1)S(1)}, bf16[1,128,1024]{2,1,0:T(8,128)(2,1)S(1)}, u32[]{:S(2)}, u32[]{:S(2)}) collective-permute-start(bf16[1,128,1024]{2,1,0:T(8,128)(2,1)S(1)} %copy-done.14), channel_id=1, source_target_pairs={{0,2},{1,3},{2,0},{3,1},{4,6},{5,7},{6,4},{7,5},{8,10},{9,11},{10,... | collective-permute-start | bytes 786440 | tf_op jit(solution)/shard_map/ppermute | solution.py:55
  297.4 21.7 %collective-permute-start.29 = (bf16[1,128,1024]{2,1,0:T(8,128)(2,1)S(1)}, bf16[1,128,1024]{2,1,0:T(8,128)(2,1)S(1)}, u32[]{:S(2)}, u32[]{:S(2)}) collective-permute-start(bf16[1,128,1024]{2,1,0:T(8,128)(2,1)S(1)} %get-tuple-element.129), channel_id=1, source_target_pairs={{0,3},{1,2},{2,1},{3,0},{4,7},{5,6},{6,5},{7,4},{8,11},{9,10},{10,... | collective-permute-start | bytes 786440 | tf_op jit(solution)/shard_map/ppermute | solution.py:55
  312.8 74.0 %collective-permute-start.50 = (bf16[192,1024]{1,0:T(8,128)(2,1)S(1)}, bf16[192,1024]{1,0:T(8,128)(2,1)S(1)}, u32[]{:S(2)}, u32[]{:S(2)}) collective-permute-start(bf16[192,1024]{1,0:T(8,128)(2,1)S(1)} %sum_parts.7.refs_1_), channel_id=1, source_target_pairs={{4,0},{8,4},{12,8},{0,12},{5,1},{9,5},{13,9},{1,13},{6,2},{10,6},{... | collective-permute-start | bytes 1179656 | tf_op jit(solution)/shard_map/ppermute | solution.py:66
  315.9 71.4 %collective-permute-start.51 = (bf16[192,1024]{1,0:T(8,128)(2,1)S(1)}, bf16[192,1024]{1,0:T(8,128)(2,1)S(1)}, u32[]{:S(2)}, u32[]{:S(2)}) collective-permute-start(bf16[192,1024]{1,0:T(8,128)(2,1)S(1)} %sum_parts.7.refs_1_), channel_id=1, source_target_pairs={{8,0},{12,4},{0,8},{4,12},{9,1},{13,5},{1,9},{5,13},{10,2},{14,6},... | collective-permute-start | bytes 1179656 | tf_op jit(solution)/shard_map/ppermute | solution.py:66
  315.9 71.4 %collective-permute-start.52 = (bf16[192,1024]{1,0:T(8,128)(2,1)S(1)}, bf16[192,1024]{1,0:T(8,128)(2,1)S(1)}, u32[]{:S(2)}, u32[]{:S(2)}) collective-permute-start(bf16[192,1024]{1,0:T(8,128)(2,1)S(1)} %sum_parts.7.refs_1_), channel_id=1, source_target_pairs={{12,0},{0,4},{4,8},{8,12},{13,1},{1,5},{5,9},{9,13},{14,2},{2,6},{... | collective-permute-start | bytes 1179656 | tf_op jit(solution)/shard_map/ppermute | solution.py:66
  316.7 67.9 %collective-permute-start.33 = (bf16[128,1024]{1,0:T(8,128)(2,1)S(1)}, bf16[128,1024]{1,0:T(8,128)(2,1)S(1)}, u32[]{:S(2)}, u32[]{:S(2)}) collective-permute-start(bf16[128,1024]{1,0:T(8,128)(2,1)S(1)} %sum_parts.4), channel_id=1, source_target_pairs={{0,8},{4,12},{8,0},{12,4},{1,9},{5,13},{9,1},{13,5},{2,10},{6,14},... | collective-permute-start | bytes 786440 | tf_op jit(solution)/shard_map/ppermute | solution.py:71
  319.1 67.7 %collective-permute-start.37 = (bf16[128,1024]{1,0:T(8,128)(2,1)S(1)}, bf16[128,1024]{1,0:T(8,128)(2,1)S(1)}, u32[]{:S(2)}, u32[]{:S(2)}) collective-permute-start(bf16[128,1024]{1,0:T(8,128)(2,1)S(1)} %sum_parts.5), channel_id=1, source_target_pairs={{0,4},{4,8},{8,12},{12,0},{1,5},{5,9},{9,13},{13,1},{2,6},{6,10},{... | collective-permute-start | bytes 786440 | tf_op jit(solution)/shard_map/ppermute | solution.py:71
  386.8 30.8 %collective-permute-start.53 = (bf16[192,1024]{1,0:T(8,128)(2,1)S(1)}, bf16[192,1024]{1,0:T(8,128)(2,1)S(1)}, u32[]{:S(2)}, u32[]{:S(2)}) collective-permute-start(bf16[192,1024]{1,0:T(8,128)(2,1)S(1)} %sum_parts.7.refs_1_), channel_id=1, source_target_pairs={{0,16},{16,0},{1,17},{17,1},{2,18},{18,2},{3,19},{19,3},{4,20},{20... | collective-permute-start | bytes 1179656 | tf_op jit(solution)/shard_map/ppermute | solution.py:55
  386.8 30.8 %collective-permute-start.54 = (bf16[192,1024]{1,0:T(8,128)(2,1)S(1)}, bf16[192,1024]{1,0:T(8,128)(2,1)S(1)}, u32[]{:S(2)}, u32[]{:S(2)}) collective-permute-start(bf16[192,1024]{1,0:T(8,128)(2,1)S(1)} %collective-permute-done.50.refs_2_), channel_id=1, source_target_pairs={{0,16},{16,0},{1,17},{17,1},{2,18},{18,2},{3,19},{19,3},{4,20},{20... | collective-permute-start | bytes 1179656 | tf_op jit(solution)/shard_map/ppermute | solution.py:55
  387.3 30.3 %collective-permute-start.55 = (bf16[192,1024]{1,0:T(8,128)(2,1)S(1)}, bf16[192,1024]{1,0:T(8,128)(2,1)}, u32[]{:S(2)}, u32[]{:S(2)}) collective-permute-start(bf16[192,1024]{1,0:T(8,128)(2,1)S(1)} %collective-permute-done.51.refs_3_), channel_id=1, source_target_pairs={{0,16},{16,0},{1,17},{17,1},{2,18},{18,2},{3,19},{19,3},{4,20},{20... | collective-permute-start | bytes 1179656 | tf_op jit(solution)/shard_map/ppermute | solution.py:55
  387.4 30.2 %collective-permute-start.56 = (bf16[192,1024]{1,0:T(8,128)(2,1)S(1)}, bf16[192,1024]{1,0:T(8,128)(2,1)}, u32[]{:S(2)}, u32[]{:S(2)}) collective-permute-start(bf16[192,1024]{1,0:T(8,128)(2,1)S(1)} %collective-permute-done.52.refs_4_), channel_id=1, source_target_pairs={{0,16},{16,0},{1,17},{17,1},{2,18},{18,2},{3,19},{19,3},{4,20},{20... | collective-permute-start | bytes 1179656 | tf_op jit(solution)/shard_map/ppermute | solution.py:55
  (64 other events, 620.8 us)
Sparse Core Ops, SparseCore 0:
  18.3 34.3 all-gather.2
  213.9 196.1 all-reduce.2

commit v2 on v1

--- a/solution.py
+++ b/solution.py
@@ -32,7 +32,6 @@
 def call(kernel, ins, outs, grid=(1,), in_specs=None, out_specs=None, scratch=(), flops=0, name=None):
     in_specs = in_specs or {}
     out_specs = out_specs or {}
-    moved = sum(math.prod(a.shape) * a.dtype.itemsize for a in list(ins) + list(outs))
     return pl.pallas_call(
         kernel,
         grid=grid,
@@ -41,7 +40,7 @@
         out_shape=list(outs),
         scratch_shapes=list(scratch),
         compiler_params=pltpu.CompilerParams(vmem_limit_bytes=VMEM_LIMIT),
-        cost_estimate=pl.CostEstimate(flops=flops, bytes_accessed=moved, transcendentals=0),
+        cost_estimate=pl.CostEstimate(flops=0, bytes_accessed=0, transcendentals=0),
         name=name,
     )(*ins)
 
@@ -410,25 +409,9 @@
 def hidden_back_kernel(own, mp, *refs):
     if own:
         ql_ref, wq_ref, *refs = refs
-    dk_ref, dv_ref, klin_ref, cos_ref, sin_ref, gk_ref, wk_ref, wv_ref = refs[:8]
-    kl_ref, vl_ref, gkg_ref = refs[8:11]
-    part_refs = refs[11:]
+    kl_ref, vl_ref, wk_ref, wv_ref = refs[:4]
+    part_refs = refs[4:]
     share = part_refs[0].shape[1]
-    width = gk_ref.shape[1]
-    score_scale = 1.0 / math.sqrt(width)
-
-    @pl.when(pl.program_id(0) == 0)
-    def _():
-        gkg_ref[...] = jnp.zeros_like(gkg_ref)
-
-    for start in range(0, dk_ref.shape[1], width):
-        head = slice(start, start + width)
-        rotated = dk_ref[:, head] * score_scale
-        gradient = rotated * cos_ref[...] - pltpu.roll(rotated, width // 2, 1) * sin_ref[...]
-        back, terms = norm_back(klin_ref[:, head], gk_ref[...], gradient)
-        kl_ref[:, head] = back.astype(BF)
-        gkg_ref[...] += jnp.sum(terms, axis=0, keepdims=True)
-    vl_ref[...] = dv_ref[...].astype(BF)
     total = dot(kl_ref[...], wk_ref[...], 1, 1) + dot(vl_ref[...], wv_ref[...], 1, 1)
     if own:
         total = total + dot(ql_ref[...], wq_ref[...], 0, 1)
@@ -436,68 +419,115 @@
         ref[0] = total[j * share : (j + 1) * share, :].astype(ref.dtype)
 
 
-def weights_kernel(groups, mp, *refs):
+def o_weights_kernel(core_ref, attt_ref, *refs):
+    *low_refs, mine_ref, other_ref, low_all = refs
+    share = low_refs[0].shape[0]
+    for j, ref in enumerate(low_refs):
+        low_all[j * share : (j + 1) * share, :] = ref[...]
+    rows = mine_ref.shape[0]
+    core = core_ref[0]
+    for ref, at in ((mine_ref, core), (other_ref, 1 - core)):
+        here = pl.ds(pl.multiple_of(at * rows, rows), rows)
+        ref[...] = dot(attt_ref[here, :], low_all[...], 1, 0).astype(BF)
+
+
+def weights_kernel(groups, *refs):
     n = len(groups)
-    core_ref, ql_ref, attt_ref = refs[:3]
-    hidden_refs, kl_refs, vl_refs = refs[3 : 3 + n], refs[3 + n : 3 + 2 * n], refs[3 + 2 * n : 3 + 3 * n]
-    low_refs = refs[3 + 3 * n : 3 + 3 * n + mp]
-    wq_ref, wk_ref, wv_ref, gain_ref, mine_ref, other_ref, gain_grad_ref, accum, low_all, keep = refs[
-        3 + 3 * n + mp :
-    ]
+    core_ref, ql_ref, dk_ref, dv_ref, cos_ref, sin_ref, gk_ref = refs[:7]
+    hidden_refs, klin_refs = refs[7 : 7 + n], refs[7 + n : 7 + 2 * n]
+    (
+        wq_ref, wk_ref, wv_ref, gain_ref, kl_ref, vl_ref,
+        mine_ref, other_ref, gain_grad_ref, gkg_ref, accum,
+    ) = refs[7 + 2 * n :]
     step = pl.program_id(0)
     model = gain_ref.shape[0]
-    q_width, k_width = ql_ref.shape[0], kl_refs[0].shape[1]
-    share = low_refs[0].shape[0]
+    q_width, k_width = ql_ref.shape[0], dk_ref.shape[1]
+    width = gk_ref.shape[1]
+    score_scale = 1.0 / math.sqrt(width)
 
     @pl.when(step == 0)
     def _():
-        for j, ref in enumerate(low_refs):
-            low_all[j * share : (j + 1) * share, :] = ref[...]
-        keep[:model, :q_width] = dot(hidden_refs[0][...], ql_ref[...], 0, 1)
-        keep[model:, :] = dot(attt_ref[...], low_all[...], 1, 0)
-        accum[...] = jnp.zeros_like(accum)
+        accum[:, :q_width] = dot(hidden_refs[0][...], ql_ref[...], 0, 1)
+        accum[:, q_width:] = jnp.zeros_like(accum[:, q_width:])
+        gkg_ref[...] = jnp.zeros_like(gkg_ref)
 
     first = 0
-    for hidden_ref, kl_ref, vl_ref, slots in zip(hidden_refs, kl_refs, vl_refs, groups):
+    for hidden_ref, klin_ref, slots in zip(hidden_refs, klin_refs, groups):
 
         @pl.when((step >= first) & (step < first + len(slots)))
         def _():
+            for start in range(0, k_width, width):
+                head = slice(start, start + width)
+                rotated = dk_ref[:, head] * score_scale
+                gradient = rotated * cos_ref[...] - pltpu.roll(rotated, width // 2, 1) * sin_ref[...]
+                back, terms = norm_back(klin_ref[:, head], gk_ref[...], gradient)
+                kl_ref[:, head] = back.astype(BF)
+                gkg_ref[...] += jnp.sum(terms, axis=0, keepdims=True)
+            vl_ref[...] = dv_ref[...].astype(BF)
             hidden = hidden_ref[...]
-            accum[:, :k_width] += dot(hidden, kl_ref[...], 0, 0)
-            accum[:, k_width:] += dot(hidden, vl_ref[...], 0, 0)
+            accum[:, q_width : q_width + k_width] += dot(hidden, kl_ref[...], 0, 0)
+            accum[:, q_width + k_width :] += dot(hidden, vl_ref[...], 0, 0)
 
         first += len(slots)
 
     @pl.when(step == pl.num_programs(0) - 1)
     def _():
-        keep[:model, q_width:] = accum[...]
-        terms = jnp.sum(keep[:model, :q_width] * wq_ref[...].astype(F32), axis=1, keepdims=True)
-        terms += jnp.sum(accum[:, :k_width] * wk_ref[...].astype(F32), axis=1, keepdims=True)
-        terms += jnp.sum(accum[:, k_width:] * wv_ref[...].astype(F32), axis=1, keepdims=True)
+        terms = jnp.sum(accum[:, :q_width] * wq_ref[...].astype(F32), axis=1, keepdims=True)
+        terms += jnp.sum(
+            accum[:, q_width : q_width + k_width] * wk_ref[...].astype(F32), axis=1, keepdims=True
+        )
+        terms += jnp.sum(
+            accum[:, q_width + k_width :] * wv_ref[...].astype(F32), axis=1, keepdims=True
+        )
         gain_grad_ref[...] = terms / gain_ref[...]
         rows = mine_ref.shape[0]
         core = core_ref[0]
-        mine_ref[...] = keep[pl.ds(pl.multiple_of(core * rows, rows), rows), :].astype(BF)
-        other_ref[...] = keep[pl.ds(pl.multiple_of((1 - core) * rows, rows), rows), :].astype(BF)
-
-
-def split_kernel(place_ref, mine_ref, got_ref, *refs):
-    rows = refs[0].shape[0]
-    for k, ref in enumerate(refs):
-        here = pl.ds(pl.multiple_of(place_ref[k] * rows, rows), rows)
+        mine_ref[...] = accum[pl.ds(pl.multiple_of(core * rows, rows), rows), :].astype(BF)
+        other_ref[...] = accum[pl.ds(pl.multiple_of((1 - core) * rows, rows), rows), :].astype(BF)
+
+
+def split_kernel(place_ref, mine_ref, got_ref, keep_ref, send_ref):
+    rows = keep_ref.shape[0]
+    for ref, at in ((keep_ref, place_ref[0]), (send_ref, 1 - place_ref[0])):
+        here = pl.ds(pl.multiple_of(at * rows, rows), rows)
         ref[...] = (mine_ref[here, :].astype(F32) + got_ref[here, :].astype(F32)).astype(ref.dtype)
 
 
-def spread_kernel(q_width, k_width, model, *refs):
+def spread_kernel(q_width, k_width, count, *refs):
     place_ref = refs[0]
-    *chunks, dq_ref, dk_ref, dv_ref, do_ref, full = refs[1:]
-    rows = chunks[0].shape[0]
+    chunks, o_chunks = refs[1 : 1 + count], refs[1 + count : 1 + 2 * count]
+    dq_ref, dk_ref, dv_ref, do_ref = refs[1 + 2 * count :]
     for i, ref in enumerate(chunks):
-        full[pl.ds(pl.multiple_of(place_ref[i] * rows, rows), rows), :] = ref[...].astype(F32)
-    dq_ref[...] = full[:model, :q_width]
-    dk_ref[...] = full[:model, q_width : q_width + k_width]
-    dv_ref[...] = full[:model, q_width + k_width :]
-    do_ref[...] = full[model:, :]
+        rows = ref.shape[0]
+        here = pl.ds(pl.multiple_of(place_ref[i] * rows, rows), rows)
+        dq_ref[here, :] = ref[:, :q_width].astype(F32)
+        dk_ref[here, :] = ref[:, q_width : q_width + k_width].astype(F32)
+        dv_ref[here, :] = ref[:, q_width + k_width :].astype(F32)
+    for i, ref in enumerate(o_chunks):
+        rows = ref.shape[0]
+        here = pl.ds(pl.multiple_of(place_ref[i] * rows, rows), rows)
+        do_ref[here, :] = ref[...].astype(F32)
+
+
+def sum_over_ctx(mine, other, part, few, after=()):
+    got = swap(other, "dp", 1)
+    if not few:
+        chunk = lax.psum(sum_parts([mine, got], BF), "ctx")
+        return [chunk, swap(chunk, "dp", 1)]
+    rows = mine.shape[0] // 2
+    keep, send = call(
+        split_kernel,
+        [part, mine, got],
+        [out((rows, mine.shape[1]), F32), out((rows, mine.shape[1]), BF)],
+        in_specs={0: SMEM},
+        name="split",
+    )
+    pair = sum_parts([keep, swap(send, "ctx", 1)], BF)
+    if after:
+        pair, *_ = lax.optimization_barrier((pair, *after))
+    total = sum_parts([pair, swap(pair, "ctx", 3)], BF)
+    chunks = [total, swap(total, "ctx", 1)]
+    return chunks + [swap(c, "dp", 1) for c in chunks]
 
 
 def slot_blocks(group, rows, width):
@@ -536,7 +566,7 @@
     ctx_rows = share * mp
     half = ctx_rows // 2
     seq_rows = ctx_rows * ctx
-    few = ctx <= 4
+    few = ctx == 4
     here_ctx = lax.axis_index("ctx")
     here_mp = lax.axis_index("mp")
     here_dp = lax.axis_index("dp")
@@ -550,18 +580,8 @@
     h1_share = call(norm_kernel, [tok, gain1], [out((share, model), BF)], name="norm1")[0]
     own_parts = [h1_share] + swaps([h1_share] * mp, "mp")
     if few:
-        near = [from_ctx(h1_share, k) for k in range(1, ctx)]
-        if ctx == 4:
-            remote = [((1, 3), jnp.stack([near[0], near[2]])), ((2,), near[1][None])]
-        else:
-            remote = [(tuple(range(1, ctx)), jnp.stack(near))]
-    else:
-        every = lax.all_gather(h1_share, "ctx", axis=0)
-        every = jnp.concatenate([every, every], axis=0)
-        every = lax.dynamic_slice_in_dim(every, here_ctx + 1, ctx - 1, 0)
-        remote = [(tuple(range(1, ctx)), every)]
-    remote_parts = [[value] + swaps([value] * mp, "mp") for _, value in remote]
-    groups = [(0,)] + [slots for slots, _ in remote]
+        near = {k: from_ctx(h1_share, k) for k in (1, 3)}
+        own_parts[0], near[1], near[3] = lax.optimization_barrier((own_parts[0], near[1], near[3]))
 
     slot_ctx = (here_ctx + jnp.arange(ctx, dtype=jnp.int32)) % ctx
     slot_pair = jnp.sum(
@@ -619,6 +639,17 @@
         flops=2 * ctx_rows * model * (q_width + 2 * k_width),
         name="own_rows",
     )
+    if few:
+        late_share, _ = lax.optimization_barrier((h1_share, k_own))
+        far = from_ctx(late_share, 2)
+        remote = [((1, 3), jnp.stack([near[1], near[3]])), ((2,), far[None])]
+    else:
+        every = lax.all_gather(h1_share, "ctx", axis=0)
+        every = jnp.concatenate([every, every], axis=0)
+        every = lax.dynamic_slice_in_dim(every, here_ctx + 1, ctx - 1, 0)
+        remote = [(tuple(range(1, ctx)), every)]
+    remote_parts = [[value] + swaps([value] * mp, "mp") for _, value in remote]
+    groups = [(0,)] + [slots for slots, _ in remote]
     keys, values, klins, hiddens = [k_own], [v_own], [klin_own], [h1_own]
     for (slots, _), parts in zip(remote, remote_parts):
         size = len(slots)
@@ -703,7 +734,8 @@
         name="resid",
     )
 
-    grad_full = lax.all_gather(og, "mp", axis=0, tiled=True)
+    og_late, *_ = lax.optimization_barrier((og, *[parts[-1] for parts in remote_parts]))
+    grad_full = lax.all_gather(og_late, "mp", axis=0, tiled=True)
     tile = 256 if feed % 256 == 0 else feed
     col_block = pl.BlockSpec((model, tile), lambda i: (0, i))
     row_block = pl.BlockSpec((tile, model), lambda i: (i, 0))
@@ -738,16 +770,29 @@
         flops=8 * ctx_rows * model * feed,
         name="feed_weights",
     )
+    h2_own, dg, du, dd = lax.optimization_barrier((h2_parts[0], dg, du, dd))
     dg, du, dd = lax.psum((dg, du, dd), ("dp", "ctx"))
 
     resid_grad, low_share, gain2_part = call(
         resid_back_kernel,
-        [resid, og, gain2, h2_parts[0]] + h2_got,
+        [resid, og, gain2, h2_own] + h2_got,
         [out((share, model), F32), out((share, model), BF), out((1, model), F32)],
         name="resid_back",
     )
     low_parts = [low_share] + swaps([low_share] * mp, "mp")
 
+    o_mine, o_other = call(
+        o_weights_kernel,
+        [here_dp[None], att_t] + low_parts,
+        [out((q_width // 2, model), BF)] * 2,
+        in_specs={0: SMEM},
+        scratch=[pltpu.VMEM((ctx_rows, model), BF)],
+        name="o_weights",
+    )
+    bit = ((here_ctx & 1) ^ ((here_ctx >> 1) & 1))[None]
+    o_chunks = sum_over_ctx(o_mine, o_other, bit, few)
+    first_low, _ = lax.optimization_barrier((low_parts[0], o_other))
+    low_parts = [first_low] + low_parts[1:]
     head_rows = pl.BlockSpec((seq_rows, width), lambda h: (0, h), **buffers)
     ql, dk, dv, gq_part = call(
         lambda *refs: attend_back_kernel(joined, ctx_rows, width, mp, *refs),
@@ -785,45 +830,75 @@
     )
 
     f_got = swaps(f_parts, "mp")
+    dk, *f_got = lax.optimization_barrier((dk, *f_got))
     output = call(
         sum_kernel, [resid, f_parts[0]] + f_got, [out((share, model), BF)], name="output"
     )[0][None]
 
-    lows = {}
+    m = len(groups)
+    starts = [sum(len(slots) for slots in groups[:i]) for i in range(m)]
+    slot_at = [slot for slots in groups for slot in slots]
+
+    def stepped(i, rows, columns):
+        first, size = starts[i], len(groups[i])
+        return pl.BlockSpec((rows, columns), lambda s: (jnp.clip(s - first, 0, size - 1), 0))
+
+    def ordered(rows, columns):
+        def place(s):
+            slot = s
+            for step, value in enumerate(slot_at):
+                if step != value:
+                    slot = jnp.where(s == step, value, slot)
+            return slot, 0
+
+        return pl.BlockSpec((rows, columns), place)
+
+    kl, vl, mine, other, gain1_part, gk_part = call(
+        lambda *refs: weights_kernel(groups, *refs),
+        [here_dp[None], ql, dk, dv, cosines, sines, gk_row]
+        + hiddens
+        + klins
+        + [q_weight, key_matrix, value_matrix, norm1_gain.astype(F32)[:, None]],
+        [out((seq_rows, k_width), BF)] * 2
+        + [out((model // 2, q_width + 2 * k_width), BF)] * 2
+        + [out((model, 1), F32), out((1, width), F32)],
+        grid=(ctx,),
+        in_specs={
+            0: SMEM,
+            2: ordered(ctx_rows, k_width),
+            3: ordered(ctx_rows, k_width),
+            4: ordered(ctx_rows, width),
+            5: ordered(ctx_rows, width),
+            **{7 + i: stepped(i, ctx_rows, model) for i in range(m)},
+            **{7 + m + i: stepped(i, ctx_rows, k_width) for i in range(m)},
+        },
+        out_specs={0: ordered(ctx_rows, k_width), 1: ordered(ctx_rows, k_width)},
+        scratch=[pltpu.VMEM((model, q_width + 2 * k_width), F32)],
+        name="weights",
+    )
 
     def hidden_back(slots):
         size = len(slots)
         own = slots == (0,)
-        at = groups.index(slots)
-        ins = ([ql, q_weight] if own else []) + [
-            dk, dv, klins[at], cosines, sines, gk_row, key_matrix, value_matrix
-        ]
+        ins = ([ql, q_weight] if own else []) + [kl, vl, key_matrix, value_matrix]
         skip = 2 if own else 0
         block = slot_blocks(slots, ctx_rows, k_width)
-        table = slot_blocks(slots, ctx_rows, width)
-        here = pl.BlockSpec((ctx_rows, k_width), lambda i: (i, 0))
-        kl, vl, gk_part, *parts = call(
+        parts = call(
             lambda *refs: hidden_back_kernel(own, mp, *refs),
             ins,
-            [out((size * ctx_rows, k_width), BF)] * 2
-            + [out((1, width), F32), out((size, share, model), F32)]
-            + [out((size, share, model), BF)] * (mp - 1),
+            [out((size, share, model), F32)] + [out((size, share, model), BF)] * (mp - 1),
             grid=(size,),
-            in_specs={skip: block, skip + 1: block, skip + 2: here, skip + 3: table, skip + 4: table},
+            in_specs={skip: block, skip + 1: block},
             out_specs={
-                0: here,
-                1: here,
-                **{3 + j: pl.BlockSpec((1, share, model), lambda i: (i, 0, 0)) for j in range(mp)},
+                j: pl.BlockSpec((1, share, model), lambda i: (i, 0, 0)) for j in range(mp)
             },
-            flops=4 * size * ctx_rows * model * k_width,
             name="hidden_back",
         )
-        lows[at] = (kl, vl, gk_part)
         return parts, swaps(parts, "mp")
 
     terms = []
     if few:
-        for slots in ([(2,), (1, 3)] if ctx == 4 else [tuple(range(1, ctx))]):
+        for slots in ((2,), (1, 3)):
             parts, got = hidden_back(slots)
             for i, slot in enumerate(slots):
                 summed = sum_parts([p[i] for p in [parts[0]] + got], BF)
@@ -836,69 +911,20 @@
         natural = lax.dynamic_slice_in_dim(padded, (ctx - here_ctx) % ctx, ctx, 0)
         terms.append(lax.psum_scatter(natural, "ctx", scatter_dimension=0, tiled=False))
     parts, got = hidden_back((0,))
+    chunks = sum_over_ctx(mine, other, bit, few, (dg, du, dd, got[-1]))
     terms = [p[0] for p in [parts[0]] + got] + terms
     input_grad = call(
         input_back_kernel, [tok, resid_grad, gain1] + terms, [out((share, model), F32)], name="input_back"
     )[0][None]
 
-    total_rows = model + q_width
-    kls, vls, gk_parts = zip(*[lows[i] for i in range(len(groups))])
-    gk_part = sum(gk_parts[1:], gk_parts[0])
-    m = len(groups)
-    starts = [sum(len(slots) for slots in groups[:i]) for i in range(m)]
-
-    def stepped(i, rows, columns):
-        first, size = starts[i], len(groups[i])
-        return pl.BlockSpec((rows, columns), lambda s: (jnp.clip(s - first, 0, size - 1), 0))
-
-    mine, other, gain1_part = call(
-        lambda *refs: weights_kernel(groups, mp, *refs),
-        [here_dp[None], ql, att_t]
-        + hiddens
-        + list(kls)
-        + list(vls)
-        + low_parts
-        + [q_weight, key_matrix, value_matrix, norm1_gain.astype(F32)[:, None]],
-        [out((total_rows // 2, q_width + 2 * k_width), BF)] * 2 + [out((model, 1), F32)],
-        grid=(ctx,),
-        in_specs={
-            0: SMEM,
-            **{3 + i: stepped(i, ctx_rows, model) for i in range(m)},
-            **{3 + m + i: stepped(i, ctx_rows, k_width) for i in range(m)},
-            **{3 + 2 * m + i: stepped(i, ctx_rows, k_width) for i in range(m)},
-        },
-        scratch=[
-            pltpu.VMEM((model, 2 * k_width), F32),
-            pltpu.VMEM((ctx_rows, model), BF),
-            pltpu.VMEM((total_rows, q_width + 2 * k_width), F32),
-        ],
-        flops=2 * model * (ctx_rows * q_width * 2 + 2 * seq_rows * k_width),
-        name="weights",
-    )
-    got = swap(other, "dp", 1)
     if few:
-        rows = total_rows // 2 // ctx
-        places = slot_ctx
-        pieces = call(
-            split_kernel,
-            [places, mine, got],
-            [out((rows, mine.shape[1]), F32)] + [out((rows, mine.shape[1]), BF)] * (ctx - 1),
-            in_specs={0: SMEM},
-            name="split",
-        )
-        chunk = sum_parts(
-            [pieces[0]] + [to_ctx(pieces[k], k) for k in range(1, ctx)], BF
-        )
-        chunks = [chunk] + [from_ctx(chunk, k) for k in range(1, ctx)]
-        chunks = chunks + [swap(c, "dp", 1) for c in chunks]
-        spots = jnp.concatenate([places + here_dp * ctx, places + (1 - here_dp) * ctx])
+        spots = jnp.concatenate([bit, 1 - bit]) + 2 * here_dp
+        spots = jnp.concatenate([spots, jnp.concatenate([bit, 1 - bit]) + 2 * (1 - here_dp)])
     else:
-        chunk = lax.psum(sum_parts([mine, got], BF), "ctx")
-        chunks = [chunk, swap(chunk, "dp", 1)]
         spots = jnp.stack([here_dp, 1 - here_dp])
     q_w_grad, k_w_grad, v_w_grad, o_w_grad = call(
-        lambda *refs: spread_kernel(q_width, k_width, model, *refs),
-        [spots] + chunks,
+        lambda *refs: spread_kernel(q_width, k_width, len(chunks), *refs),
+        [spots] + chunks + o_chunks,
         [
             out((model, q_width), F32),
             out((model, k_width), F32),
@@ -906,7 +932,6 @@
             out((q_width, model), F32),
         ],
         in_specs={0: SMEM},
-        scratch=[pltpu.VMEM((total_rows, q_width + 2 * k_width), F32)],
         name="spread",
     )
 
@@ -914,9 +939,10 @@
         [gain1_part.reshape(-1), gain2_part.reshape(-1), gq_part.reshape(-1), gk_part.reshape(-1)]
     )
     if few:
-        gains = gains + swap(gains, "dp", 1)
-        gains = sum(swaps([gains] * mp, "mp"), gains)
-        gains = sum([from_ctx(gains, k) for k in range(1, ctx)], gains)
+        for axis in ("dp", "mp", "ctx"):
+            for step in (1, 2, 4):
+                if step < lax.axis_size(axis):
+                    gains = gains + swap(gains, axis, step)
     else:
         gains = lax.psum(gains, ("dp", "ctx", "mp"))
     return (

time: 432 us -> 348 us (0.81)
  waiting for transfers between devices: 198 us -> 120 us
  starting transfers between devices: 84.8 us -> 67.9 us
  local copies, waits for them, and re-layouts: 13.8 us -> 23.1 us
    ppermute x6 -> x3, waiting for transfers between devices: 93.5 us -> 9.05 us  [to_ctx(): lax.ppermute(value, 'ctx', [(i, (i + step) % size) for i in range(size)])]
    ppermute x9 -> x3, starting transfers between devices: 31.8 us -> 5.9 us  [from_ctx(): lax.ppermute(value, 'ctx', [((i + step) % size, i) for i in range(size)])]
    psum x1, waiting for transfers between devices: 12.5 us -> 25.9 us  [on_device(): dg, du, dd = lax.psum((dg, du, dd), ('dp', 'ctx'))]
    ppermute x42 -> x50, starting transfers between devices: 43 us -> 53.2 us  [swap(): return lax.ppermute(value, axis, [(i, i ^ step) for i in range(size)])]
    unnamed x75 -> x105, local copies, waits for them, and re-layouts: 8.91 us -> 18.3 us
    ppermute x42 -> x50, waiting for transfers between devices: 81.4 us -> 75 us  [swap(): return lax.ppermute(value, axis, [(i, i ^ step) for i in range(size)])]
    pallas_call x22 -> x27, Pallas kernels: 100 us -> 104 us  [call(): pl.pallas_call(kernel, grid=grid, in_specs=[in_specs.get(i, whole_spec(a)...]
    ppermute x6 -> x3, starting transfers between devices: 9.97 us -> 8.55 us  [to_ctx(): lax.ppermute(value, 'ctx', [(i, (i + step) % size) for i in range(size)])]
  transfers between devices with their start and end apart: 59 -> 58, of which waited for: 24 -> 25; matrix products, arithmetic and copies ran while one was open for 5% -> 6% of each run, Pallas kernels for 10% -> 24%
where the time goes in v2:
time: 348 us; the launch traced here: 347 us
  waiting for transfers between devices  120 us (34%)
  Pallas kernels  104 us (30%)
  starting transfers between devices  67.9 us (20%)
  local copies, waits for them, and re-layouts  23.1 us (7%)
  other arithmetic  16.9 us (5%)
  between operations  14.7 us (4%)
    pallas_call x27, Pallas kernels, call(): pl.pallas_call(kernel, grid=grid, in_specs=[in_specs.get(i, whole_spec(a)...  104 us
    ppermute x50, waiting for transfers between devices, swap(): return lax.ppermute(value, axis, [(i, i ^ step) for i in range(size)])  75 us
    ppermute x50, starting transfers between devices, swap(): return lax.ppermute(value, axis, [(i, i ^ step) for i in range(size)])  53.2 us
    psum x1, waiting for transfers between devices, on_device(): dg, du, dd = lax.psum((dg, du, dd), ('dp', 'ctx'))  25.9 us
    unnamed x105, local copies, waits for them, and re-layouts  18.3 us
    ppermute x3, waiting for transfers between devices, from_ctx(): lax.ppermute(value, 'ctx', [((i + step) % size, i) for i in range(size)])  10.4 us
    ppermute x3, waiting for transfers between devices, to_ctx(): lax.ppermute(value, 'ctx', [(i, (i + step) % size) for i in range(size)])  9.05 us
    ppermute x3, starting transfers between devices, to_ctx(): lax.ppermute(value, 'ctx', [(i, (i + step) % size) for i in range(size)])  8.55 us
  transfers between devices with their start and end apart: 58, of which 25 were waited for; matrix products, arithmetic and copies ran while one was open for 6% of the time, Pallas kernels for 24%

profile of v2, /device:TPU:0, one launch (start us, length us, event | category | flops | bytes accessed | tf_op | source)
XLA Modules:
  0.0 347.0 jit_solution(10151350410923135810)
XLA Ops:
  9.0 5.1 %collective-permute-start = (bf16[128,1024]{1,0:T(8,128)(2,1)S(1)}, bf16[128,1024]{1,0:T(8,128)(2,1)S(1)}, u32[]{:S(2)}, u32[]{:S(2)}) collective-permute-start(bf16[128,1024]{1,0:T(8,128)(2,1)S(1)} %norm1.1.refs_0_), channel_id=1, source_target_pairs={{4,0},{8,4},{12,8},{0,12},{5,1},{9,5},{13,9},{1,13},{6,2},{10,6},{... | collective-permute-start | bytes 786440 | tf_op jit(solution)/shard_map/ppermute | solution.py:65
  20.7 3.7 %fusion = (f32[2048,64]{1,0:T(8,128)S(1)}, f32[2048,64]{1,0:T(8,128)S(1)}, f32[2048,64]{1,0:T(8,128)S(1)}) fusion(f32[64]{0:T(128)S(1)} %multiply_power_fusion, f32[2048]{0:T(1024)S(1)} %bitcast.92), kind=kLoop, calls=%fused_computation.7 | loop fusion | flops 262144 | bytes 1581312 | tf_op jit(solution)/shard_map/neg | solution.py:617
  28.8 4.6 %own_rows.1 = (bf16[512,512]{1,0:T(8,128)(2,1)}, f32[512,512]{1,0:T(8,128)}, bf16[512,256]{1,0:T(8,128)(2,1)S(1)}, bf16[512,256]{1,0:T(8,128)(2,1)S(1)}, f32[512,256]{1,0:T(8,128)}, /*index=5*/bf16[512,1024]{1,0:T(8,128)(2,1)}) custom-call(bf16[128,1024]{1,0:T(8,128)(2,1)S(1)} %norm1.1.refs_0_, bf16[128,1024]{1,0:T(8,128)(2,1)S(1)} %collective-permute-done.2.refs_1_, ...), custom_call_target="tpu_custom_call" | custom-call | tf_op jit(solution)/shard_map/own_rows/pallas_call | solution.py:35
  36.2 10.4 %collective-permute-done.8 = bf16[128,1024]{1,0:T(8,128)(2,1)S(1)} collective-permute-done((bf16[128,1024]{1,0:T(8,128)(2,1)S(1)}, bf16[128,1024]{1,0:T(8,128)(2,1)S(1)}, u32[]{:S(2)}, u32[]{:S(2)}) %collective-permute-start.8) | collective-permute-done | bytes 262176 | tf_op jit(solution)/shard_map/ppermute | solution.py:65
  48.5 6.5 %collective-permute-done.11.refs_3_ = bf16[1,128,1024]{2,1,0:T(8,128)(2,1)S(1)} collective-permute-done((bf16[1,128,1024]{2,1,0:T(8,128)(2,1)S(1)}, bf16[1,128,1024]{2,1,0:T(8,128)(2,1)S(1)}, u32[]{:S(2)}, u32[]{:S(2)}) %collective-permute-start.11) | collective-permute-done | bytes 262176 | tf_op jit(solution)/shard_map/ppermute | solution.py:54
  60.2 12.8 %collective-permute-done.5.refs_1_ = bf16[2,128,1024]{2,1,0:T(8,128)(2,1)S(1)} collective-permute-done((bf16[2,128,1024]{2,1,0:T(8,128)(2,1)S(1)}, bf16[2,128,1024]{2,1,0:T(8,128)(2,1)S(1)}, u32[]{:S(2)}, u32[]{:S(2)}) %collective-permute-start.5) | collective-permute-done | bytes 524320 | tf_op jit(solution)/shard_map/ppermute | solution.py:54
  74.5 5.5 %remote_rows.2 = (bf16[1024,256]{1,0:T(8,128)(2,1)S(1)}, bf16[1024,256]{1,0:T(8,128)(2,1)S(1)}, f32[1024,256]{1,0:T(8,128)}, bf16[1024,1024]{1,0:T(8,128)(2,1)}) custom-call(bf16[2,128,1024]{2,1,0:T(8,128)(2,1)S(1)} %pad_maximum_fusion.2.refs_0_, bf16[2,128,1024]{2,1,0:T(8,128)(2,1)} %copy-done.45, bf16[2,128,1024]{2,1,0:T(8,128)(2,1)} %collective-permute-done.6.refs_2_, ...), custom_call_target="tpu_custom_call" | custom-call | tf_op jit(solution)/shard_map/remote_rows/pallas_call | solution.py:35
  81.6 3.8 %remote_rows.3 = (bf16[512,256]{1,0:T(8,128)(2,1)S(1)}, bf16[512,256]{1,0:T(8,128)(2,1)S(1)}, f32[512,256]{1,0:T(8,128)}, bf16[512,1024]{1,0:T(8,128)(2,1)}) custom-call(bf16[1,128,1024]{2,1,0:T(8,128)(2,1)S(1)} %bitcast.70, bf16[1,128,1024]{2,1,0:T(8,128)(2,1)S(1)} %collective-permute-done.9.refs_1_, ...), custom_call_target="tpu_custom_call" | custom-call | tf_op jit(solution)/shard_map/remote_rows/pallas_call | solution.py:35
  85.4 11.4 %attend.1 = (f32[512,512]{1,0:T(8,128)}, bf16[512,512]{1,0:T(8,128)(2,1)}, f32[2,2,512]{2,1,0:T(2,128)S(1)}, f32[128,1024]{1,0:T(8,128)}, bf16[128,1024]{1,0:T(8...) custom-call(s32[8]{0:T(128)S(1)} %select_reduce_fusion.1.refs_0_, ...), custom_call_target="tpu_custom_call" | custom-call | tf_op jit(solution)/shard_map/attend/pallas_call | solution.py:35
  100.4 2.9 collective-permute-done.12.refs_0_
  103.3 3.0 collective-permute-done.13.refs_1_
  114.0 2.9 collective-permute-done.15.refs_2_
  120.7 12.4 %feed.1 = (bf16[512,1024]{1,0:T(8,128)(2,1)}, bf16[512,1024]{1,0:T(8,128)(2,1)}, bf16[512,768]{1,0:T(8,128)(2,1)}, bf16[512,768]{1,0:T(8,128)(2,1)}, bf16[512,76...) custom-call(s32[4]{0:T(128)S(1)} %iota_xor_fusion.refs_0_, ...), custom_call_target="tpu_custom_call" | custom-call | tf_op jit(solution)/shard_map/feed/pallas_call | solution.py:35
  136.7 8.4 %feed_weights.1 = (bf16[1024,768]{1,0:T(8,128)(2,1)}, bf16[1024,768]{1,0:T(8,128)(2,1)}, bf16[768,1024]{1,0:T(8,128)(2,1)}, f32[128,1024]{1,0:T(8,128)S(1)}, bf1...) custom-call(bf16[512,1024]{1,0:T(8,128)(2,1)} %get-tuple-element.120.hidden_ref, ...), custom_call_target="tpu_custom_call" | custom-call | tf_op jit(solution)/shard_map/feed_weights/pallas_call | solution.py:35
  163.0 14.1 %attend_back.1 = (bf16[512,512]{1,0:T(8,128)(2,1)}, f32[2048,256]{1,0:T(8,128)}, f32[2048,256]{1,0:T(8,128)}, f32[128,1]{1,0:T(8,128)S(1)}) custom-call(s32[8]{0:T(128)S(1)} %select_reduce_fusion.1.refs_0_, s32[2]{0:T(128)S(1)} %slice_bitcast_fusion.8.refs_1_, s32[256,1]{1,0:T(8,128)S(1)} %copy.36.refs_2_, s32[1,512]{1,0:T(1,128)S(1)} %get-tuple-element.210.refs_3_, ...), custom_call_target="tpu_custom_call" | custom-call | tf_op jit(solution)/shard_map/attend_back/pallas_call | solution.py:35
  178.5 12.9 %weights.1 = (bf16[2048,256]{1,0:T(8,128)(2,1)}, bf16[2048,256]{1,0:T(8,128)(2,1)}, bf16[512,1024]{1,0:T(8,128)(2,1)}, bf16[512,1024]{1,0:T(8,128)(2,1)}, f32[1024,1]{1,0:T(8,128)S(1)}, /*index=5*/f32[1,128]{1,0:T(1,128)S(1)}) custom-call(s32[1]{0:T(128)} %bitcast.18.core_ref.refs_0_, bf16[512,512]{1,0:T(8,128)(2,1)S(1)} %copy-done.6, ...), custom_call_target="tpu_custom_call" | custom-call | tf_op jit(solution)/shard_map/weights/pallas_call | solution.py:35
  191.6 2.9 collective-permute-done.44.got_ref
  201.1 3.8 %hidden_back.3 = (f32[1,128,1024]{2,1,0:T(8,128)S(1)}, bf16[1,128,1024]{2,1,0:T(8,128)(2,1)S(1)}, bf16[1,128,1024]{2,1,0:T(8,128)(2,1)}, bf16[1,128,1024]{2,1,0:T(8,128)(2,1)}) custom-call(bf16[512,512]{1,0:T(8,128)(2,1)S(1)} %copy-done.7, bf16[1024,512]{1,0:T(8,128)(2,1)} %refs_1_.1, bf16[2048,256]{1,0:T(8,128)(2,1)} %get-tuple-element.158.refs_2_.refs_0_, ...), custom_call_target="tpu_custom_call" | custom-call | tf_op jit(solution)/shard_map/hidden_back/pallas_call | solution.py:35
  209.2 5.6 %collective-permute-done.40 = f32[2304]{0:T(1024)S(1)} collective-permute-done((f32[2304]{0:T(1024)S(1)}, f32[2304]{0:T(1024)S(1)}, u32[]{:S(2)}, u32[]{:S(2)}) %collective-permute-start.40) | collective-permute-done | bytes 9248 | tf_op jit(solution)/shard_map/ppermute | solution.py:54
  216.4 2.8 hidden_back.4
  220.0 3.2 collective-permute-done.42
  227.3 3.7 %hidden_back.5 = (f32[2,128,1024]{2,1,0:T(8,128)}, bf16[2,128,1024]{2,1,0:T(8,128)(2,1)}, bf16[2,128,1024]{2,1,0:T(8,128)(2,1)S(1)}, bf16[2,128,1024]{2,1,0:T(8,128)(2,1)S(1)}) custom-call(bf16[2048,256]{1,0:T(8,128)(2,1)} %get-tuple-element.158.refs_2_.refs_0_, bf16[2048,256]{1,0:T(8,128)(2,1)} %get-tuple-element.159.refs_3_.refs_1_, ...), custom_call_target="tpu_custom_call" | custom-call | tf_op jit(solution)/shard_map/hidden_back/pallas_call | solution.py:35
  233.3 25.9 %all-reduce.3.cloned.1.call-done = (bf16[1024,768]{1,0:T(8,128)(2,1)}, bf16[1024,768]{1,0:T(8,128)(2,1)}, bf16[768,1024]{1,0:T(8,128)(2,1)}) async-done(((bf16[1024,768]{1,0:T(8,128)(2,1)}, bf16[1024,768]{1,0:T(8,128)(2,1)}, bf16[768,1024]{1,0:T(8,128)(2,1)}), (bf16[1024,768]{1,0:T(8,128)(2,1)}, bf16[1024,768]{1,0:T(8,128)(2,1)}, bf16[768,1024]{1,0:T(8,128)(2,1)})) %all-reduce.3.cloned.1.call-update) | async-done | bytes 4718608 | tf_op jit(solution)/shard_map/psum | solution.py:774
  269.1 11.5 %collective-permute-done.51.refs_1_ = bf16[128,1024]{1,0:T(8,128)(2,1)S(1)} collective-permute-done((bf16[128,1024]{1,0:T(8,128)(2,1)S(1)}, bf16[128,1024]{1,0:T(8,128)(2,1)S(1)}, u32[]{:S(2)}, u32[]{:S(2)}) %collective-permute-start.51) | collective-permute-done | bytes 262176 | tf_op jit(solution)/shard_map/ppermute | solution.py:54
  283.7 3.4 collective-permute-done.35
  292.6 5.7 %collective-permute-start.33 = (bf16[128,1024]{1,0:T(8,128)(2,1)}, bf16[128,1024]{1,0:T(8,128)(2,1)}, u32[]{:S(2)}, u32[]{:S(2)}) collective-permute-start(bf16[128,1024]{1,0:T(8,128)(2,1)} %sum_parts.7), channel_id=1, source_target_pairs={{0,8},{4,12},{8,0},{12,4},{1,9},{5,13},{9,1},{13,5},{2,10},{6,14},... | collective-permute-start | bytes 786440 | tf_op jit(solution)/shard_map/ppermute | solution.py:70
  298.3 3.5 %collective-permute-done.43 = f32[2304]{0:T(1024)S(1)} collective-permute-done((f32[2304]{0:T(1024)S(1)}, f32[2304]{0:T(1024)S(1)}, u32[]{:S(2)}, u32[]{:S(2)}) %collective-permute-start.43) | collective-permute-done | bytes 9248 | tf_op jit(solution)/shard_map/ppermute | solution.py:54
  301.9 2.8 collective-permute-start.37
  311.2 5.5 %collective-permute-done.33.refs_4_ = bf16[128,1024]{1,0:T(8,128)(2,1)} collective-permute-done((bf16[128,1024]{1,0:T(8,128)(2,1)}, bf16[128,1024]{1,0:T(8,128)(2,1)}, u32[]{:S(2)}, u32[]{:S(2)}) %collective-permute-start.33) | collective-permute-done | bytes 262176 | tf_op jit(solution)/shard_map/ppermute | solution.py:70
  316.8 4.0 %collective-permute-done.53.refs_6_ = bf16[128,1024]{1,0:T(8,128)(2,1)} collective-permute-done((bf16[128,1024]{1,0:T(8,128)(2,1)S(1)}, bf16[128,1024]{1,0:T(8,128)(2,1)}, u32[]{:S(2)}, u32[]{:S(2)}) %collective-permute-start.53) | collective-permute-done | bytes 262176 | tf_op jit(solution)/shard_map/ppermute | solution.py:54
  321.8 3.5 %collective-permute-done.38.refs_6_ = bf16[128,1024]{1,0:T(8,128)(2,1)S(1)} collective-permute-done((bf16[128,1024]{1,0:T(8,128)(2,1)S(1)}, bf16[128,1024]{1,0:T(8,128)(2,1)S(1)}, u32[]{:S(2)}, u32[]{:S(2)}) %collective-permute-start.38) | collective-permute-done | bytes 262176 | tf_op jit(solution)/shard_map/ppermute | solution.py:70
  335.7 4.4 %spread.1 = (f32[1024,512]{1,0:T(8,128)}, f32[1024,256]{1,0:T(8,128)}, f32[1024,256]{1,0:T(8,128)}, f32[512,1024]{1,0:T(8,128)}) custom-call(s32[4]{0:T(128)S(1)} %pad_add_fusion.1.refs_0_, bf16[256,1024]{1,0:T(8,128)(2,1)S(1)} %sum_parts.11.refs_1_, bf16[256,1024]{1,0:T(8,128)(2,1)} %collective-permute-done.47.refs_2_, bf16[256,1024]{1,0:T(8,128)(2,1)} %copy-done.42, ...), custom_call_target="tpu_custom_call" | custom-call | tf_op jit(solution)/shard_map/spread/pallas_call | solution.py:35
  (267 shorter events, 119.7 us)
Async XLA Ops:
  7.2 113.5 %all-gather.2.cloned.1.call-start = ((), (), s32[]{:S(2)}) async-start(), calls=%async_computation | async-start | bytes 1310720 | tf_op jit(solution)/shard_map/all_gather | solution.py:738
  9.0 18.1 %collective-permute-start = (bf16[128,1024]{1,0:T(8,128)(2,1)S(1)}, bf16[128,1024]{1,0:T(8,128)(2,1)S(1)}, u32[]{:S(2)}, u32[]{:S(2)}) collective-permute-start(bf16[128,1024]{1,0:T(8,128)(2,1)S(1)} %norm1.1.refs_0_), channel_id=1, source_target_pairs={{4,0},{8,4},{12,8},{0,12},{5,1},{9,5},{13,9},{1,13},{6,2},{10,6},{... | collective-permute-start | bytes 786440 | tf_op jit(solution)/shard_map/ppermute | solution.py:65
  34.2 14.3 %collective-permute-start.7 = (bf16[2,128,1024]{2,1,0:T(8,128)(2,1)S(1)}, bf16[2,128,1024]{2,1,0:T(8,128)(2,1)S(1)}, u32[]{:S(2)}, u32[]{:S(2)}) collective-permute-start(bf16[2,128,1024]{2,1,0:T(8,128)(2,1)S(1)} %pad_maximum_fusion.2.refs_0_), channel_id=1, source_target_pairs={{0,3},{1,2},{2,1},{3,0},{4,7},{5,6},{6,5},{7,4},{8,11},{9,10},{10,... | collective-permute-start | bytes 1572872 | tf_op jit(solution)/shard_map/ppermute | solution.py:54
  55.0 204.2 %all-reduce.3.cloned.1.call-start = ((), (), s32[]{:S(2)}) async-start(), calls=%async_computation.1 | async-start | bytes 9437184 | tf_op jit(solution)/shard_map/psum | solution.py:774
  55.3 17.7 %collective-permute-start.5 = (bf16[2,128,1024]{2,1,0:T(8,128)(2,1)S(1)}, bf16[2,128,1024]{2,1,0:T(8,128)(2,1)S(1)}, u32[]{:S(2)}, u32[]{:S(2)}) collective-permute-start(bf16[2,128,1024]{2,1,0:T(8,128)(2,1)S(1)} %pad_maximum_fusion.2.refs_0_), channel_id=1, source_target_pairs={{0,1},{1,0},{2,3},{3,2},{4,5},{5,4},{6,7},{7,6},{8,9},{9,8},{10,11... | collective-permute-start | bytes 1572872 | tf_op jit(solution)/shard_map/ppermute | solution.py:54
  56.8 17.7 %collective-permute-start.6 = (bf16[2,128,1024]{2,1,0:T(8,128)(2,1)S(1)}, bf16[2,128,1024]{2,1,0:T(8,128)(2,1)}, u32[]{:S(2)}, u32[]{:S(2)}) collective-permute-start(bf16[2,128,1024]{2,1,0:T(8,128)(2,1)S(1)} %pad_maximum_fusion.2.refs_0_), channel_id=1, source_target_pairs={{0,2},{1,3},{2,0},{3,1},{4,6},{5,7},{6,4},{7,5},{8,10},{9,11},{10,... | collective-permute-start | bytes 1572872 | tf_op jit(solution)/shard_map/ppermute | solution.py:54
  58.0 23.6 %collective-permute-start.9 = (bf16[1,128,1024]{2,1,0:T(8,128)(2,1)S(1)}, bf16[1,128,1024]{2,1,0:T(8,128)(2,1)S(1)}, u32[]{:S(2)}, u32[]{:S(2)}) collective-permute-start(bf16[1,128,1024]{2,1,0:T(8,128)(2,1)S(1)} %bitcast.68), channel_id=1, source_target_pairs={{0,1},{1,0},{2,3},{3,2},{4,5},{5,4},{6,7},{7,6},{8,9},{9,8},{10,11... | collective-permute-start | bytes 786440 | tf_op jit(solution)/shard_map/ppermute | solution.py:54
  58.6 23.1 %collective-permute-start.10 = (bf16[1,128,1024]{2,1,0:T(8,128)(2,1)S(1)}, bf16[1,128,1024]{2,1,0:T(8,128)(2,1)S(1)}, u32[]{:S(2)}, u32[]{:S(2)}) collective-permute-start(bf16[1,128,1024]{2,1,0:T(8,128)(2,1)S(1)} %bitcast.69), channel_id=1, source_target_pairs={{0,2},{1,3},{2,0},{3,1},{4,6},{5,7},{6,4},{7,5},{8,10},{9,11},{10,... | collective-permute-start | bytes 786440 | tf_op jit(solution)/shard_map/ppermute | solution.py:54
  152.7 24.5 %collective-permute-start.24 = (bf16[128,1024]{1,0:T(8,128)(2,1)}, bf16[128,1024]{1,0:T(8,128)(2,1)S(1)}, u32[]{:S(2)}, u32[]{:S(2)}) collective-permute-start(bf16[128,1024]{1,0:T(8,128)(2,1)} %get-tuple-element.142), channel_id=1, source_target_pairs={{0,1},{1,0},{2,3},{3,2},{4,5},{5,4},{6,7},{7,6},{8,9},{9,8},{10,11... | collective-permute-start | bytes 786440 | tf_op jit(solution)/shard_map/ppermute | solution.py:54
  153.7 23.5 %collective-permute-start.25 = (bf16[128,1024]{1,0:T(8,128)(2,1)}, bf16[128,1024]{1,0:T(8,128)(2,1)S(1)}, u32[]{:S(2)}, u32[]{:S(2)}) collective-permute-start(bf16[128,1024]{1,0:T(8,128)(2,1)} %get-tuple-element.143), channel_id=1, source_target_pairs={{0,2},{1,3},{2,0},{3,1},{4,6},{5,7},{6,4},{7,5},{8,10},{9,11},{10,... | collective-permute-start | bytes 786440 | tf_op jit(solution)/shard_map/ppermute | solution.py:54
  156.7 20.6 %collective-permute-start.26 = (bf16[128,1024]{1,0:T(8,128)(2,1)}, bf16[128,1024]{1,0:T(8,128)(2,1)S(1)}, u32[]{:S(2)}, u32[]{:S(2)}) collective-permute-start(bf16[128,1024]{1,0:T(8,128)(2,1)} %get-tuple-element.144), channel_id=1, source_target_pairs={{0,3},{1,2},{2,1},{3,0},{4,7},{5,6},{6,5},{7,4},{8,11},{9,10},{10,... | collective-permute-start | bytes 786440 | tf_op jit(solution)/shard_map/ppermute | solution.py:54
  198.9 32.1 %collective-permute-start.45 = (bf16[256,1024]{1,0:T(8,128)(2,1)}, bf16[256,1024]{1,0:T(8,128)(2,1)S(1)}, u32[]{:S(2)}, u32[]{:S(2)}) collective-permute-start(bf16[256,1024]{1,0:T(8,128)(2,1)} %get-tuple-element.179), channel_id=1, source_target_pairs={{0,4},{4,0},{8,12},{12,8},{1,5},{5,1},{9,13},{13,9},{2,6},{6,2},{1... | collective-permute-start | bytes 1572872 | tf_op jit(solution)/shard_map/ppermute | solution.py:54
  201.1 59.6 %collective-permute-start.50 = (bf16[256,1024]{1,0:T(8,128)(2,1)}, bf16[256,1024]{1,0:T(8,128)(2,1)}, u32[]{:S(2)}, u32[]{:S(2)}) collective-permute-start(bf16[256,1024]{1,0:T(8,128)(2,1)} %get-tuple-element.136), channel_id=1, source_target_pairs={{0,16},{16,0},{1,17},{17,1},{2,18},{18,2},{3,19},{19,3},{4,20},{20... | collective-permute-start | bytes 1572872 | tf_op jit(solution)/shard_map/ppermute | solution.py:54
  205.7 18.9 %collective-permute-start.29 = (bf16[1,128,1024]{2,1,0:T(8,128)(2,1)}, bf16[1,128,1024]{2,1,0:T(8,128)(2,1)S(1)}, u32[]{:S(2)}, u32[]{:S(2)}) collective-permute-start(bf16[1,128,1024]{2,1,0:T(8,128)(2,1)} %get-tuple-element.163), channel_id=1, source_target_pairs={{0,3},{1,2},{2,1},{3,0},{4,7},{5,6},{6,5},{7,4},{8,11},{9,10},{10,... | collective-permute-start | bytes 786440 | tf_op jit(solution)/shard_map/ppermute | solution.py:54
  219.2 40.0 %collective-permute-start.30 = (bf16[1,128,1024]{2,1,0:T(8,128)(2,1)}, bf16[1,128,1024]{2,1,0:T(8,128)(2,1)S(1)}, u32[]{:S(2)}, u32[]{:S(2)}) collective-permute-start(bf16[1,128,1024]{2,1,0:T(8,128)(2,1)} %get-tuple-element.165), channel_id=1, source_target_pairs={{0,1},{1,0},{2,3},{3,2},{4,5},{5,4},{6,7},{7,6},{8,9},{9,8},{10,11... | collective-permute-start | bytes 786440 | tf_op jit(solution)/shard_map/ppermute | solution.py:54
  223.2 40.2 %collective-permute-start.31 = (bf16[1,128,1024]{2,1,0:T(8,128)(2,1)}, bf16[1,128,1024]{2,1,0:T(8,128)(2,1)S(1)}, u32[]{:S(2)}, u32[]{:S(2)}) collective-permute-start(bf16[1,128,1024]{2,1,0:T(8,128)(2,1)} %get-tuple-element.166), channel_id=1, source_target_pairs={{0,2},{1,3},{2,0},{3,1},{4,6},{5,7},{6,4},{7,5},{8,10},{9,11},{10,... | collective-permute-start | bytes 786440 | tf_op jit(solution)/shard_map/ppermute | solution.py:54
  225.4 39.6 %collective-permute-start.32 = (bf16[1,128,1024]{2,1,0:T(8,128)(2,1)}, bf16[1,128,1024]{2,1,0:T(8,128)(2,1)S(1)}, u32[]{:S(2)}, u32[]{:S(2)}) collective-permute-start(bf16[1,128,1024]{2,1,0:T(8,128)(2,1)} %get-tuple-element.167), channel_id=1, source_target_pairs={{0,3},{1,2},{2,1},{3,0},{4,7},{5,6},{6,5},{7,4},{8,11},{9,10},{10,... | collective-permute-start | bytes 786440 | tf_op jit(solution)/shard_map/ppermute | solution.py:54
  231.0 36.4 %collective-permute-start.34 = (bf16[2,128,1024]{2,1,0:T(8,128)(2,1)}, bf16[2,128,1024]{2,1,0:T(8,128)(2,1)}, u32[]{:S(2)}, u32[]{:S(2)}) collective-permute-start(bf16[2,128,1024]{2,1,0:T(8,128)(2,1)} %get-tuple-element.169), channel_id=1, source_target_pairs={{0,1},{1,0},{2,3},{3,2},{4,5},{5,4},{6,7},{7,6},{8,9},{9,8},{10,11... | collective-permute-start | bytes 1572872 | tf_op jit(solution)/shard_map/ppermute | solution.py:54
  259.2 22.2 %collective-permute-start.46 = (bf16[256,1024]{1,0:T(8,128)(2,1)S(1)}, bf16[256,1024]{1,0:T(8,128)(2,1)S(1)}, u32[]{:S(2)}, u32[]{:S(2)}) collective-permute-start(bf16[256,1024]{1,0:T(8,128)(2,1)S(1)} %sum_parts.10.refs_0_), channel_id=1, source_target_pairs={{0,12},{4,8},{8,4},{12,0},{1,13},{5,9},{9,5},{13,1},{2,14},{6,10},... | collective-permute-start | bytes 1572872 | tf_op jit(solution)/shard_map/ppermute | solution.py:54
  260.8 26.4 %collective-permute-start.35 = (bf16[2,128,1024]{2,1,0:T(8,128)(2,1)}, bf16[2,128,1024]{2,1,0:T(8,128)(2,1)}, u32[]{:S(2)}, u32[]{:S(2)}) collective-permute-start(bf16[2,128,1024]{2,1,0:T(8,128)(2,1)} %copy-done.34), channel_id=1, source_target_pairs={{0,2},{1,3},{2,0},{3,1},{4,6},{5,7},{6,4},{7,5},{8,10},{9,11},{10,... | collective-permute-start | bytes 1572872 | tf_op jit(solution)/shard_map/ppermute | solution.py:54
  263.4 25.0 %collective-permute-start.36 = (bf16[2,128,1024]{2,1,0:T(8,128)(2,1)}, bf16[2,128,1024]{2,1,0:T(8,128)(2,1)S(1)}, u32[]{:S(2)}, u32[]{:S(2)}) collective-permute-start(bf16[2,128,1024]{2,1,0:T(8,128)(2,1)} %copy-done.33), channel_id=1, source_target_pairs={{0,3},{1,2},{2,1},{3,0},{4,7},{5,6},{6,5},{7,4},{8,11},{9,10},{10,... | collective-permute-start | bytes 1572872 | tf_op jit(solution)/shard_map/ppermute | solution.py:54
  265.7 14.9 %collective-permute-start.51 = (bf16[128,1024]{1,0:T(8,128)(2,1)S(1)}, bf16[128,1024]{1,0:T(8,128)(2,1)S(1)}, u32[]{:S(2)}, u32[]{:S(2)}) collective-permute-start(bf16[128,1024]{1,0:T(8,128)(2,1)S(1)} %get-tuple-element.186), channel_id=1, source_target_pairs={{0,4},{4,0},{8,12},{12,8},{1,5},{5,1},{9,13},{13,9},{2,6},{6,2},{1... | collective-permute-start | bytes 786440 | tf_op jit(solution)/shard_map/ppermute | solution.py:54
  267.4 37.3 %collective-permute-start.27 = (bf16[1,128,1024]{2,1,0:T(8,128)(2,1)S(1)}, bf16[1,128,1024]{2,1,0:T(8,128)(2,1)S(1)}, u32[]{:S(2)}, u32[]{:S(2)}) collective-permute-start(bf16[1,128,1024]{2,1,0:T(8,128)(2,1)S(1)} %copy-done.36), channel_id=1, source_target_pairs={{0,1},{1,0},{2,3},{3,2},{4,5},{5,4},{6,7},{7,6},{8,9},{9,8},{10,11... | collective-permute-start | bytes 786440 | tf_op jit(solution)/shard_map/ppermute | solution.py:54
  280.6 26.2 %collective-permute-start.28 = (bf16[1,128,1024]{2,1,0:T(8,128)(2,1)}, bf16[1,128,1024]{2,1,0:T(8,128)(2,1)}, u32[]{:S(2)}, u32[]{:S(2)}) collective-permute-start(bf16[1,128,1024]{2,1,0:T(8,128)(2,1)} %get-tuple-element.162), channel_id=1, source_target_pairs={{0,2},{1,3},{2,0},{3,1},{4,6},{5,7},{6,4},{7,5},{8,10},{9,11},{10,... | collective-permute-start | bytes 786440 | tf_op jit(solution)/shard_map/ppermute | solution.py:54
  287.1 19.7 %collective-permute-start.47 = (bf16[256,1024]{1,0:T(8,128)(2,1)S(1)}, bf16[256,1024]{1,0:T(8,128)(2,1)}, u32[]{:S(2)}, u32[]{:S(2)}) collective-permute-start(bf16[256,1024]{1,0:T(8,128)(2,1)S(1)} %sum_parts.11.refs_1_), channel_id=1, source_target_pairs={{0,4},{4,0},{8,12},{12,8},{1,5},{5,1},{9,13},{13,9},{2,6},{6,2},{1... | collective-permute-start | bytes 1572872 | tf_op jit(solution)/shard_map/ppermute | solution.py:54
  288.4 13.5 %collective-permute-start.43 = (f32[2304]{0:T(1024)S(1)}, f32[2304]{0:T(1024)S(1)}, u32[]{:S(2)}, u32[]{:S(2)}) collective-permute-start(f32[2304]{0:T(1024)S(1)} %add.117), channel_id=1, source_target_pairs={{0,8},{4,12},{8,0},{12,4},{1,9},{5,13},{9,1},{13,5},{2,10},{6,14},... | collective-permute-start | bytes 27656 | tf_op jit(solution)/shard_map/ppermute | solution.py:54
  292.6 24.2 %collective-permute-start.33 = (bf16[128,1024]{1,0:T(8,128)(2,1)}, bf16[128,1024]{1,0:T(8,128)(2,1)}, u32[]{:S(2)}, u32[]{:S(2)}) collective-permute-start(bf16[128,1024]{1,0:T(8,128)(2,1)} %sum_parts.7), channel_id=1, source_target_pairs={{0,8},{4,12},{8,0},{12,4},{1,9},{5,13},{9,1},{13,5},{2,10},{6,14},... | collective-permute-start | bytes 786440 | tf_op jit(solution)/shard_map/ppermute | solution.py:70
  301.9 14.9 %collective-permute-start.37 = (bf16[128,1024]{1,0:T(8,128)(2,1)}, bf16[128,1024]{1,0:T(8,128)(2,1)}, u32[]{:S(2)}, u32[]{:S(2)}) collective-permute-start(bf16[128,1024]{1,0:T(8,128)(2,1)} %sum_parts.8), channel_id=1, source_target_pairs={{0,4},{4,8},{8,12},{12,0},{1,5},{5,9},{9,13},{13,1},{2,6},{6,10},{... | collective-permute-start | bytes 786440 | tf_op jit(solution)/shard_map/ppermute | solution.py:70
  305.4 15.3 %collective-permute-start.53 = (bf16[128,1024]{1,0:T(8,128)(2,1)S(1)}, bf16[128,1024]{1,0:T(8,128)(2,1)}, u32[]{:S(2)}, u32[]{:S(2)}) collective-permute-start(bf16[128,1024]{1,0:T(8,128)(2,1)S(1)} %sum_parts.13.refs_5_), channel_id=1, source_target_pairs={{0,4},{4,0},{8,12},{12,8},{1,5},{5,1},{9,13},{13,9},{2,6},{6,2},{1... | collective-permute-start | bytes 786440 | tf_op jit(solution)/shard_map/ppermute | solution.py:54
  306.8 27.3 %collective-permute-start.48 = (bf16[256,1024]{1,0:T(8,128)(2,1)S(1)}, bf16[256,1024]{1,0:T(8,128)(2,1)S(1)}, u32[]{:S(2)}, u32[]{:S(2)}) collective-permute-start(bf16[256,1024]{1,0:T(8,128)(2,1)S(1)} %sum_parts.11.refs_1_), channel_id=1, source_target_pairs={{0,16},{16,0},{1,17},{17,1},{2,18},{18,2},{3,19},{19,3},{4,20},{20... | collective-permute-start | bytes 1572872 | tf_op jit(solution)/shard_map/ppermute | solution.py:54
  306.8 27.3 %collective-permute-start.49 = (bf16[256,1024]{1,0:T(8,128)(2,1)}, bf16[256,1024]{1,0:T(8,128)(2,1)S(1)}, u32[]{:S(2)}, u32[]{:S(2)}) collective-permute-start(bf16[256,1024]{1,0:T(8,128)(2,1)} %collective-permute-done.47.refs_2_), channel_id=1, source_target_pairs={{0,16},{16,0},{1,17},{17,1},{2,18},{18,2},{3,19},{19,3},{4,20},{20... | collective-permute-start | bytes 1572872 | tf_op jit(solution)/shard_map/ppermute | solution.py:54
  316.7 17.3 %collective-permute-start.54 = (bf16[128,1024]{1,0:T(8,128)(2,1)S(1)}, bf16[128,1024]{1,0:T(8,128)(2,1)S(1)}, u32[]{:S(2)}, u32[]{:S(2)}) collective-permute-start(bf16[128,1024]{1,0:T(8,128)(2,1)S(1)} %sum_parts.13.refs_5_), channel_id=1, source_target_pairs={{0,16},{16,0},{1,17},{17,1},{2,18},{18,2},{3,19},{19,3},{4,20},{20... | collective-permute-start | bytes 786440 | tf_op jit(solution)/shard_map/ppermute | solution.py:54
  (78 other events, 656.5 us)
Sparse Core Ops, SparseCore 0:
  55.2 28.9 all-gather.1
  146.0 113.1 all-reduce.2

commit v3 on v2

--- a/solution.py
+++ b/solution.py
@@ -224,17 +224,23 @@
         numer[...] = jnp.zeros_like(numer)
         sums[...] = jnp.zeros_like(sums)
 
-        def step(i, carry):
+        def block(i):
             start = pl.multiple_of(order_ref[i] * half, half)
             scores = dot(k_all[pl.ds(start, half), :], queries, 1, 0)
             kpos = kpos_ref[...] + i * half
             seen = (kpos <= qpos) & (kpos >= qlow)
             weights = jnp.where(seen, jnp.exp2(scores * scale), 0.0)
-            sums[...] += jnp.sum(weights, axis=0, keepdims=True)
-            numer[...] += dot(v_all[pl.ds(start, half), :], weights.astype(BF), 0, 0)
+            added = dot(v_all[pl.ds(start, half), :], weights.astype(BF), 0, 0)
+            return jnp.sum(weights, axis=0, keepdims=True), added
+
+        def step(i, carry):
+            first_sum, first = block(2 * i)
+            second_sum, second = block(2 * i + 1)
+            sums[...] += first_sum + second_sum
+            numer[...] += first + second
             return carry
 
-        lax.fori_loop(0, last_ref[t] + 1, step, 0)
+        lax.fori_loop(0, last_ref[t] // 2 + 1, step, 0)
         total = sums[...]
         sums_ref[0, t : t + 1, :] = total
         result = numer[...] / total
@@ -277,17 +283,19 @@
             grads_ref[j * share : (j + 1) * share, :] = grad_ref[pl.ds(place, share), :]
 
     hidden = hidden_ref[...]
-    gate = dot(hidden, wg_ref[...], 1, 0)
-    up = dot(hidden, wu_ref[...], 1, 0)
+    tile = wg_ref.shape[1]
+    both = jnp.concatenate([wg_ref[...], wu_ref[...]], axis=1)
+    product = dot(hidden, both, 1, 0)
+    gate, up = product[:, :tile], product[:, tile:]
     act_grad = dot(grads_ref[...], wd_ref[...], 1, 1)
-    sig = 1.0 / (1.0 + jnp.exp(-gate))
+    sig = 0.5 * jnp.tanh(0.5 * gate) + 0.5
     silu = gate * sig
     act_ref[...] = (silu * up).astype(BF)
     gate_grad = (act_grad * up * sig * (1.0 + gate * (1.0 - sig))).astype(BF)
     up_grad = (act_grad * silu).astype(BF)
     gg_ref[...] = gate_grad
     ug_ref[...] = up_grad
-    added = dot(gate_grad, wg_ref[...], 1, 1) + dot(up_grad, wu_ref[...], 1, 1)
+    added = dot(jnp.concatenate([gate_grad, up_grad], axis=1), both, 1, 1)
 
     @pl.when(step == 0)
     def _():
@@ -374,7 +382,7 @@
         qlow = jnp.concatenate([qlow_ref[:, t * half : (t + 1) * half]] * per_group, axis=1)
         dq[...] = jnp.zeros_like(dq)
 
-        def step(i, carry):
+        def block(i):
             start = pl.multiple_of(order_ref[i] * half, half)
             keys = k_all[pl.ds(start, half), :]
             scores = dot(keys, queries, 1, 0)
@@ -385,10 +393,14 @@
             score_grad = (weights * (prob_grad - shift)).astype(BF)
             dv[pl.ds(start, half), :] += dot(weights.astype(BF), scaled, 1, 1)
             dk[pl.ds(start, half), :] += dot(score_grad, queries, 1, 1)
-            dq[...] += dot(keys, score_grad, 0, 0)
+            return dot(keys, score_grad, 0, 0)
+
+        def step(i, carry):
+            first = block(2 * i)
+            dq[...] += first + block(2 * i + 1)
             return carry
 
-        lax.fori_loop(0, last_ref[t] + 1, step, 0)
+        lax.fori_loop(0, last_ref[t] // 2 + 1, step, 0)
         for head in range(per_group):
             dqt[head * width : (head + 1) * width, t * half : (t + 1) * half] = dq[
                 :, head * half : (head + 1) * half

time: 348 us -> 344 us (0.989)
  Pallas kernels: 104 us -> 100 us
    pallas_call x27, Pallas kernels: 104 us -> 100 us  [call(): pl.pallas_call(kernel, grid=grid, in_specs=[in_specs.get(i, whole_spec(a)...]
  transfers between devices with their start and end apart: 58 -> 58, of which waited for: 25 -> 26; matrix products, arithmetic and copies ran while one was open for 6% -> 6% of each run, Pallas kernels for 24% -> 23%
where the time goes in v3:
time: 344 us; the launch traced here: 343 us
  waiting for transfers between devices  121 us (35%)
  Pallas kernels  100 us (29%)
  starting transfers between devices  67.6 us (20%)
  local copies, waits for them, and re-layouts  23.1 us (7%)
  other arithmetic  16.9 us (5%)
  between operations  14.6 us (4%)
    pallas_call x27, Pallas kernels, call(): pl.pallas_call(kernel, grid=grid, in_specs=[in_specs.get(i, whole_spec(a)...  100 us
    ppermute x50, waiting for transfers between devices, swap(): return lax.ppermute(value, axis, [(i, i ^ step) for i in range(size)])  75.5 us
    ppermute x50, starting transfers between devices, swap(): return lax.ppermute(value, axis, [(i, i ^ step) for i in range(size)])  52.9 us
    psum x1, waiting for transfers between devices, on_device(): dg, du, dd = lax.psum((dg, du, dd), ('dp', 'ctx'))  25.9 us
    unnamed x105, local copies, waits for them, and re-layouts  18.3 us
    ppermute x3, waiting for transfers between devices, from_ctx(): lax.ppermute(value, 'ctx', [((i + step) % size, i) for i in range(size)])  10.4 us
    ppermute x3, waiting for transfers between devices, to_ctx(): lax.ppermute(value, 'ctx', [(i, (i + step) % size) for i in range(size)])  8.88 us
    ppermute x3, starting transfers between devices, to_ctx(): lax.ppermute(value, 'ctx', [(i, (i + step) % size) for i in range(size)])  8.56 us
  transfers between devices with their start and end apart: 58, of which 26 were waited for; matrix products, arithmetic and copies ran while one was open for 6% of the time, Pallas kernels for 23%

profile of v3, /device:TPU:0, one launch (start us, length us, event | category | flops | bytes accessed | tf_op | source)
XLA Modules:
  0.0 343.3 jit_solution(13823232481699972908)
XLA Ops:
  9.0 5.1 %collective-permute-start = (bf16[128,1024]{1,0:T(8,128)(2,1)S(1)}, bf16[128,1024]{1,0:T(8,128)(2,1)S(1)}, u32[]{:S(2)}, u32[]{:S(2)}) collective-permute-start(bf16[128,1024]{1,0:T(8,128)(2,1)S(1)} %norm1.1.refs_0_), channel_id=1, source_target_pairs={{4,0},{8,4},{12,8},{0,12},{5,1},{9,5},{13,9},{1,13},{6,2},{10,6},{... | collective-permute-start | bytes 786440 | tf_op jit(solution)/shard_map/ppermute | solution.py:65
  20.7 3.7 %fusion = (f32[2048,64]{1,0:T(8,128)S(1)}, f32[2048,64]{1,0:T(8,128)S(1)}, f32[2048,64]{1,0:T(8,128)S(1)}) fusion(f32[64]{0:T(128)S(1)} %multiply_power_fusion, f32[2048]{0:T(1024)S(1)} %bitcast.92), kind=kLoop, calls=%fused_computation.7 | loop fusion | flops 262144 | bytes 1581312 | tf_op jit(solution)/shard_map/neg | solution.py:629
  28.8 4.6 %own_rows.1 = (bf16[512,512]{1,0:T(8,128)(2,1)}, f32[512,512]{1,0:T(8,128)}, bf16[512,256]{1,0:T(8,128)(2,1)S(1)}, bf16[512,256]{1,0:T(8,128)(2,1)S(1)}, f32[512,256]{1,0:T(8,128)}, /*index=5*/bf16[512,1024]{1,0:T(8,128)(2,1)}) custom-call(bf16[128,1024]{1,0:T(8,128)(2,1)S(1)} %norm1.1.refs_0_, bf16[128,1024]{1,0:T(8,128)(2,1)S(1)} %collective-permute-done.2.refs_1_, ...), custom_call_target="tpu_custom_call" | custom-call | tf_op jit(solution)/shard_map/own_rows/pallas_call | solution.py:35
  36.2 10.4 %collective-permute-done.8 = bf16[128,1024]{1,0:T(8,128)(2,1)S(1)} collective-permute-done((bf16[128,1024]{1,0:T(8,128)(2,1)S(1)}, bf16[128,1024]{1,0:T(8,128)(2,1)S(1)}, u32[]{:S(2)}, u32[]{:S(2)}) %collective-permute-start.8) | collective-permute-done | bytes 262176 | tf_op jit(solution)/shard_map/ppermute | solution.py:65
  48.5 6.5 %collective-permute-done.11.refs_3_ = bf16[1,128,1024]{2,1,0:T(8,128)(2,1)S(1)} collective-permute-done((bf16[1,128,1024]{2,1,0:T(8,128)(2,1)S(1)}, bf16[1,128,1024]{2,1,0:T(8,128)(2,1)S(1)}, u32[]{:S(2)}, u32[]{:S(2)}) %collective-permute-start.11) | collective-permute-done | bytes 262176 | tf_op jit(solution)/shard_map/ppermute | solution.py:54
  60.2 12.8 %collective-permute-done.5.refs_1_ = bf16[2,128,1024]{2,1,0:T(8,128)(2,1)S(1)} collective-permute-done((bf16[2,128,1024]{2,1,0:T(8,128)(2,1)S(1)}, bf16[2,128,1024]{2,1,0:T(8,128)(2,1)S(1)}, u32[]{:S(2)}, u32[]{:S(2)}) %collective-permute-start.5) | collective-permute-done | bytes 524320 | tf_op jit(solution)/shard_map/ppermute | solution.py:54
  74.5 5.5 %remote_rows.2 = (bf16[1024,256]{1,0:T(8,128)(2,1)S(1)}, bf16[1024,256]{1,0:T(8,128)(2,1)S(1)}, f32[1024,256]{1,0:T(8,128)}, bf16[1024,1024]{1,0:T(8,128)(2,1)}) custom-call(bf16[2,128,1024]{2,1,0:T(8,128)(2,1)S(1)} %pad_maximum_fusion.2.refs_0_, bf16[2,128,1024]{2,1,0:T(8,128)(2,1)} %copy-done.45, bf16[2,128,1024]{2,1,0:T(8,128)(2,1)} %collective-permute-done.6.refs_2_, ...), custom_call_target="tpu_custom_call" | custom-call | tf_op jit(solution)/shard_map/remote_rows/pallas_call | solution.py:35
  81.6 3.8 %remote_rows.3 = (bf16[512,256]{1,0:T(8,128)(2,1)S(1)}, bf16[512,256]{1,0:T(8,128)(2,1)S(1)}, f32[512,256]{1,0:T(8,128)}, bf16[512,1024]{1,0:T(8,128)(2,1)}) custom-call(bf16[1,128,1024]{2,1,0:T(8,128)(2,1)S(1)} %bitcast.70, bf16[1,128,1024]{2,1,0:T(8,128)(2,1)S(1)} %collective-permute-done.9.refs_1_, ...), custom_call_target="tpu_custom_call" | custom-call | tf_op jit(solution)/shard_map/remote_rows/pallas_call | solution.py:35
  85.4 9.8 %attend.1 = (f32[512,512]{1,0:T(8,128)}, bf16[512,512]{1,0:T(8,128)(2,1)}, f32[2,2,512]{2,1,0:T(2,128)S(1)}, f32[128,1024]{1,0:T(8,128)}, bf16[128,1024]{1,0:T(8...) custom-call(s32[8]{0:T(128)S(1)} %select_reduce_fusion.1.refs_0_, ...), custom_call_target="tpu_custom_call" | custom-call | tf_op jit(solution)/shard_map/attend/pallas_call | solution.py:35
  98.8 2.9 collective-permute-done.12.refs_0_
  101.7 3.2 collective-permute-done.13.refs_1_
  112.4 2.9 collective-permute-done.15.refs_2_
  119.1 10.8 %feed.1 = (bf16[512,1024]{1,0:T(8,128)(2,1)}, bf16[512,1024]{1,0:T(8,128)(2,1)}, bf16[512,768]{1,0:T(8,128)(2,1)}, bf16[512,768]{1,0:T(8,128)(2,1)}, bf16[512,76...) custom-call(s32[4]{0:T(128)S(1)} %iota_xor_fusion.refs_0_, ...), custom_call_target="tpu_custom_call" | custom-call | tf_op jit(solution)/shard_map/feed/pallas_call | solution.py:35
  133.5 8.4 %feed_weights.1 = (bf16[1024,768]{1,0:T(8,128)(2,1)}, bf16[1024,768]{1,0:T(8,128)(2,1)}, bf16[768,1024]{1,0:T(8,128)(2,1)}, f32[128,1024]{1,0:T(8,128)S(1)}, bf1...) custom-call(bf16[512,1024]{1,0:T(8,128)(2,1)} %get-tuple-element.120.hidden_ref, ...), custom_call_target="tpu_custom_call" | custom-call | tf_op jit(solution)/shard_map/feed_weights/pallas_call | solution.py:35
  159.9 13.6 %attend_back.1 = (bf16[512,512]{1,0:T(8,128)(2,1)}, f32[2048,256]{1,0:T(8,128)}, f32[2048,256]{1,0:T(8,128)}, f32[128,1]{1,0:T(8,128)S(1)}) custom-call(s32[8]{0:T(128)S(1)} %select_reduce_fusion.1.refs_0_, s32[2]{0:T(128)S(1)} %slice_bitcast_fusion.8.refs_1_, s32[256,1]{1,0:T(8,128)S(1)} %copy.36.refs_2_, s32[1,512]{1,0:T(1,128)S(1)} %get-tuple-element.210.refs_3_, ...), custom_call_target="tpu_custom_call" | custom-call | tf_op jit(solution)/shard_map/attend_back/pallas_call | solution.py:35
  174.8 13.0 %weights.1 = (bf16[2048,256]{1,0:T(8,128)(2,1)}, bf16[2048,256]{1,0:T(8,128)(2,1)}, bf16[512,1024]{1,0:T(8,128)(2,1)}, bf16[512,1024]{1,0:T(8,128)(2,1)}, f32[1024,1]{1,0:T(8,128)S(1)}, /*index=5*/f32[1,128]{1,0:T(1,128)S(1)}) custom-call(s32[1]{0:T(128)} %bitcast.18.core_ref.refs_0_, bf16[512,512]{1,0:T(8,128)(2,1)S(1)} %copy-done.6, ...), custom_call_target="tpu_custom_call" | custom-call | tf_op jit(solution)/shard_map/weights/pallas_call | solution.py:35
  187.9 2.9 collective-permute-done.44.got_ref
  197.4 3.8 %hidden_back.3 = (f32[1,128,1024]{2,1,0:T(8,128)S(1)}, bf16[1,128,1024]{2,1,0:T(8,128)(2,1)S(1)}, bf16[1,128,1024]{2,1,0:T(8,128)(2,1)}, bf16[1,128,1024]{2,1,0:T(8,128)(2,1)}) custom-call(bf16[512,512]{1,0:T(8,128)(2,1)S(1)} %copy-done.7, bf16[1024,512]{1,0:T(8,128)(2,1)} %refs_1_.1, bf16[2048,256]{1,0:T(8,128)(2,1)} %get-tuple-element.158.refs_2_.refs_0_, ...), custom_call_target="tpu_custom_call" | custom-call | tf_op jit(solution)/shard_map/hidden_back/pallas_call | solution.py:35
  205.5 5.6 %collective-permute-done.40 = f32[2304]{0:T(1024)S(1)} collective-permute-done((f32[2304]{0:T(1024)S(1)}, f32[2304]{0:T(1024)S(1)}, u32[]{:S(2)}, u32[]{:S(2)}) %collective-permute-start.40) | collective-permute-done | bytes 9248 | tf_op jit(solution)/shard_map/ppermute | solution.py:54
  216.3 3.2 collective-permute-done.42
  223.5 3.7 %hidden_back.5 = (f32[2,128,1024]{2,1,0:T(8,128)}, bf16[2,128,1024]{2,1,0:T(8,128)(2,1)}, bf16[2,128,1024]{2,1,0:T(8,128)(2,1)S(1)}, bf16[2,128,1024]{2,1,0:T(8,128)(2,1)S(1)}) custom-call(bf16[2048,256]{1,0:T(8,128)(2,1)} %get-tuple-element.158.refs_2_.refs_0_, bf16[2048,256]{1,0:T(8,128)(2,1)} %get-tuple-element.159.refs_3_.refs_1_, ...), custom_call_target="tpu_custom_call" | custom-call | tf_op jit(solution)/shard_map/hidden_back/pallas_call | solution.py:35
  229.5 25.9 %all-reduce.3.cloned.1.call-done = (bf16[1024,768]{1,0:T(8,128)(2,1)}, bf16[1024,768]{1,0:T(8,128)(2,1)}, bf16[768,1024]{1,0:T(8,128)(2,1)}) async-done(((bf16[1024,768]{1,0:T(8,128)(2,1)}, bf16[1024,768]{1,0:T(8,128)(2,1)}, bf16[768,1024]{1,0:T(8,128)(2,1)}), (bf16[1024,768]{1,0:T(8,128)(2,1)}, bf16[1024,768]{1,0:T(8,128)(2,1)}, bf16[768,1024]{1,0:T(8,128)(2,1)})) %all-reduce.3.cloned.1.call-update) | async-done | bytes 4718608 | tf_op jit(solution)/shard_map/psum | solution.py:786
  265.4 11.4 %collective-permute-done.51.refs_1_ = bf16[128,1024]{1,0:T(8,128)(2,1)S(1)} collective-permute-done((bf16[128,1024]{1,0:T(8,128)(2,1)S(1)}, bf16[128,1024]{1,0:T(8,128)(2,1)S(1)}, u32[]{:S(2)}, u32[]{:S(2)}) %collective-permute-start.51) | collective-permute-done | bytes 262176 | tf_op jit(solution)/shard_map/ppermute | solution.py:54
  279.9 3.5 %collective-permute-done.35 = bf16[2,128,1024]{2,1,0:T(8,128)(2,1)} collective-permute-done((bf16[2,128,1024]{2,1,0:T(8,128)(2,1)}, bf16[2,128,1024]{2,1,0:T(8,128)(2,1)}, u32[]{:S(2)}, u32[]{:S(2)}) %collective-permute-start.35) | collective-permute-done | bytes 524320 | tf_op jit(solution)/shard_map/ppermute | solution.py:54
  288.9 5.5 %collective-permute-start.33 = (bf16[128,1024]{1,0:T(8,128)(2,1)}, bf16[128,1024]{1,0:T(8,128)(2,1)}, u32[]{:S(2)}, u32[]{:S(2)}) collective-permute-start(bf16[128,1024]{1,0:T(8,128)(2,1)} %sum_parts.7), channel_id=1, source_target_pairs={{0,8},{4,12},{8,0},{12,4},{1,9},{5,13},{9,1},{13,5},{2,10},{6,14},... | collective-permute-start | bytes 786440 | tf_op jit(solution)/shard_map/ppermute | solution.py:70
  294.5 3.5 %collective-permute-done.43 = f32[2304]{0:T(1024)S(1)} collective-permute-done((f32[2304]{0:T(1024)S(1)}, f32[2304]{0:T(1024)S(1)}, u32[]{:S(2)}, u32[]{:S(2)}) %collective-permute-start.43) | collective-permute-done | bytes 9248 | tf_op jit(solution)/shard_map/ppermute | solution.py:54
  298.1 3.0 collective-permute-start.37
  307.4 5.6 %collective-permute-done.33.refs_4_ = bf16[128,1024]{1,0:T(8,128)(2,1)} collective-permute-done((bf16[128,1024]{1,0:T(8,128)(2,1)}, bf16[128,1024]{1,0:T(8,128)(2,1)}, u32[]{:S(2)}, u32[]{:S(2)}) %collective-permute-start.33) | collective-permute-done | bytes 262176 | tf_op jit(solution)/shard_map/ppermute | solution.py:70
  312.9 4.3 %collective-permute-done.53.refs_6_ = bf16[128,1024]{1,0:T(8,128)(2,1)} collective-permute-done((bf16[128,1024]{1,0:T(8,128)(2,1)S(1)}, bf16[128,1024]{1,0:T(8,128)(2,1)}, u32[]{:S(2)}, u32[]{:S(2)}) %collective-permute-start.53) | collective-permute-done | bytes 262176 | tf_op jit(solution)/shard_map/ppermute | solution.py:54
  318.4 3.3 collective-permute-done.38.refs_6_
  321.7 2.8 input_back.1
  332.1 4.4 %spread.1 = (f32[1024,512]{1,0:T(8,128)}, f32[1024,256]{1,0:T(8,128)}, f32[1024,256]{1,0:T(8,128)}, f32[512,1024]{1,0:T(8,128)}) custom-call(s32[4]{0:T(128)S(1)} %pad_add_fusion.1.refs_0_, bf16[256,1024]{1,0:T(8,128)(2,1)S(1)} %sum_parts.11.refs_1_, bf16[256,1024]{1,0:T(8,128)(2,1)} %collective-permute-done.47.refs_2_, bf16[256,1024]{1,0:T(8,128)(2,1)} %copy-done.42, ...), custom_call_target="tpu_custom_call" | custom-call | tf_op jit(solution)/shard_map/spread/pallas_call | solution.py:35
  (267 shorter events, 119.4 us)
Async XLA Ops:
  7.2 111.9 %all-gather.2.cloned.1.call-start = ((), (), s32[]{:S(2)}) async-start(), calls=%async_computation | async-start | bytes 1310720 | tf_op jit(solution)/shard_map/all_gather | solution.py:750
  9.0 18.1 %collective-permute-start = (bf16[128,1024]{1,0:T(8,128)(2,1)S(1)}, bf16[128,1024]{1,0:T(8,128)(2,1)S(1)}, u32[]{:S(2)}, u32[]{:S(2)}) collective-permute-start(bf16[128,1024]{1,0:T(8,128)(2,1)S(1)} %norm1.1.refs_0_), channel_id=1, source_target_pairs={{4,0},{8,4},{12,8},{0,12},{5,1},{9,5},{13,9},{1,13},{6,2},{10,6},{... | collective-permute-start | bytes 786440 | tf_op jit(solution)/shard_map/ppermute | solution.py:65
  34.2 14.3 %collective-permute-start.7 = (bf16[2,128,1024]{2,1,0:T(8,128)(2,1)S(1)}, bf16[2,128,1024]{2,1,0:T(8,128)(2,1)S(1)}, u32[]{:S(2)}, u32[]{:S(2)}) collective-permute-start(bf16[2,128,1024]{2,1,0:T(8,128)(2,1)S(1)} %pad_maximum_fusion.2.refs_0_), channel_id=1, source_target_pairs={{0,3},{1,2},{2,1},{3,0},{4,7},{5,6},{6,5},{7,4},{8,11},{9,10},{10,... | collective-permute-start | bytes 1572872 | tf_op jit(solution)/shard_map/ppermute | solution.py:54
  55.0 200.4 %all-reduce.3.cloned.1.call-start = ((), (), s32[]{:S(2)}) async-start(), calls=%async_computation.1 | async-start | bytes 9437184 | tf_op jit(solution)/shard_map/psum | solution.py:786
  55.3 17.7 %collective-permute-start.5 = (bf16[2,128,1024]{2,1,0:T(8,128)(2,1)S(1)}, bf16[2,128,1024]{2,1,0:T(8,128)(2,1)S(1)}, u32[]{:S(2)}, u32[]{:S(2)}) collective-permute-start(bf16[2,128,1024]{2,1,0:T(8,128)(2,1)S(1)} %pad_maximum_fusion.2.refs_0_), channel_id=1, source_target_pairs={{0,1},{1,0},{2,3},{3,2},{4,5},{5,4},{6,7},{7,6},{8,9},{9,8},{10,11... | collective-permute-start | bytes 1572872 | tf_op jit(solution)/shard_map/ppermute | solution.py:54
  56.8 17.7 %collective-permute-start.6 = (bf16[2,128,1024]{2,1,0:T(8,128)(2,1)S(1)}, bf16[2,128,1024]{2,1,0:T(8,128)(2,1)}, u32[]{:S(2)}, u32[]{:S(2)}) collective-permute-start(bf16[2,128,1024]{2,1,0:T(8,128)(2,1)S(1)} %pad_maximum_fusion.2.refs_0_), channel_id=1, source_target_pairs={{0,2},{1,3},{2,0},{3,1},{4,6},{5,7},{6,4},{7,5},{8,10},{9,11},{10,... | collective-permute-start | bytes 1572872 | tf_op jit(solution)/shard_map/ppermute | solution.py:54
  58.0 23.6 %collective-permute-start.9 = (bf16[1,128,1024]{2,1,0:T(8,128)(2,1)S(1)}, bf16[1,128,1024]{2,1,0:T(8,128)(2,1)S(1)}, u32[]{:S(2)}, u32[]{:S(2)}) collective-permute-start(bf16[1,128,1024]{2,1,0:T(8,128)(2,1)S(1)} %bitcast.68), channel_id=1, source_target_pairs={{0,1},{1,0},{2,3},{3,2},{4,5},{5,4},{6,7},{7,6},{8,9},{9,8},{10,11... | collective-permute-start | bytes 786440 | tf_op jit(solution)/shard_map/ppermute | solution.py:54
  58.6 23.1 %collective-permute-start.10 = (bf16[1,128,1024]{2,1,0:T(8,128)(2,1)S(1)}, bf16[1,128,1024]{2,1,0:T(8,128)(2,1)S(1)}, u32[]{:S(2)}, u32[]{:S(2)}) collective-permute-start(bf16[1,128,1024]{2,1,0:T(8,128)(2,1)S(1)} %bitcast.69), channel_id=1, source_target_pairs={{0,2},{1,3},{2,0},{3,1},{4,6},{5,7},{6,4},{7,5},{8,10},{9,11},{10,... | collective-permute-start | bytes 786440 | tf_op jit(solution)/shard_map/ppermute | solution.py:54
  149.5 23.9 %collective-permute-start.24 = (bf16[128,1024]{1,0:T(8,128)(2,1)}, bf16[128,1024]{1,0:T(8,128)(2,1)S(1)}, u32[]{:S(2)}, u32[]{:S(2)}) collective-permute-start(bf16[128,1024]{1,0:T(8,128)(2,1)} %get-tuple-element.142), channel_id=1, source_target_pairs={{0,1},{1,0},{2,3},{3,2},{4,5},{5,4},{6,7},{7,6},{8,9},{9,8},{10,11... | collective-permute-start | bytes 786440 | tf_op jit(solution)/shard_map/ppermute | solution.py:54
  150.5 23.0 %collective-permute-start.25 = (bf16[128,1024]{1,0:T(8,128)(2,1)}, bf16[128,1024]{1,0:T(8,128)(2,1)S(1)}, u32[]{:S(2)}, u32[]{:S(2)}) collective-permute-start(bf16[128,1024]{1,0:T(8,128)(2,1)} %get-tuple-element.143), channel_id=1, source_target_pairs={{0,2},{1,3},{2,0},{3,1},{4,6},{5,7},{6,4},{7,5},{8,10},{9,11},{10,... | collective-permute-start | bytes 786440 | tf_op jit(solution)/shard_map/ppermute | solution.py:54
  153.5 20.0 %collective-permute-start.26 = (bf16[128,1024]{1,0:T(8,128)(2,1)}, bf16[128,1024]{1,0:T(8,128)(2,1)S(1)}, u32[]{:S(2)}, u32[]{:S(2)}) collective-permute-start(bf16[128,1024]{1,0:T(8,128)(2,1)} %get-tuple-element.144), channel_id=1, source_target_pairs={{0,3},{1,2},{2,1},{3,0},{4,7},{5,6},{6,5},{7,4},{8,11},{9,10},{10,... | collective-permute-start | bytes 786440 | tf_op jit(solution)/shard_map/ppermute | solution.py:54
  195.2 32.0 %collective-permute-start.45 = (bf16[256,1024]{1,0:T(8,128)(2,1)}, bf16[256,1024]{1,0:T(8,128)(2,1)S(1)}, u32[]{:S(2)}, u32[]{:S(2)}) collective-permute-start(bf16[256,1024]{1,0:T(8,128)(2,1)} %get-tuple-element.179), channel_id=1, source_target_pairs={{0,4},{4,0},{8,12},{12,8},{1,5},{5,1},{9,13},{13,9},{2,6},{6,2},{1... | collective-permute-start | bytes 1572872 | tf_op jit(solution)/shard_map/ppermute | solution.py:54
  197.4 59.6 %collective-permute-start.50 = (bf16[256,1024]{1,0:T(8,128)(2,1)}, bf16[256,1024]{1,0:T(8,128)(2,1)}, u32[]{:S(2)}, u32[]{:S(2)}) collective-permute-start(bf16[256,1024]{1,0:T(8,128)(2,1)} %get-tuple-element.136), channel_id=1, source_target_pairs={{0,16},{16,0},{1,17},{17,1},{2,18},{18,2},{3,19},{19,3},{4,20},{20... | collective-permute-start | bytes 1572872 | tf_op jit(solution)/shard_map/ppermute | solution.py:54
  202.0 19.0 %collective-permute-start.29 = (bf16[1,128,1024]{2,1,0:T(8,128)(2,1)}, bf16[1,128,1024]{2,1,0:T(8,128)(2,1)S(1)}, u32[]{:S(2)}, u32[]{:S(2)}) collective-permute-start(bf16[1,128,1024]{2,1,0:T(8,128)(2,1)} %get-tuple-element.163), channel_id=1, source_target_pairs={{0,3},{1,2},{2,1},{3,0},{4,7},{5,6},{6,5},{7,4},{8,11},{9,10},{10,... | collective-permute-start | bytes 786440 | tf_op jit(solution)/shard_map/ppermute | solution.py:54
  215.4 40.0 %collective-permute-start.30 = (bf16[1,128,1024]{2,1,0:T(8,128)(2,1)}, bf16[1,128,1024]{2,1,0:T(8,128)(2,1)S(1)}, u32[]{:S(2)}, u32[]{:S(2)}) collective-permute-start(bf16[1,128,1024]{2,1,0:T(8,128)(2,1)} %get-tuple-element.165), channel_id=1, source_target_pairs={{0,1},{1,0},{2,3},{3,2},{4,5},{5,4},{6,7},{7,6},{8,9},{9,8},{10,11... | collective-permute-start | bytes 786440 | tf_op jit(solution)/shard_map/ppermute | solution.py:54
  219.4 40.1 %collective-permute-start.31 = (bf16[1,128,1024]{2,1,0:T(8,128)(2,1)}, bf16[1,128,1024]{2,1,0:T(8,128)(2,1)S(1)}, u32[]{:S(2)}, u32[]{:S(2)}) collective-permute-start(bf16[1,128,1024]{2,1,0:T(8,128)(2,1)} %get-tuple-element.166), channel_id=1, source_target_pairs={{0,2},{1,3},{2,0},{3,1},{4,6},{5,7},{6,4},{7,5},{8,10},{9,11},{10,... | collective-permute-start | bytes 786440 | tf_op jit(solution)/shard_map/ppermute | solution.py:54
  221.7 39.5 %collective-permute-start.32 = (bf16[1,128,1024]{2,1,0:T(8,128)(2,1)}, bf16[1,128,1024]{2,1,0:T(8,128)(2,1)S(1)}, u32[]{:S(2)}, u32[]{:S(2)}) collective-permute-start(bf16[1,128,1024]{2,1,0:T(8,128)(2,1)} %get-tuple-element.167), channel_id=1, source_target_pairs={{0,3},{1,2},{2,1},{3,0},{4,7},{5,6},{6,5},{7,4},{8,11},{9,10},{10,... | collective-permute-start | bytes 786440 | tf_op jit(solution)/shard_map/ppermute | solution.py:54
  227.2 36.4 %collective-permute-start.34 = (bf16[2,128,1024]{2,1,0:T(8,128)(2,1)}, bf16[2,128,1024]{2,1,0:T(8,128)(2,1)}, u32[]{:S(2)}, u32[]{:S(2)}) collective-permute-start(bf16[2,128,1024]{2,1,0:T(8,128)(2,1)} %get-tuple-element.169), channel_id=1, source_target_pairs={{0,1},{1,0},{2,3},{3,2},{4,5},{5,4},{6,7},{7,6},{8,9},{9,8},{10,11... | collective-permute-start | bytes 1572872 | tf_op jit(solution)/shard_map/ppermute | solution.py:54
  255.4 22.4 %collective-permute-start.46 = (bf16[256,1024]{1,0:T(8,128)(2,1)S(1)}, bf16[256,1024]{1,0:T(8,128)(2,1)S(1)}, u32[]{:S(2)}, u32[]{:S(2)}) collective-permute-start(bf16[256,1024]{1,0:T(8,128)(2,1)S(1)} %sum_parts.10.refs_0_), channel_id=1, source_target_pairs={{0,12},{4,8},{8,4},{12,0},{1,13},{5,9},{9,5},{13,1},{2,14},{6,10},... | collective-permute-start | bytes 1572872 | tf_op jit(solution)/shard_map/ppermute | solution.py:54
  257.0 26.4 %collective-permute-start.35 = (bf16[2,128,1024]{2,1,0:T(8,128)(2,1)}, bf16[2,128,1024]{2,1,0:T(8,128)(2,1)}, u32[]{:S(2)}, u32[]{:S(2)}) collective-permute-start(bf16[2,128,1024]{2,1,0:T(8,128)(2,1)} %copy-done.34), channel_id=1, source_target_pairs={{0,2},{1,3},{2,0},{3,1},{4,6},{5,7},{6,4},{7,5},{8,10},{9,11},{10,... | collective-permute-start | bytes 1572872 | tf_op jit(solution)/shard_map/ppermute | solution.py:54
  259.5 25.1 %collective-permute-start.36 = (bf16[2,128,1024]{2,1,0:T(8,128)(2,1)}, bf16[2,128,1024]{2,1,0:T(8,128)(2,1)S(1)}, u32[]{:S(2)}, u32[]{:S(2)}) collective-permute-start(bf16[2,128,1024]{2,1,0:T(8,128)(2,1)} %copy-done.33), channel_id=1, source_target_pairs={{0,3},{1,2},{2,1},{3,0},{4,7},{5,6},{6,5},{7,4},{8,11},{9,10},{10,... | collective-permute-start | bytes 1572872 | tf_op jit(solution)/shard_map/ppermute | solution.py:54
  261.9 14.9 %collective-permute-start.51 = (bf16[128,1024]{1,0:T(8,128)(2,1)S(1)}, bf16[128,1024]{1,0:T(8,128)(2,1)S(1)}, u32[]{:S(2)}, u32[]{:S(2)}) collective-permute-start(bf16[128,1024]{1,0:T(8,128)(2,1)S(1)} %get-tuple-element.186), channel_id=1, source_target_pairs={{0,4},{4,0},{8,12},{12,8},{1,5},{5,1},{9,13},{13,9},{2,6},{6,2},{1... | collective-permute-start | bytes 786440 | tf_op jit(solution)/shard_map/ppermute | solution.py:54
  263.6 37.4 %collective-permute-start.27 = (bf16[1,128,1024]{2,1,0:T(8,128)(2,1)S(1)}, bf16[1,128,1024]{2,1,0:T(8,128)(2,1)S(1)}, u32[]{:S(2)}, u32[]{:S(2)}) collective-permute-start(bf16[1,128,1024]{2,1,0:T(8,128)(2,1)S(1)} %copy-done.36), channel_id=1, source_target_pairs={{0,1},{1,0},{2,3},{3,2},{4,5},{5,4},{6,7},{7,6},{8,9},{9,8},{10,11... | collective-permute-start | bytes 786440 | tf_op jit(solution)/shard_map/ppermute | solution.py:54
  276.8 26.2 %collective-permute-start.28 = (bf16[1,128,1024]{2,1,0:T(8,128)(2,1)}, bf16[1,128,1024]{2,1,0:T(8,128)(2,1)}, u32[]{:S(2)}, u32[]{:S(2)}) collective-permute-start(bf16[1,128,1024]{2,1,0:T(8,128)(2,1)} %get-tuple-element.162), channel_id=1, source_target_pairs={{0,2},{1,3},{2,0},{3,1},{4,6},{5,7},{6,4},{7,5},{8,10},{9,11},{10,... | collective-permute-start | bytes 786440 | tf_op jit(solution)/shard_map/ppermute | solution.py:54
  283.4 19.7 %collective-permute-start.47 = (bf16[256,1024]{1,0:T(8,128)(2,1)S(1)}, bf16[256,1024]{1,0:T(8,128)(2,1)}, u32[]{:S(2)}, u32[]{:S(2)}) collective-permute-start(bf16[256,1024]{1,0:T(8,128)(2,1)S(1)} %sum_parts.11.refs_1_), channel_id=1, source_target_pairs={{0,4},{4,0},{8,12},{12,8},{1,5},{5,1},{9,13},{13,9},{2,6},{6,2},{1... | collective-permute-start | bytes 1572872 | tf_op jit(solution)/shard_map/ppermute | solution.py:54
  284.6 13.4 %collective-permute-start.43 = (f32[2304]{0:T(1024)S(1)}, f32[2304]{0:T(1024)S(1)}, u32[]{:S(2)}, u32[]{:S(2)}) collective-permute-start(f32[2304]{0:T(1024)S(1)} %add.117), channel_id=1, source_target_pairs={{0,8},{4,12},{8,0},{12,4},{1,9},{5,13},{9,1},{13,5},{2,10},{6,14},... | collective-permute-start | bytes 27656 | tf_op jit(solution)/shard_map/ppermute | solution.py:54
  288.9 24.0 %collective-permute-start.33 = (bf16[128,1024]{1,0:T(8,128)(2,1)}, bf16[128,1024]{1,0:T(8,128)(2,1)}, u32[]{:S(2)}, u32[]{:S(2)}) collective-permute-start(bf16[128,1024]{1,0:T(8,128)(2,1)} %sum_parts.7), channel_id=1, source_target_pairs={{0,8},{4,12},{8,0},{12,4},{1,9},{5,13},{9,1},{13,5},{2,10},{6,14},... | collective-permute-start | bytes 786440 | tf_op jit(solution)/shard_map/ppermute | solution.py:70
  298.1 14.9 %collective-permute-start.37 = (bf16[128,1024]{1,0:T(8,128)(2,1)}, bf16[128,1024]{1,0:T(8,128)(2,1)}, u32[]{:S(2)}, u32[]{:S(2)}) collective-permute-start(bf16[128,1024]{1,0:T(8,128)(2,1)} %sum_parts.8), channel_id=1, source_target_pairs={{0,4},{4,8},{8,12},{12,0},{1,5},{5,9},{9,13},{13,1},{2,6},{6,10},{... | collective-permute-start | bytes 786440 | tf_op jit(solution)/shard_map/ppermute | solution.py:70
  301.8 15.5 %collective-permute-start.53 = (bf16[128,1024]{1,0:T(8,128)(2,1)S(1)}, bf16[128,1024]{1,0:T(8,128)(2,1)}, u32[]{:S(2)}, u32[]{:S(2)}) collective-permute-start(bf16[128,1024]{1,0:T(8,128)(2,1)S(1)} %sum_parts.13.refs_5_), channel_id=1, source_target_pairs={{0,4},{4,0},{8,12},{12,8},{1,5},{5,1},{9,13},{13,9},{2,6},{6,2},{1... | collective-permute-start | bytes 786440 | tf_op jit(solution)/shard_map/ppermute | solution.py:54
  303.0 27.5 %collective-permute-start.48 = (bf16[256,1024]{1,0:T(8,128)(2,1)S(1)}, bf16[256,1024]{1,0:T(8,128)(2,1)S(1)}, u32[]{:S(2)}, u32[]{:S(2)}) collective-permute-start(bf16[256,1024]{1,0:T(8,128)(2,1)S(1)} %sum_parts.11.refs_1_), channel_id=1, source_target_pairs={{0,16},{16,0},{1,17},{17,1},{2,18},{18,2},{3,19},{19,3},{4,20},{20... | collective-permute-start | bytes 1572872 | tf_op jit(solution)/shard_map/ppermute | solution.py:54
  303.1 27.4 %collective-permute-start.49 = (bf16[256,1024]{1,0:T(8,128)(2,1)}, bf16[256,1024]{1,0:T(8,128)(2,1)S(1)}, u32[]{:S(2)}, u32[]{:S(2)}) collective-permute-start(bf16[256,1024]{1,0:T(8,128)(2,1)} %collective-permute-done.47.refs_2_), channel_id=1, source_target_pairs={{0,16},{16,0},{1,17},{17,1},{2,18},{18,2},{3,19},{19,3},{4,20},{20... | collective-permute-start | bytes 1572872 | tf_op jit(solution)/shard_map/ppermute | solution.py:54
  312.9 17.5 %collective-permute-start.54 = (bf16[128,1024]{1,0:T(8,128)(2,1)S(1)}, bf16[128,1024]{1,0:T(8,128)(2,1)S(1)}, u32[]{:S(2)}, u32[]{:S(2)}) collective-permute-start(bf16[128,1024]{1,0:T(8,128)(2,1)S(1)} %sum_parts.13.refs_5_), channel_id=1, source_target_pairs={{0,16},{16,0},{1,17},{17,1},{2,18},{18,2},{3,19},{19,3},{4,20},{20... | collective-permute-start | bytes 786440 | tf_op jit(solution)/shard_map/ppermute | solution.py:54
  (78 other events, 650.1 us)
Sparse Core Ops, SparseCore 0:
  55.2 28.9 all-gather.1
  142.8 112.5 all-reduce.2

commit v4 on v3

--- a/solution.py
+++ b/solution.py
@@ -538,8 +538,11 @@
     if after:
         pair, *_ = lax.optimization_barrier((pair, *after))
     total = sum_parts([pair, swap(pair, "ctx", 3)], BF)
-    chunks = [total, swap(total, "ctx", 1)]
-    return chunks + [swap(c, "dp", 1) for c in chunks]
+    far = swap(total, "ctx", 1)
+    near = total
+    if after:
+        near, *_ = lax.optimization_barrier((total, *[a.astype(F32) for a in after[:3]]))
+    return [total, far, swap(near, "dp", 1), swap(far, "dp", 1)]
 
 
 def slot_blocks(group, rows, width):

time: 344 us -> 338 us (0.983)
  local copies, waits for them, and re-layouts: 23.1 us -> 19.4 us
    ppermute x3, waiting for transfers between devices: 8.88 us -> 4.55 us  [to_ctx(): lax.ppermute(value, 'ctx', [(i, (i + step) % size) for i in range(size)])]
    unnamed x105 -> x99, local copies, waits for them, and re-layouts: 18.3 us -> 14.6 us
  transfers between devices with their start and end apart: 58 -> 58, of which waited for: 26 -> 25; matrix products, arithmetic and copies ran while one was open for 6% -> 7% of each run, Pallas kernels for 23% -> 23%
where the time goes in v4:
time: 338 us; the launch traced here: 337 us
  waiting for transfers between devices  118 us (35%)
  Pallas kernels  98.7 us (29%)
  starting transfers between devices  67.8 us (20%)
  local copies, waits for them, and re-layouts  19.4 us (6%)
  other arithmetic  18.4 us (5%)
  between operations  14.7 us (4%)
    pallas_call x27, Pallas kernels, call(): pl.pallas_call(kernel, grid=grid, in_specs=[in_specs.get(i, whole_spec(a)...  98.7 us
    ppermute x50, waiting for transfers between devices, swap(): return lax.ppermute(value, axis, [(i, i ^ step) for i in range(size)])  77.3 us
    ppermute x50, starting transfers between devices, swap(): return lax.ppermute(value, axis, [(i, i ^ step) for i in range(size)])  53.1 us
    psum x1, waiting for transfers between devices, on_device(): dg, du, dd = lax.psum((dg, du, dd), ('dp', 'ctx'))  25.9 us
    unnamed x99, local copies, waits for them, and re-layouts  14.6 us
    ppermute x3, waiting for transfers between devices, from_ctx(): lax.ppermute(value, 'ctx', [((i + step) % size, i) for i in range(size)])  10.4 us
    ppermute x3, starting transfers between devices, to_ctx(): lax.ppermute(value, 'ctx', [(i, (i + step) % size) for i in range(size)])  8.57 us
    convert_element_type x3, other arithmetic, sum_over_ctx(): a.astype(F32)  7.38 us
  transfers between devices with their start and end apart: 58, of which 25 were waited for; matrix products, arithmetic and copies ran while one was open for 7% of the time, Pallas kernels for 23%

profile of v4, /device:TPU:0, one launch (start us, length us, event | category | flops | bytes accessed | tf_op | source)
XLA Modules:
  0.0 337.2 jit_solution(1489446465270413800)
XLA Ops:
  9.0 5.1 %collective-permute-start = (bf16[128,1024]{1,0:T(8,128)(2,1)S(1)}, bf16[128,1024]{1,0:T(8,128)(2,1)S(1)}, u32[]{:S(2)}, u32[]{:S(2)}) collective-permute-start(bf16[128,1024]{1,0:T(8,128)(2,1)S(1)} %norm1.1.refs_0_), channel_id=1, source_target_pairs={{4,0},{8,4},{12,8},{0,12},{5,1},{9,5},{13,9},{1,13},{6,2},{10,6},{... | collective-permute-start | bytes 786440 | tf_op jit(solution)/shard_map/ppermute | solution.py:65
  20.7 3.7 %fusion = (f32[2048,64]{1,0:T(8,128)S(1)}, f32[2048,64]{1,0:T(8,128)S(1)}, f32[2048,64]{1,0:T(8,128)S(1)}) fusion(f32[64]{0:T(128)S(1)} %multiply_power_fusion, f32[2048]{0:T(1024)S(1)} %bitcast.92), kind=kLoop, calls=%fused_computation.7 | loop fusion | flops 262144 | bytes 1581312 | tf_op jit(solution)/shard_map/neg | solution.py:632
  28.8 4.6 %own_rows.1 = (bf16[512,512]{1,0:T(8,128)(2,1)}, f32[512,512]{1,0:T(8,128)}, bf16[512,256]{1,0:T(8,128)(2,1)S(1)}, bf16[512,256]{1,0:T(8,128)(2,1)S(1)}, f32[512,256]{1,0:T(8,128)}, /*index=5*/bf16[512,1024]{1,0:T(8,128)(2,1)}) custom-call(bf16[128,1024]{1,0:T(8,128)(2,1)S(1)} %norm1.1.refs_0_, bf16[128,1024]{1,0:T(8,128)(2,1)S(1)} %collective-permute-done.2.refs_1_, ...), custom_call_target="tpu_custom_call" | custom-call | tf_op jit(solution)/shard_map/own_rows/pallas_call | solution.py:35
  36.2 10.4 %collective-permute-done.8 = bf16[128,1024]{1,0:T(8,128)(2,1)S(1)} collective-permute-done((bf16[128,1024]{1,0:T(8,128)(2,1)S(1)}, bf16[128,1024]{1,0:T(8,128)(2,1)S(1)}, u32[]{:S(2)}, u32[]{:S(2)}) %collective-permute-start.8) | collective-permute-done | bytes 262176 | tf_op jit(solution)/shard_map/ppermute | solution.py:65
  48.5 6.5 %collective-permute-done.11.refs_3_ = bf16[1,128,1024]{2,1,0:T(8,128)(2,1)S(1)} collective-permute-done((bf16[1,128,1024]{2,1,0:T(8,128)(2,1)S(1)}, bf16[1,128,1024]{2,1,0:T(8,128)(2,1)S(1)}, u32[]{:S(2)}, u32[]{:S(2)}) %collective-permute-start.11) | collective-permute-done | bytes 262176 | tf_op jit(solution)/shard_map/ppermute | solution.py:54
  60.2 12.8 %collective-permute-done.5.refs_1_ = bf16[2,128,1024]{2,1,0:T(8,128)(2,1)S(1)} collective-permute-done((bf16[2,128,1024]{2,1,0:T(8,128)(2,1)S(1)}, bf16[2,128,1024]{2,1,0:T(8,128)(2,1)S(1)}, u32[]{:S(2)}, u32[]{:S(2)}) %collective-permute-start.5) | collective-permute-done | bytes 524320 | tf_op jit(solution)/shard_map/ppermute | solution.py:54
  74.5 5.5 %remote_rows.2 = (bf16[1024,256]{1,0:T(8,128)(2,1)S(1)}, bf16[1024,256]{1,0:T(8,128)(2,1)S(1)}, f32[1024,256]{1,0:T(8,128)}, bf16[1024,1024]{1,0:T(8,128)(2,1)}) custom-call(bf16[2,128,1024]{2,1,0:T(8,128)(2,1)S(1)} %pad_maximum_fusion.2.refs_0_, bf16[2,128,1024]{2,1,0:T(8,128)(2,1)} %copy-done.42, bf16[2,128,1024]{2,1,0:T(8,128)(2,1)} %collective-permute-done.6.refs_2_, ...), custom_call_target="tpu_custom_call" | custom-call | tf_op jit(solution)/shard_map/remote_rows/pallas_call | solution.py:35
  81.6 3.8 %remote_rows.3 = (bf16[512,256]{1,0:T(8,128)(2,1)S(1)}, bf16[512,256]{1,0:T(8,128)(2,1)S(1)}, f32[512,256]{1,0:T(8,128)}, bf16[512,1024]{1,0:T(8,128)(2,1)}) custom-call(bf16[1,128,1024]{2,1,0:T(8,128)(2,1)S(1)} %bitcast.70, bf16[1,128,1024]{2,1,0:T(8,128)(2,1)S(1)} %collective-permute-done.9.refs_1_, ...), custom_call_target="tpu_custom_call" | custom-call | tf_op jit(solution)/shard_map/remote_rows/pallas_call | solution.py:35
  85.4 9.8 %attend.1 = (f32[512,512]{1,0:T(8,128)}, bf16[512,512]{1,0:T(8,128)(2,1)}, f32[2,2,512]{2,1,0:T(2,128)S(1)}, f32[128,1024]{1,0:T(8,128)}, bf16[128,1024]{1,0:T(8...) custom-call(s32[8]{0:T(128)S(1)} %select_reduce_fusion.1.refs_0_, ...), custom_call_target="tpu_custom_call" | custom-call | tf_op jit(solution)/shard_map/attend/pallas_call | solution.py:35
  98.8 2.9 collective-permute-done.12.refs_0_
  101.6 3.2 collective-permute-done.13.refs_1_
  112.3 2.9 collective-permute-done.15.refs_2_
  115.2 2.7 collective-permute-done.16.refs_3_
  119.1 10.8 %feed.1 = (bf16[512,1024]{1,0:T(8,128)(2,1)}, bf16[512,1024]{1,0:T(8,128)(2,1)}, bf16[512,768]{1,0:T(8,128)(2,1)}, bf16[512,768]{1,0:T(8,128)(2,1)}, bf16[512,76...) custom-call(s32[4]{0:T(128)S(1)} %iota_xor_fusion.refs_0_, ...), custom_call_target="tpu_custom_call" | custom-call | tf_op jit(solution)/shard_map/feed/pallas_call | solution.py:35
  133.4 8.4 %feed_weights.1 = (bf16[1024,768]{1,0:T(8,128)(2,1)}, bf16[1024,768]{1,0:T(8,128)(2,1)}, bf16[768,1024]{1,0:T(8,128)(2,1)}, f32[128,1024]{1,0:T(8,128)S(1)}, bf1...) custom-call(bf16[512,1024]{1,0:T(8,128)(2,1)} %get-tuple-element.121.hidden_ref, ...), custom_call_target="tpu_custom_call" | custom-call | tf_op jit(solution)/shard_map/feed_weights/pallas_call | solution.py:35
  159.7 13.6 %attend_back.1 = (bf16[512,512]{1,0:T(8,128)(2,1)}, f32[2048,256]{1,0:T(8,128)}, f32[2048,256]{1,0:T(8,128)}, f32[128,1]{1,0:T(8,128)S(1)}) custom-call(s32[8]{0:T(128)S(1)} %select_reduce_fusion.1.refs_0_, s32[2]{0:T(128)S(1)} %slice_bitcast_fusion.8.refs_1_, s32[256,1]{1,0:T(8,128)S(1)} %copy.36.refs_2_, s32[1,512]{1,0:T(1,128)S(1)} %get-tuple-element.212.refs_3_, ...), custom_call_target="tpu_custom_call" | custom-call | tf_op jit(solution)/shard_map/attend_back/pallas_call | solution.py:35
  174.7 13.0 %weights.1 = (bf16[2048,256]{1,0:T(8,128)(2,1)}, bf16[2048,256]{1,0:T(8,128)(2,1)}, bf16[512,1024]{1,0:T(8,128)(2,1)}, bf16[512,1024]{1,0:T(8,128)(2,1)}, f32[1024,1]{1,0:T(8,128)S(1)}, /*index=5*/f32[1,128]{1,0:T(1,128)S(1)}) custom-call(s32[1]{0:T(128)} %bitcast.18.core_ref.refs_0_, bf16[512,512]{1,0:T(8,128)(2,1)S(1)} %copy-done.6, ...), custom_call_target="tpu_custom_call" | custom-call | tf_op jit(solution)/shard_map/weights/pallas_call | solution.py:35
  187.8 2.9 collective-permute-done.44.got_ref
  197.3 3.8 %hidden_back.3 = (f32[1,128,1024]{2,1,0:T(8,128)S(1)}, bf16[1,128,1024]{2,1,0:T(8,128)(2,1)S(1)}, bf16[1,128,1024]{2,1,0:T(8,128)(2,1)}, bf16[1,128,1024]{2,1,0:T(8,128)(2,1)}) custom-call(bf16[512,512]{1,0:T(8,128)(2,1)S(1)} %copy-done.7, bf16[1024,512]{1,0:T(8,128)(2,1)} %refs_1_.1, bf16[2048,256]{1,0:T(8,128)(2,1)} %get-tuple-element.159.refs_2_.refs_0_, ...), custom_call_target="tpu_custom_call" | custom-call | tf_op jit(solution)/shard_map/hidden_back/pallas_call | solution.py:35
  205.5 5.6 %collective-permute-done.40 = f32[2304]{0:T(1024)S(1)} collective-permute-done((f32[2304]{0:T(1024)S(1)}, f32[2304]{0:T(1024)S(1)}, u32[]{:S(2)}, u32[]{:S(2)}) %collective-permute-start.40) | collective-permute-done | bytes 9248 | tf_op jit(solution)/shard_map/ppermute | solution.py:54
  216.2 3.2 collective-permute-done.42
  223.5 3.7 %hidden_back.5 = (f32[2,128,1024]{2,1,0:T(8,128)}, bf16[2,128,1024]{2,1,0:T(8,128)(2,1)}, bf16[2,128,1024]{2,1,0:T(8,128)(2,1)S(1)}, bf16[2,128,1024]{2,1,0:T(8,128)(2,1)S(1)}) custom-call(bf16[2048,256]{1,0:T(8,128)(2,1)} %get-tuple-element.159.refs_2_.refs_0_, bf16[2048,256]{1,0:T(8,128)(2,1)} %get-tuple-element.160.refs_3_.refs_1_, ...), custom_call_target="tpu_custom_call" | custom-call | tf_op jit(solution)/shard_map/hidden_back/pallas_call | solution.py:35
  229.4 25.9 %all-reduce.3.cloned.1.call-done = (bf16[1024,768]{1,0:T(8,128)(2,1)}, bf16[1024,768]{1,0:T(8,128)(2,1)}, bf16[768,1024]{1,0:T(8,128)(2,1)}) async-done(((bf16[1024,768]{1,0:T(8,128)(2,1)}, bf16[1024,768]{1,0:T(8,128)(2,1)}, bf16[768,1024]{1,0:T(8,128)(2,1)}), (bf16[1024,768]{1,0:T(8,128)(2,1)}, bf16[1024,768]{1,0:T(8,128)(2,1)}, bf16[768,1024]{1,0:T(8,128)(2,1)})) %all-reduce.3.cloned.1.call-update) | async-done | bytes 4718608 | tf_op jit(solution)/shard_map/psum | solution.py:789
  264.7 12.0 %collective-permute-done.51.refs_1_ = bf16[128,1024]{1,0:T(8,128)(2,1)S(1)} collective-permute-done((bf16[128,1024]{1,0:T(8,128)(2,1)S(1)}, bf16[128,1024]{1,0:T(8,128)(2,1)S(1)}, u32[]{:S(2)}, u32[]{:S(2)}) %collective-permute-start.51) | collective-permute-done | bytes 262176 | tf_op jit(solution)/shard_map/ppermute | solution.py:54
  279.8 3.5 %collective-permute-done.35 = bf16[2,128,1024]{2,1,0:T(8,128)(2,1)} collective-permute-done((bf16[2,128,1024]{2,1,0:T(8,128)(2,1)}, bf16[2,128,1024]{2,1,0:T(8,128)(2,1)}, u32[]{:S(2)}, u32[]{:S(2)}) %collective-permute-start.35) | collective-permute-done | bytes 524320 | tf_op jit(solution)/shard_map/ppermute | solution.py:54
  288.9 5.4 %collective-permute-start.33 = (bf16[128,1024]{1,0:T(8,128)(2,1)S(1)}, bf16[128,1024]{1,0:T(8,128)(2,1)}, u32[]{:S(2)}, u32[]{:S(2)}) collective-permute-start(bf16[128,1024]{1,0:T(8,128)(2,1)S(1)} %sum_parts.7), channel_id=1, source_target_pairs={{0,8},{4,12},{8,0},{12,4},{1,9},{5,13},{9,1},{13,5},{2,10},{6,14},... | collective-permute-start | bytes 786440 | tf_op jit(solution)/shard_map/ppermute | solution.py:70
  294.4 3.5 %collective-permute-done.43 = f32[2304]{0:T(1024)S(1)} collective-permute-done((f32[2304]{0:T(1024)S(1)}, f32[2304]{0:T(1024)S(1)}, u32[]{:S(2)}, u32[]{:S(2)}) %collective-permute-start.43) | collective-permute-done | bytes 9248 | tf_op jit(solution)/shard_map/ppermute | solution.py:54
  297.9 3.1 collective-permute-start.37
  302.1 3.4 %convert_element_type.37 = f32[1024,768]{1,0:T(8,128)} convert(bf16[1024,768]{1,0:T(8,128)(2,1)} %get-tuple-element.193) | non-fusion elementwise | flops 786432 | bytes 4718592 | tf_op jit(solution)/shard_map/convert_element_type | solution.py:544
  312.6 4.8 %collective-permute-done.53.refs_6_ = bf16[128,1024]{1,0:T(8,128)(2,1)} collective-permute-done((bf16[128,1024]{1,0:T(8,128)(2,1)S(1)}, bf16[128,1024]{1,0:T(8,128)(2,1)}, u32[]{:S(2)}, u32[]{:S(2)}) %collective-permute-start.53) | collective-permute-done | bytes 262176 | tf_op jit(solution)/shard_map/ppermute | solution.py:54
  318.5 3.1 collective-permute-done.38.refs_6_
  325.9 4.4 %spread.1 = (f32[1024,512]{1,0:T(8,128)}, f32[1024,256]{1,0:T(8,128)}, f32[1024,256]{1,0:T(8,128)}, f32[512,1024]{1,0:T(8,128)}) custom-call(s32[4]{0:T(128)S(1)} %pad_add_fusion.1.refs_0_, bf16[256,1024]{1,0:T(8,128)(2,1)S(1)} %sum_parts.11.refs_1_, bf16[256,1024]{1,0:T(8,128)(2,1)} %collective-permute-done.47.refs_2_, bf16[256,1024]{1,0:T(8,128)(2,1)} %copy-done.39, ...), custom_call_target="tpu_custom_call" | custom-call | tf_op jit(solution)/shard_map/spread/pallas_call | solution.py:35
  (261 shorter events, 114.4 us)
Async XLA Ops:
  7.2 111.9 %all-gather.2.cloned.1.call-start = ((), (), s32[]{:S(2)}) async-start(), calls=%async_computation | async-start | bytes 1310720 | tf_op jit(solution)/shard_map/all_gather | solution.py:753
  9.0 18.1 %collective-permute-start = (bf16[128,1024]{1,0:T(8,128)(2,1)S(1)}, bf16[128,1024]{1,0:T(8,128)(2,1)S(1)}, u32[]{:S(2)}, u32[]{:S(2)}) collective-permute-start(bf16[128,1024]{1,0:T(8,128)(2,1)S(1)} %norm1.1.refs_0_), channel_id=1, source_target_pairs={{4,0},{8,4},{12,8},{0,12},{5,1},{9,5},{13,9},{1,13},{6,2},{10,6},{... | collective-permute-start | bytes 786440 | tf_op jit(solution)/shard_map/ppermute | solution.py:65
  33.4 13.2 %collective-permute-start.8 = (bf16[128,1024]{1,0:T(8,128)(2,1)S(1)}, bf16[128,1024]{1,0:T(8,128)(2,1)S(1)}, u32[]{:S(2)}, u32[]{:S(2)}) collective-permute-start(bf16[128,1024]{1,0:T(8,128)(2,1)S(1)} %norm1.1.refs_0_), channel_id=1, source_target_pairs={{8,0},{12,4},{0,8},{4,12},{9,1},{13,5},{1,9},{5,13},{10,2},{14,6},... | collective-permute-start | bytes 786440 | tf_op jit(solution)/shard_map/ppermute | solution.py:65
  34.2 14.3 %collective-permute-start.7 = (bf16[2,128,1024]{2,1,0:T(8,128)(2,1)S(1)}, bf16[2,128,1024]{2,1,0:T(8,128)(2,1)S(1)}, u32[]{:S(2)}, u32[]{:S(2)}) collective-permute-start(bf16[2,128,1024]{2,1,0:T(8,128)(2,1)S(1)} %pad_maximum_fusion.2.refs_0_), channel_id=1, source_target_pairs={{0,3},{1,2},{2,1},{3,0},{4,7},{5,6},{6,5},{7,4},{8,11},{9,10},{10,... | collective-permute-start | bytes 1572872 | tf_op jit(solution)/shard_map/ppermute | solution.py:54
  55.0 200.3 %all-reduce.3.cloned.1.call-start = ((), (), s32[]{:S(2)}) async-start(), calls=%async_computation.1 | async-start | bytes 9437184 | tf_op jit(solution)/shard_map/psum | solution.py:789
  55.3 17.7 %collective-permute-start.5 = (bf16[2,128,1024]{2,1,0:T(8,128)(2,1)S(1)}, bf16[2,128,1024]{2,1,0:T(8,128)(2,1)S(1)}, u32[]{:S(2)}, u32[]{:S(2)}) collective-permute-start(bf16[2,128,1024]{2,1,0:T(8,128)(2,1)S(1)} %pad_maximum_fusion.2.refs_0_), channel_id=1, source_target_pairs={{0,1},{1,0},{2,3},{3,2},{4,5},{5,4},{6,7},{7,6},{8,9},{9,8},{10,11... | collective-permute-start | bytes 1572872 | tf_op jit(solution)/shard_map/ppermute | solution.py:54
  56.8 17.7 %collective-permute-start.6 = (bf16[2,128,1024]{2,1,0:T(8,128)(2,1)S(1)}, bf16[2,128,1024]{2,1,0:T(8,128)(2,1)}, u32[]{:S(2)}, u32[]{:S(2)}) collective-permute-start(bf16[2,128,1024]{2,1,0:T(8,128)(2,1)S(1)} %pad_maximum_fusion.2.refs_0_), channel_id=1, source_target_pairs={{0,2},{1,3},{2,0},{3,1},{4,6},{5,7},{6,4},{7,5},{8,10},{9,11},{10,... | collective-permute-start | bytes 1572872 | tf_op jit(solution)/shard_map/ppermute | solution.py:54
  58.0 23.6 %collective-permute-start.9 = (bf16[1,128,1024]{2,1,0:T(8,128)(2,1)S(1)}, bf16[1,128,1024]{2,1,0:T(8,128)(2,1)S(1)}, u32[]{:S(2)}, u32[]{:S(2)}) collective-permute-start(bf16[1,128,1024]{2,1,0:T(8,128)(2,1)S(1)} %bitcast.68), channel_id=1, source_target_pairs={{0,1},{1,0},{2,3},{3,2},{4,5},{5,4},{6,7},{7,6},{8,9},{9,8},{10,11... | collective-permute-start | bytes 786440 | tf_op jit(solution)/shard_map/ppermute | solution.py:54
  58.6 23.0 %collective-permute-start.10 = (bf16[1,128,1024]{2,1,0:T(8,128)(2,1)S(1)}, bf16[1,128,1024]{2,1,0:T(8,128)(2,1)S(1)}, u32[]{:S(2)}, u32[]{:S(2)}) collective-permute-start(bf16[1,128,1024]{2,1,0:T(8,128)(2,1)S(1)} %bitcast.69), channel_id=1, source_target_pairs={{0,2},{1,3},{2,0},{3,1},{4,6},{5,7},{6,4},{7,5},{8,10},{9,11},{10,... | collective-permute-start | bytes 786440 | tf_op jit(solution)/shard_map/ppermute | solution.py:54
  149.4 23.9 %collective-permute-start.24 = (bf16[128,1024]{1,0:T(8,128)(2,1)}, bf16[128,1024]{1,0:T(8,128)(2,1)S(1)}, u32[]{:S(2)}, u32[]{:S(2)}) collective-permute-start(bf16[128,1024]{1,0:T(8,128)(2,1)} %get-tuple-element.143), channel_id=1, source_target_pairs={{0,1},{1,0},{2,3},{3,2},{4,5},{5,4},{6,7},{7,6},{8,9},{9,8},{10,11... | collective-permute-start | bytes 786440 | tf_op jit(solution)/shard_map/ppermute | solution.py:54
  150.3 23.0 %collective-permute-start.25 = (bf16[128,1024]{1,0:T(8,128)(2,1)}, bf16[128,1024]{1,0:T(8,128)(2,1)S(1)}, u32[]{:S(2)}, u32[]{:S(2)}) collective-permute-start(bf16[128,1024]{1,0:T(8,128)(2,1)} %get-tuple-element.144), channel_id=1, source_target_pairs={{0,2},{1,3},{2,0},{3,1},{4,6},{5,7},{6,4},{7,5},{8,10},{9,11},{10,... | collective-permute-start | bytes 786440 | tf_op jit(solution)/shard_map/ppermute | solution.py:54
  153.4 20.0 %collective-permute-start.26 = (bf16[128,1024]{1,0:T(8,128)(2,1)}, bf16[128,1024]{1,0:T(8,128)(2,1)S(1)}, u32[]{:S(2)}, u32[]{:S(2)}) collective-permute-start(bf16[128,1024]{1,0:T(8,128)(2,1)} %get-tuple-element.145), channel_id=1, source_target_pairs={{0,3},{1,2},{2,1},{3,0},{4,7},{5,6},{6,5},{7,4},{8,11},{9,10},{10,... | collective-permute-start | bytes 786440 | tf_op jit(solution)/shard_map/ppermute | solution.py:54
  195.1 32.0 %collective-permute-start.45 = (bf16[256,1024]{1,0:T(8,128)(2,1)}, bf16[256,1024]{1,0:T(8,128)(2,1)S(1)}, u32[]{:S(2)}, u32[]{:S(2)}) collective-permute-start(bf16[256,1024]{1,0:T(8,128)(2,1)} %get-tuple-element.180), channel_id=1, source_target_pairs={{0,4},{4,0},{8,12},{12,8},{1,5},{5,1},{9,13},{13,9},{2,6},{6,2},{1... | collective-permute-start | bytes 1572872 | tf_op jit(solution)/shard_map/ppermute | solution.py:54
  197.3 59.6 %collective-permute-start.50 = (bf16[256,1024]{1,0:T(8,128)(2,1)}, bf16[256,1024]{1,0:T(8,128)(2,1)}, u32[]{:S(2)}, u32[]{:S(2)}) collective-permute-start(bf16[256,1024]{1,0:T(8,128)(2,1)} %get-tuple-element.137), channel_id=1, source_target_pairs={{0,16},{16,0},{1,17},{17,1},{2,18},{18,2},{3,19},{19,3},{4,20},{20... | collective-permute-start | bytes 1572872 | tf_op jit(solution)/shard_map/ppermute | solution.py:54
  201.9 19.0 %collective-permute-start.29 = (bf16[1,128,1024]{2,1,0:T(8,128)(2,1)}, bf16[1,128,1024]{2,1,0:T(8,128)(2,1)S(1)}, u32[]{:S(2)}, u32[]{:S(2)}) collective-permute-start(bf16[1,128,1024]{2,1,0:T(8,128)(2,1)} %get-tuple-element.164), channel_id=1, source_target_pairs={{0,3},{1,2},{2,1},{3,0},{4,7},{5,6},{6,5},{7,4},{8,11},{9,10},{10,... | collective-permute-start | bytes 786440 | tf_op jit(solution)/shard_map/ppermute | solution.py:54
  215.3 40.0 %collective-permute-start.30 = (bf16[1,128,1024]{2,1,0:T(8,128)(2,1)}, bf16[1,128,1024]{2,1,0:T(8,128)(2,1)S(1)}, u32[]{:S(2)}, u32[]{:S(2)}) collective-permute-start(bf16[1,128,1024]{2,1,0:T(8,128)(2,1)} %get-tuple-element.166), channel_id=1, source_target_pairs={{0,1},{1,0},{2,3},{3,2},{4,5},{5,4},{6,7},{7,6},{8,9},{9,8},{10,11... | collective-permute-start | bytes 786440 | tf_op jit(solution)/shard_map/ppermute | solution.py:54
  219.4 40.1 %collective-permute-start.31 = (bf16[1,128,1024]{2,1,0:T(8,128)(2,1)}, bf16[1,128,1024]{2,1,0:T(8,128)(2,1)S(1)}, u32[]{:S(2)}, u32[]{:S(2)}) collective-permute-start(bf16[1,128,1024]{2,1,0:T(8,128)(2,1)} %get-tuple-element.167), channel_id=1, source_target_pairs={{0,2},{1,3},{2,0},{3,1},{4,6},{5,7},{6,4},{7,5},{8,10},{9,11},{10,... | collective-permute-start | bytes 786440 | tf_op jit(solution)/shard_map/ppermute | solution.py:54
  221.6 39.5 %collective-permute-start.32 = (bf16[1,128,1024]{2,1,0:T(8,128)(2,1)}, bf16[1,128,1024]{2,1,0:T(8,128)(2,1)S(1)}, u32[]{:S(2)}, u32[]{:S(2)}) collective-permute-start(bf16[1,128,1024]{2,1,0:T(8,128)(2,1)} %get-tuple-element.168), channel_id=1, source_target_pairs={{0,3},{1,2},{2,1},{3,0},{4,7},{5,6},{6,5},{7,4},{8,11},{9,10},{10,... | collective-permute-start | bytes 786440 | tf_op jit(solution)/shard_map/ppermute | solution.py:54
  227.2 35.7 %collective-permute-start.34 = (bf16[2,128,1024]{2,1,0:T(8,128)(2,1)}, bf16[2,128,1024]{2,1,0:T(8,128)(2,1)}, u32[]{:S(2)}, u32[]{:S(2)}) collective-permute-start(bf16[2,128,1024]{2,1,0:T(8,128)(2,1)} %get-tuple-element.170), channel_id=1, source_target_pairs={{0,1},{1,0},{2,3},{3,2},{4,5},{5,4},{6,7},{7,6},{8,9},{9,8},{10,11... | collective-permute-start | bytes 1572872 | tf_op jit(solution)/shard_map/ppermute | solution.py:54
  255.4 22.4 %collective-permute-start.46 = (bf16[256,1024]{1,0:T(8,128)(2,1)S(1)}, bf16[256,1024]{1,0:T(8,128)(2,1)S(1)}, u32[]{:S(2)}, u32[]{:S(2)}) collective-permute-start(bf16[256,1024]{1,0:T(8,128)(2,1)S(1)} %sum_parts.10.refs_0_), channel_id=1, source_target_pairs={{0,12},{4,8},{8,4},{12,0},{1,13},{5,9},{9,5},{13,1},{2,14},{6,10},... | collective-permute-start | bytes 1572872 | tf_op jit(solution)/shard_map/ppermute | solution.py:54
  256.9 26.4 %collective-permute-start.35 = (bf16[2,128,1024]{2,1,0:T(8,128)(2,1)}, bf16[2,128,1024]{2,1,0:T(8,128)(2,1)}, u32[]{:S(2)}, u32[]{:S(2)}) collective-permute-start(bf16[2,128,1024]{2,1,0:T(8,128)(2,1)} %copy-done.32), channel_id=1, source_target_pairs={{0,2},{1,3},{2,0},{3,1},{4,6},{5,7},{6,4},{7,5},{8,10},{9,11},{10,... | collective-permute-start | bytes 1572872 | tf_op jit(solution)/shard_map/ppermute | solution.py:54
  259.4 25.1 %collective-permute-start.36 = (bf16[2,128,1024]{2,1,0:T(8,128)(2,1)}, bf16[2,128,1024]{2,1,0:T(8,128)(2,1)S(1)}, u32[]{:S(2)}, u32[]{:S(2)}) collective-permute-start(bf16[2,128,1024]{2,1,0:T(8,128)(2,1)} %copy-done.31), channel_id=1, source_target_pairs={{0,3},{1,2},{2,1},{3,0},{4,7},{5,6},{6,5},{7,4},{8,11},{9,10},{10,... | collective-permute-start | bytes 1572872 | tf_op jit(solution)/shard_map/ppermute | solution.py:54
  261.8 15.0 %collective-permute-start.51 = (bf16[128,1024]{1,0:T(8,128)(2,1)S(1)}, bf16[128,1024]{1,0:T(8,128)(2,1)S(1)}, u32[]{:S(2)}, u32[]{:S(2)}) collective-permute-start(bf16[128,1024]{1,0:T(8,128)(2,1)S(1)} %get-tuple-element.188), channel_id=1, source_target_pairs={{0,4},{4,0},{8,12},{12,8},{1,5},{5,1},{9,13},{13,9},{2,6},{6,2},{1... | collective-permute-start | bytes 786440 | tf_op jit(solution)/shard_map/ppermute | solution.py:54
  262.8 38.2 %collective-permute-start.27 = (bf16[1,128,1024]{2,1,0:T(8,128)(2,1)S(1)}, bf16[1,128,1024]{2,1,0:T(8,128)(2,1)S(1)}, u32[]{:S(2)}, u32[]{:S(2)}) collective-permute-start(bf16[1,128,1024]{2,1,0:T(8,128)(2,1)S(1)} %copy-done.34), channel_id=1, source_target_pairs={{0,1},{1,0},{2,3},{3,2},{4,5},{5,4},{6,7},{7,6},{8,9},{9,8},{10,11... | collective-permute-start | bytes 786440 | tf_op jit(solution)/shard_map/ppermute | solution.py:54
  276.8 32.8 %collective-permute-start.28 = (bf16[1,128,1024]{2,1,0:T(8,128)(2,1)}, bf16[1,128,1024]{2,1,0:T(8,128)(2,1)}, u32[]{:S(2)}, u32[]{:S(2)}) collective-permute-start(bf16[1,128,1024]{2,1,0:T(8,128)(2,1)} %get-tuple-element.163), channel_id=1, source_target_pairs={{0,2},{1,3},{2,0},{3,1},{4,6},{5,7},{6,4},{7,5},{8,10},{9,11},{10,... | collective-permute-start | bytes 786440 | tf_op jit(solution)/shard_map/ppermute | solution.py:54
  283.3 26.3 %collective-permute-start.47 = (bf16[256,1024]{1,0:T(8,128)(2,1)S(1)}, bf16[256,1024]{1,0:T(8,128)(2,1)}, u32[]{:S(2)}, u32[]{:S(2)}) collective-permute-start(bf16[256,1024]{1,0:T(8,128)(2,1)S(1)} %sum_parts.11.refs_1_), channel_id=1, source_target_pairs={{0,4},{4,0},{8,12},{12,8},{1,5},{5,1},{9,13},{13,9},{2,6},{6,2},{1... | collective-permute-start | bytes 1572872 | tf_op jit(solution)/shard_map/ppermute | solution.py:54
  284.6 13.4 %collective-permute-start.43 = (f32[2304]{0:T(1024)S(1)}, f32[2304]{0:T(1024)S(1)}, u32[]{:S(2)}, u32[]{:S(2)}) collective-permute-start(f32[2304]{0:T(1024)S(1)} %add.117), channel_id=1, source_target_pairs={{0,8},{4,12},{8,0},{12,4},{1,9},{5,13},{9,1},{13,5},{2,10},{6,14},... | collective-permute-start | bytes 27656 | tf_op jit(solution)/shard_map/ppermute | solution.py:54
  288.9 23.7 %collective-permute-start.33 = (bf16[128,1024]{1,0:T(8,128)(2,1)S(1)}, bf16[128,1024]{1,0:T(8,128)(2,1)}, u32[]{:S(2)}, u32[]{:S(2)}) collective-permute-start(bf16[128,1024]{1,0:T(8,128)(2,1)S(1)} %sum_parts.7), channel_id=1, source_target_pairs={{0,8},{4,12},{8,0},{12,4},{1,9},{5,13},{9,1},{13,5},{2,10},{6,14},... | collective-permute-start | bytes 786440 | tf_op jit(solution)/shard_map/ppermute | solution.py:70
  297.9 14.7 %collective-permute-start.37 = (bf16[128,1024]{1,0:T(8,128)(2,1)S(1)}, bf16[128,1024]{1,0:T(8,128)(2,1)}, u32[]{:S(2)}, u32[]{:S(2)}) collective-permute-start(bf16[128,1024]{1,0:T(8,128)(2,1)S(1)} %sum_parts.8), channel_id=1, source_target_pairs={{0,4},{4,8},{8,12},{12,0},{1,5},{5,9},{9,13},{13,1},{2,6},{6,10},{... | collective-permute-start | bytes 786440 | tf_op jit(solution)/shard_map/ppermute | solution.py:70
  301.1 16.4 %collective-permute-start.53 = (bf16[128,1024]{1,0:T(8,128)(2,1)S(1)}, bf16[128,1024]{1,0:T(8,128)(2,1)}, u32[]{:S(2)}, u32[]{:S(2)}) collective-permute-start(bf16[128,1024]{1,0:T(8,128)(2,1)S(1)} %sum_parts.13.refs_5_), channel_id=1, source_target_pairs={{0,4},{4,0},{8,12},{12,8},{1,5},{5,1},{9,13},{13,9},{2,6},{6,2},{1... | collective-permute-start | bytes 786440 | tf_op jit(solution)/shard_map/ppermute | solution.py:54
  309.6 14.7 %collective-permute-start.48 = (bf16[256,1024]{1,0:T(8,128)(2,1)S(1)}, bf16[256,1024]{1,0:T(8,128)(2,1)S(1)}, u32[]{:S(2)}, u32[]{:S(2)}) collective-permute-start(bf16[256,1024]{1,0:T(8,128)(2,1)S(1)} %sum_parts.11.refs_1_), channel_id=1, source_target_pairs={{0,16},{16,0},{1,17},{17,1},{2,18},{18,2},{3,19},{19,3},{4,20},{20... | collective-permute-start | bytes 1572872 | tf_op jit(solution)/shard_map/ppermute | solution.py:54
  309.6 14.7 %collective-permute-start.49 = (bf16[256,1024]{1,0:T(8,128)(2,1)}, bf16[256,1024]{1,0:T(8,128)(2,1)S(1)}, u32[]{:S(2)}, u32[]{:S(2)}) collective-permute-start(bf16[256,1024]{1,0:T(8,128)(2,1)} %collective-permute-done.47.refs_2_), channel_id=1, source_target_pairs={{0,16},{16,0},{1,17},{17,1},{2,18},{18,2},{3,19},{19,3},{4,20},{20... | collective-permute-start | bytes 1572872 | tf_op jit(solution)/shard_map/ppermute | solution.py:54
  (75 other events, 593.3 us)
Sparse Core Ops, SparseCore 0:
  55.2 28.9 all-gather.1
  142.7 112.5 all-reduce.2
